TPU v7x, 256 devices: a whole 4x4x8 slice. The times are simulated.
256 devices in a mesh: var: 16 (over x_lo, z), tok: 16 (over y, x_hi, core).
Axes of the slice: x: 4 (x_hi: 2, x_lo: 2; x = x_hi * 2 + x_lo), y: 4, z: 8, core: 2. Of those that a mesh axis runs over, the one named last changes fastest.
Arguments:
- patches: bfloat16 [96, 16, 2048], P('var', None, 'tok'), may hold values from -6 to 6
- slot_variable: int32 [96], P('var'), may hold values from -1 to 90, as said below
- embed_weight: bfloat16 [96, 16, 4096], P('var'), may hold values from -1.5 to 1.5
- variable_embed: bfloat16 [91, 4096], replicated, may hold values from -6 to 6
- norm_gain: bfloat16 [4096], replicated, may hold values from 0.099609375 to 1.8984375
- pool_keys: bfloat16 [4096, 16], replicated, may hold values from -150 to 150
- pool_value: bfloat16 [4096, 2048], P('tok', 'var'), may hold values from -0.09375 to 0.09375
- pool_out: bfloat16 [2048, 4096], P('var'), may hold values from -0.875 to 0.875
- block_gain: bfloat16 [4096], replicated, may hold values from 0.099609375 to 1.8984375
- attend_weight: bfloat16 [3, 4096, 2048], P(None, None, 'var'), may hold values from -6 to 6
- out_proj: bfloat16 [2048, 4096], P('var'), may hold values from -1.25 to 1.25
Outputs:
- aggregated: bfloat16 [2048, 4096], P('tok', 'var')
- attended: bfloat16 [2048, 4096], P('tok', 'var')
Inputs may be any that keep to these rules, and one draw needn't show every extreme that they name: `slot_variable`: every variable 0 to 90 stands in exactly one slot; the other 5 slots hold -1 and carry no variable.
All inputs are finite; a program needn't handle non-finite values.
Results may differ from a plain program's by a relative error of at most 0.04.
The roundings to bfloat16 on the way count: a program that leaves them out, or rounds other values in their place, can miss the bound.
Values may be sent and summed in bfloat16 or wider, within the bound.
No kernel may reach another device: no remote copies, remote signals or barrier semaphores. Data moves between devices by JAX's collectives and lax.ppermute only.
A program may use at most 128 MiB of HBM per device.

v0:
```python
import math

import jax
import jax.numpy as jnp
from jax import lax
from jax.sharding import PartitionSpec as P

HEADS = 16
HEAD_DIM = 128


def layer_norm(inputs, gain_vector):
    centered = inputs - jnp.mean(inputs, axis=-1, keepdims=True)
    spread = jnp.mean(centered * centered, axis=-1, keepdims=True)
    return centered * lax.rsqrt(spread + 1e-05) * gain_vector.astype(jnp.float32)


def shards(
    patches,
    slot_variable,
    embed_weight,
    variable_embed,
    norm_gain,
    pool_keys,
    pool_value,
    pool_out,
    block_gain,
    attend_weight,
    out_proj,
):
    slot_count, patch_count, tok_rows = patches.shape
    model_width = embed_weight.shape[2]
    head_share = HEADS // lax.axis_size("var")
    score_scale = 1.0 / math.sqrt(HEAD_DIM)
    occupied = (slot_variable >= 0)[None, :, None]
    lookup = (
        slot_variable[:, None] == jnp.arange(variable_embed.shape[0], dtype=jnp.int32)[None, :]
    ).astype(jnp.bfloat16)
    var_rows = jnp.dot(lookup, variable_embed, preferred_element_type=jnp.float32)
    embedded = (
        jnp.einsum("spt,spd->tsd", patches, embed_weight, preferred_element_type=jnp.float32)
        + var_rows[None]
    )
    normed = (
        layer_norm(embedded, norm_gain)
        .astype(jnp.bfloat16)
        .reshape(tok_rows * slot_count, model_width)
    )
    scores = (
        jnp.dot(normed, pool_keys, preferred_element_type=jnp.float32).reshape(
            tok_rows, slot_count, HEADS
        )
        * score_scale
    )
    head_cols = lax.all_gather(pool_value, "tok", axis=0, tiled=True)
    values = jnp.dot(
        normed,
        lax.all_gather(head_cols, "var", axis=1, tiled=True),
        preferred_element_type=jnp.float32,
    )
    values = values.reshape(tok_rows, slot_count, HEADS, HEAD_DIM)
    masked = jnp.where(occupied, scores, -1e30)
    local_max = jnp.max(masked, axis=1)
    highest = lax.pmax(local_max, "var")
    weights = jnp.where(occupied, jnp.exp(masked - highest[:, None, :]), 0.0)
    numerator = jnp.einsum("tsh,tshe->the", weights, values, precision=lax.Precision.HIGHEST)
    denominator = jnp.sum(weights, axis=1)
    numerator, denominator = (
        lax.psum_scatter(numerator, "var", scatter_dimension=1, tiled=True),
        lax.psum_scatter(denominator, "var", scatter_dimension=1, tiled=True),
    )
    pooled = (
        (numerator / denominator[..., None])
        .astype(jnp.bfloat16)
        .reshape(tok_rows, head_share * HEAD_DIM)
    )
    partial_tokens = jnp.dot(pooled, pool_out, preferred_element_type=jnp.float32)
    var_index = lax.axis_index("var")
    col_share = model_width // lax.axis_size("var")
    token_state = lax.psum(partial_tokens, "var")
    aggregated = lax.dynamic_slice_in_dim(token_state, var_index * col_share, col_share, 1).astype(
        jnp.bfloat16
    )
    normed_tokens = layer_norm(token_state, block_gain).astype(jnp.bfloat16)
    projected = jnp.einsum(
        "td,cdf->ctf", normed_tokens, attend_weight, preferred_element_type=jnp.float32
    )
    queries = projected[0].astype(jnp.bfloat16).reshape(tok_rows, head_share, HEAD_DIM)
    key_rows = projected[1].astype(jnp.bfloat16).reshape(tok_rows, head_share, HEAD_DIM)
    value_rows = projected[2].astype(jnp.bfloat16).reshape(tok_rows, head_share, HEAD_DIM)
    running_max = jnp.full((head_share, tok_rows), -1e30, jnp.float32)
    key_part = lax.all_gather(key_rows, "tok", axis=0, tiled=True)
    value_part = lax.all_gather(value_rows, "tok", axis=0, tiled=True)
    att_scores = (
        jnp.einsum("qhe,khe->hqk", queries, key_part, preferred_element_type=jnp.float32)
        * score_scale
    )
    new_max = jnp.maximum(running_max, jnp.max(att_scores, axis=2))
    exp_scores = jnp.exp(att_scores - new_max[..., None])
    running = jnp.sum(exp_scores, axis=2)
    accumulated = jnp.einsum(
        "hqk,khe->hqe",
        exp_scores.astype(jnp.bfloat16),
        value_part,
        preferred_element_type=jnp.float32,
    )
    running_max, running, accumulated = (new_max, running, accumulated)
    context = (accumulated / running[..., None]).astype(jnp.bfloat16)
    context = jnp.transpose(context, (1, 0, 2)).reshape(tok_rows, head_share * HEAD_DIM)
    attended = lax.psum_scatter(
        jnp.dot(context, out_proj, preferred_element_type=jnp.float32),
        "var",
        scatter_dimension=1,
        tiled=True,
    ).astype(jnp.bfloat16)
    return (aggregated, attended)


def solution(mesh):
    return jax.shard_map(
        shards,
        mesh=mesh,
        in_specs=(
            P("var", None, "tok"),
            P("var"),
            P("var", None, None),
            P(),
            P(),
            P(),
            P("tok", "var"),
            P("var", None),
            P(),
            P(None, None, "var"),
            P("var", None),
        ),
        out_specs=(P("tok", "var"), P("tok", "var")),
        check_vma=False,
    )
```

profile of v0, /device:TPU:34, one launch (start us, length us, event | category | flops | bytes accessed | tf_op | source)
XLA Modules:
  0.0 670.9 jit_solution(8865102129616724498)
XLA Ops:
  7.2 0.7 all-gather.5.cloned.1.call-update
  8.0 54.4 %all-gather.5.cloned.1.call-done = bf16[4096,128]{1,0:T(8,128)(2,1)} async-done(((bf16[256,128]{1,0:T(8,128)(2,1)}), bf16[4096,128]{1,0:T(8,128)(2,1)}) %all-gather.5.cloned.1.call-update) | async-done | bytes 1048592 | tf_op jit(solution)/shard_map/all_gather | solution.py:55
  62.5 0.7 convert_element_type.58
  63.2 0.7 broadcast_compare_fusion
  63.8 1.4 fusion.28
  65.2 6.4 bitcast_reduce_fusion
  71.7 7.0 %multiply_reduce_fusion = f32[128,6]{0,1:T(8,128)S(1)} fusion(f32[6,4096,128]{2,1,0:T(8,128)S(1)} %get-tuple-element.7, f32[128,6]{0,1:T(8,128)S(1)} %broadcast_multiply_fusion, f32[6,4096]{1,0:T(8,128)S(1)} %fusion.28), kind=kLoop, calls=%fused_computation.3 | loop fusion | flops 12582144 | bytes 12687360 | tf_op jit(solution)/shard_map/reduce_sum | solution.py:14
  78.8 4.8 multiply_convert_fusion
  83.6 2.6 copy-done.1
  86.2 0.9 fusion.31
  87.1 33.9 %pmax.7 = f32[128,16]{0,1:T(8,128)S(1)} all-reduce(f32[128,16]{0,1:T(8,128)S(1)} %get-tuple-element.8), channel_id=1, replica_groups=mesh['var'=16,'tok'=16] {'var'}, use_global_device_ids=true, to_apply=%region_3.4 | all-reduce | flops 2048 | bytes 16384 | tf_op jit(solution)/shard_map/pmax | solution.py:64
  121.0 1.3 copy.20
  122.4 140.9 %all-gather.7.cloned.1.call-done = bf16[4096,2048]{1,0:T(8,128)(2,1)} async-done(((bf16[4096,128]{1,0:T(8,128)(2,1)}), bf16[4096,2048]{1,0:T(8,128)(2,1)}) %all-gather.7.cloned.1.call-update) | async-done | bytes 16777232 | tf_op jit(solution)/shard_map/all_gather | solution.py:58
  263.3 20.7 %copy.16 = bf16[2048,4096]{1,0:T(8,128)(2,1)} copy(bf16[2048,4096]{0,1:T(8,128)(2,1)} %bitcast.60) | data formatting | bytes 33554432 | tf_op jit(solution)/shard_map/dot_general | solution.py:56
  284.0 16.9 %fusion.2 = f32[128,6,16,128]{3,0,2,1:T(8,128)S(1)} fusion(bf16[16,128,4096,1]{2,1,0,3:T(8,128)(2,1)} %bitcast.61, bf16[128,6,4096]{0,2,1:T(8,128)(2,1)} %copy-done.1), kind=kOutput, calls=%fused_computation.6 | convolution fusion | flops 12884901888 | bytes 29360128 | tf_op jit(solution)/shard_map/dot_general | solution.py:56
  300.9 20.0 %fusion = f32[128,16,1,128]{3,2,1,0:T(1,128)S(1)} fusion(f32[128,6,16,1]{1,3,2,0:T(1,128)S(1)} %copy-done.3, f32[128,6,16,128]{3,0,2,1:T(8,128)S(1)} %fusion.2), kind=kOutput, calls=%fused_computation.4 | convolution fusion | flops 18874368 | bytes 7389184 | tf_op jit(solution)/shard_map/tsh,tshe->the/dot_general | solution.py:66
  320.9 1.3 copy.28
  322.9 33.2 %all-reduce = f32[128,16]{0,1:T(8,128)S(1)} all-reduce(f32[128,16]{0,1:T(8,128)S(1)} %get-tuple-element.4), channel_id=5, replica_groups=mesh['var'=16,'tok'=16] {'var'}, use_global_device_ids=true, to_apply=%region_6.7.clone | all-reduce | flops 2048 | bytes 16384
  356.1 0.7 dynamic-slice_bitcast_fusion
  356.8 34.5 %reduce-scatter.3.cloned.1.call-done = f32[128,1,128]{2,0,1:T(8,128)} async-done(((f32[128,16,128]{2,0,1:T(8,128)}), f32[128,1,128]{2,0,1:T(8,128)}) %reduce-scatter.3.cloned.1.call-update) | async-done | bytes 65552 | tf_op jit(solution)/shard_map/reduce_scatter | solution.py:69
  391.3 3.0 fusion.25
  394.6 139.1 %all-reduce.3.cloned.1.call-done = f32[128,4096]{1,0:T(8,128)} async-done(((f32[128,4096]{1,0:T(8,128)}), f32[128,4096]{1,0:T(8,128)}) %all-reduce.3.cloned.1.call-update) | async-done | bytes 2097168 | tf_op jit(solution)/shard_map/psum | solution.py:80
  533.8 1.8 reduce_sum.57
  535.5 1.9 multiply_reduce_fusion.1
  537.5 2.4 fusion.4
  539.9 27.0 %all-gather.1 = bf16[1,2048,128]{2,1,0:T(8,128)(2,1)} all-gather(bf16[1,128,128]{2,1,0:T(8,128)(2,1)S(1)} %get-tuple-element.2), channel_id=3, replica_groups=mesh['var'=16,'tok'=16] {'tok'}, dimensions={1}, use_global_device_ids=true | all-gather | bytes 557056 | tf_op jit(solution)/shard_map/all_gather | solution.py:93
  566.9 21.6 %all-gather = bf16[1,2048,128]{2,1,0:T(8,128)(2,1)S(1)} all-gather(bf16[1,128,128]{2,1,0:T(8,128)(2,1)S(1)} %get-tuple-element.3), channel_id=2, replica_groups=mesh['var'=16,'tok'=16] {'tok'}, dimensions={1}, use_global_device_ids=true | all-gather | bytes 557056 | tf_op jit(solution)/shard_map/all_gather | solution.py:92
  588.9 1.0 copy-done.2
  590.1 3.7 fusion.7
  593.9 1.5 dynamic-slice_convert_fusion
  595.4 67.3 %reduce-scatter.5.cloned.1.call-done = f32[128,256]{1,0:T(8,128)} async-done(((f32[128,4096]{1,0:T(8,128)}), f32[128,256]{1,0:T(8,128)}) %reduce-scatter.5.cloned.1.call-update) | async-done | bytes 131088 | tf_op jit(solution)/shard_map/reduce_scatter | solution.py:110
  662.8 1.5 convert_element_type.69
  (32 shorter events, 1.9 us)
Async XLA Ops:
  7.2 530.3 %copy-start = (bf16[3,4096,128]{2,1,0:T(8,128)(2,1)S(1)}, bf16[3,4096,128]{2,1,0:T(8,128)(2,1)}, u32[]{:S(2)}) copy-start(bf16[3,4096,128]{2,1,0:T(8,128)(2,1)} %param.20) | copy-start | bytes 9437188
  7.2 55.2 %all-gather.5.cloned.1.call-start = ((), (), s32[]{:S(2)}) async-start(), calls=%async_computation.2 | async-start | bytes 1114112 | tf_op jit(solution)/shard_map/all_gather | solution.py:55
  7.9 255.4 %all-gather.7.cloned.1.call-start = ((), (), s32[]{:S(2)}) async-start(), calls=%async_computation.3 | async-start | bytes 17825792 | tf_op jit(solution)/shard_map/all_gather | solution.py:58
  62.4 328.8 %reduce-scatter.3.cloned.1.call-start = ((), (), s32[]{:S(2)}) async-start(), calls=%async_computation.4 | async-start | bytes 1114112 | tf_op jit(solution)/shard_map/reduce_scatter | solution.py:69
  78.8 7.4 %copy-start.4 = (bf16[4096,16]{0,1:T(8,128)(2,1)S(1)}, bf16[4096,16]{0,1:T(8,128)(2,1)}, u32[]{:S(2)}) copy-start(bf16[4096,16]{0,1:T(8,128)(2,1)} %param.16) | copy-start | bytes 393220
  83.6 2.6 copy-start.1
  284.0 16.9 %copy-start.3 = (f32[128,6,16,1]{1,3,2,0:T(1,128)S(1)}, f32[128,6,16,1]{1,3,2,0:T(1,128)}, u32[]{:S(2)}) copy-start(f32[128,6,16,1]{1,3,2,0:T(1,128)} %copy.20) | copy-start | bytes 147460
  300.9 21.4 %copy-start.6 = (u32[256]{0:T(256)S(1)}, u32[256]{0:T(256)}, u32[]{:S(2)}) copy-start(u32[256]{0:T(256)} %constant.37) | copy-start | bytes 3076
  320.9 73.7 %copy-start.5 = (bf16[4096]{0:T(1024)(128)(2,1)S(1)}, bf16[4096]{0:T(1024)(128)(2,1)}, u32[]{:S(2)}) copy-start(bf16[4096]{0:T(1024)(128)(2,1)} %param.19) | copy-start | bytes 24580
  322.3 211.5 %all-reduce.3.cloned.1.call-start = ((), (), s32[]{:S(2)}) async-start(), calls=%async_computation.5 | async-start | bytes 4194304 | tf_op jit(solution)/shard_map/psum | solution.py:80
  394.3 268.5 %reduce-scatter.5.cloned.1.call-start = ((), (), s32[]{:S(2)}) async-start(), calls=%async_computation.6 | async-start | bytes 2228224 | tf_op jit(solution)/shard_map/reduce_scatter | solution.py:110
  588.8 1.0 copy-start.2
Sparse Core Ops, SparseCore 0:
  10.8 51.5 all-gather.4
  64.1 199.1 all-gather.6
  322.4 68.8 reduce-scatter.2
  394.4 139.2 all-reduce.2
  594.0 68.7 reduce-scatter.4
where the time goes:
time: 676 us; the launch traced here: 671 us
  waiting for transfers between devices  437 us (65%)
  blocking collectives  116 us (17%)
  matrix products  55.2 us (8%)
  local copies, waits for them, and re-layouts  29.7 us (4%)
  other arithmetic  18.9 us (3%)
  between operations  14 us (2%)
    all_gather x1, waiting for transfers between devices, shards(): lax.all_gather(head_cols, 'var', axis=1, tiled=True)  141 us
    psum x1, waiting for transfers between devices, shards(): token_state = lax.psum(partial_tokens, 'var')  139 us
    reduce_scatter x1, waiting for transfers between devices, shards(): lax.psum_scatter(jnp.dot(context, out_proj, preferred_element_type=jnp.fl...  67.3 us
    all_gather x1, waiting for transfers between devices, shards(): head_cols = lax.all_gather(pool_value, 'tok', axis=0, tiled=True)  54.4 us
    reduce_scatter x1, waiting for transfers between devices, shards(): lax.psum_scatter(numerator, 'var', scatter_dimension=1, tiled=True)  34.5 us
    pmax x1, blocking collectives, shards(): highest = lax.pmax(local_max, 'var')  33.9 us
    unnamed x1, blocking collectives  33.2 us
    all_gather x1, blocking collectives, shards(): value_part = lax.all_gather(value_rows, 'tok', axis=0, tiled=True)  27 us
  transfers between devices with their start and end apart: 5, of which 5 were waited for; matrix products, arithmetic and copies ran while one was open for 4% of the time, Pallas kernels for 0%

commit v1 on v0

v1 whole, which is shorter than its diff:
```python
import functools
import math

import jax
import jax.numpy as jnp
from jax import lax
from jax.experimental import pallas as pl
from jax.experimental.pallas import tpu as pltpu
from jax.sharding import PartitionSpec as P

F32 = jnp.float32
BF = jnp.bfloat16
N = 16
SLOTS = 6
TOK = 128
COLS = 256
D = 4096
E = 128
SCALE = 1.0 / math.sqrt(128)

R_U0, R_U1, R_P, R_WH, R_WL, R_M, R_ST, R_PC, ROWS = 0, 96, 192, 288, 384, 480, 528, 576, 608


def split2(x):
    hi = x.astype(BF)
    return hi, (x - hi.astype(F32)).astype(BF)


def split3(x):
    hi = x.astype(BF)
    rest = x - hi.astype(F32)
    mid = rest.astype(BF)
    return hi, mid, (rest - mid.astype(F32)).astype(BF)


def call(kernel, out_shape, n_in, scratch=(), smem=(), flops=0, size=0):
    specs = [
        pl.BlockSpec(memory_space=pltpu.SMEM if i in smem else pltpu.VMEM) for i in range(n_in)
    ]
    many = isinstance(out_shape, (tuple, list))
    vm = pl.BlockSpec(memory_space=pltpu.VMEM)
    return pl.pallas_call(
        kernel,
        out_shape=out_shape,
        in_specs=specs,
        out_specs=[vm] * len(out_shape) if many else vm,
        scratch_shapes=list(scratch),
        compiler_params=pltpu.CompilerParams(vmem_limit_bytes=48 * 1024 * 1024),
        cost_estimate=pl.CostEstimate(flops=flops, bytes_accessed=size, transcendentals=0),
    )


def embed_kernel(slot, patches, weight, table, gain, keys, pieces, out, columns, stats):
    wide = table.shape[0]
    row = lax.broadcasted_iota(jnp.int32, (8, wide), 0)
    col = lax.broadcasted_iota(jnp.int32, (8, wide), 1)
    pick = jnp.zeros((8, wide), F32)
    for s in range(SLOTS):
        pick = jnp.where((row == s) & (col == slot[s]), 1.0, pick)
    var_rows = jnp.dot(pick.astype(BF), table[...], preferred_element_type=F32)
    gain_row = gain[...].astype(F32)
    columns[...] = jnp.zeros_like(columns)
    for s in range(SLOTS):
        emb = lax.dot_general(
            patches[s], weight[s], (((0,), (0,)), ((), ())), preferred_element_type=F32
        )
        emb = emb + var_rows[s : s + 1]
        mean = jnp.sum(emb, axis=1, keepdims=True) * (1.0 / D)
        emb = emb - mean
        spread = jnp.sum(emb * emb, axis=1, keepdims=True) * (1.0 / D)
        rstd = lax.rsqrt(spread + 1e-05)
        normed = (emb * rstd * gain_row).astype(BF)
        columns[:, 16 * s : 16 * s + 16] = jnp.dot(
            normed, keys[...], preferred_element_type=F32
        )
        columns[:, 96 + s : 97 + s] = mean
        columns[:, 102 + s : 103 + s] = rstd
    turned = jnp.transpose(columns[...])
    scores = [
        jnp.where(slot[s] >= 0, turned[16 * s : 16 * s + 16] * SCALE, -1e30) for s in range(SLOTS)
    ]
    top = scores[0]
    for s in range(1, SLOTS):
        top = jnp.maximum(top, scores[s])
    w_hi, w_lo = [], []
    for s in range(SLOTS):
        hi, lo = split2(jnp.where(slot[s] >= 0, jnp.exp(scores[s] - top), 0.0))
        w_hi.append(hi)
        w_lo.append(lo)
    tops = split3(top)
    means = split3(turned[96:102])
    rstds = split3(turned[102:108])
    for i in range(3):
        stats[6 * i : 6 * i + 6] = means[i].astype(F32)
        stats[18 + 6 * i : 24 + 6 * i] = rstds[i].astype(F32)
    for v in range(N):
        for s in range(SLOTS):
            a = 16 * s
            out[v, R_U0 + a : R_U0 + a + 16] = weight[s, :, COLS * v : COLS * v + 128]
            out[v, R_U1 + a : R_U1 + a + 16] = weight[s, :, COLS * v + 128 : COLS * v + 256]
            out[v, R_P + a : R_P + a + 16] = patches[s]
            out[v, R_WH + a : R_WH + a + 16] = w_hi[s]
            out[v, R_WL + a : R_WL + a + 16] = w_lo[s]
        for i in range(3):
            out[v, R_M + 16 * i : R_M + 16 * i + 16] = tops[i]
        stats[36:42] = var_rows[:6, COLS * v : COLS * v + 128]
        stats[42:48] = var_rows[:6, COLS * v + 128 : COLS * v + 256]
        out[v, R_ST : R_ST + 48] = stats[...].astype(BF)
        out[v, R_PC : R_PC + 32] = pieces[v]


def pool_kernel(got, gain, value, out, weights, turned, rows, summed):
    tops = []
    for v in range(N):
        m = [got[v, R_M + 16 * i : R_M + 16 * i + 16].astype(F32) for i in range(3)]
        tops.append((m[0] + m[1]) + m[2])
    top = tops[0]
    for v in range(1, N):
        top = jnp.maximum(top, tops[v])
    total = jnp.zeros((16, TOK), F32)
    for v in range(N):
        factor = jnp.exp(tops[v] - top)
        for s in range(SLOTS):
            a = 16 * s
            w = got[v, R_WH + a : R_WH + a + 16].astype(F32) + got[
                v, R_WL + a : R_WL + a + 16
            ].astype(F32)
            w = w * factor
            total = total + w
            weights[96 * v + a : 96 * v + a + 16] = w
    inverse = 1.0 / total
    for h in range(N):
        w = weights[pl.ds(h, 96, stride=16)] * inverse[h : h + 1]
        w = jnp.transpose(jnp.concatenate([w, jnp.zeros((32, TOK), F32)], 0))
        hi = w.astype(BF).astype(F32)
        turned[pl.ds(h, TOK, stride=32)] = hi
        turned[pl.ds(16 + h, TOK, stride=32)] = (w - hi).astype(BF).astype(F32)
    gain_row = gain[...].astype(F32)

    def source(v, carry):
        st = got[v, R_ST : R_ST + 48].astype(F32)
        mean = (st[0:6] + st[6:12]) + st[12:18]
        rstd = (st[18:24] + st[24:30]) + st[30:36]
        both = jnp.concatenate([mean, rstd, jnp.zeros((116, TOK), F32)], 0)
        both = jnp.transpose(both)
        var0, var1 = st[36:42], st[42:48]
        for s in range(SLOTS):
            a = 16 * s
            p = got[v, R_P + a : R_P + a + 16]
            col_mean, col_rstd = both[:, s : s + 1], both[:, 6 + s : 7 + s]
            for half, var in ((0, var0), (1, var1)):
                u = got[v, 96 * half + a : 96 * half + a + 16]
                emb = lax.dot_general(
                    p, u, (((0,), (0,)), ((), ())), preferred_element_type=F32
                )
                emb = emb + var[s : s + 1]
                x = (emb - col_mean) * col_rstd * gain_row[:, 128 * half : 128 * half + 128]
                rows[half, pl.ds(6 * v + s, TOK, stride=96)] = x
        return carry

    lax.fori_loop(0, N, source, 0)

    def token(t, carry):
        at = pl.multiple_of(t * 96, 8)
        lhs = turned[pl.ds(pl.multiple_of(t * 32, 32), 32)].astype(BF)[:, :96]
        for half in range(2):
            rhs = rows[half, pl.ds(at, 96)].astype(BF)
            y = jnp.dot(lhs, rhs, preferred_element_type=F32)
            summed[half, pl.ds(t, 16, stride=TOK)] = y[:16] + y[16:]
        return carry

    lax.fori_loop(0, TOK, token, 0, unroll=8)
    for h in range(N):
        at = pl.ds(TOK * h, TOK)
        hi, lo = split2(jnp.concatenate([summed[0, at], summed[1, at]], 1))
        out[h] = jnp.dot(hi, value[h], preferred_element_type=F32) + jnp.dot(
            lo, value[h], preferred_element_type=F32
        )


def pooled_kernel(got, out):
    total = got[0]
    for v in range(1, N):
        total = total + got[v]
    total = total.astype(BF)
    for v in range(N):
        out[v] = total


def columns_of(blocks, weight):
    halves = []
    for half in range(2):
        acc = None
        for h in range(0, N, 2):
            left = jnp.concatenate([blocks[h], blocks[h + 1]], 1)
            right = jnp.concatenate(
                [weight[2 * j + half, h + i] for i in range(2) for j in range(8)], 0
            )
            term = jnp.dot(left, right, preferred_element_type=F32)
            acc = term if acc is None else acc + term
        halves.append(acc)
    return halves


def state_kernel(got, weight, state, aggregated, stats, columns):
    halves = columns_of(got, weight)
    mean = (
        jnp.sum(halves[0], axis=1, keepdims=True) + jnp.sum(halves[1], axis=1, keepdims=True)
    ) * (1.0 / COLS)
    spread = None
    for i in range(2):
        state[:, 128 * i : 128 * i + 128] = halves[i]
        aggregated[:, 128 * i : 128 * i + 128] = halves[i].astype(BF)
        c = halves[i] - mean
        term = jnp.sum(c * c, axis=1, keepdims=True)
        spread = term if spread is None else spread + term
    columns[...] = jnp.zeros_like(columns)
    columns[:, 0:1] = mean
    columns[:, 1:2] = spread
    turned = jnp.transpose(columns[...])[0:8]
    for v in range(N):
        stats[v] = turned


def norm_kernel(got, state, gain, out):
    mean = got[0, 0:1]
    for v in range(1, N):
        mean = mean + got[v, 0:1]
    mean = mean * (1.0 / N)
    spread = jnp.zeros((1, TOK), F32)
    for v in range(N):
        gap = got[v, 0:1] - mean
        spread = spread + (got[v, 1:2] + COLS * gap * gap)
    rstd = lax.rsqrt(spread * (1.0 / D) + 1e-05)
    both = jnp.transpose(jnp.concatenate([mean, rstd, jnp.zeros((126, TOK), F32)], 0))
    normed = ((state[...] - both[:, 0:1]) * both[:, 1:2] * gain[...].astype(F32)).astype(BF)
    for v in range(N):
        out[v] = normed


def project_kernel(got, weight, query, out):
    for c in range(3):
        acc = None
        for v in range(N):
            term = jnp.dot(
                got[v], weight[c, COLS * v : COLS * v + COLS], preferred_element_type=F32
            )
            acc = term if acc is None else acc + term
        acc = acc.astype(BF)
        if c == 0:
            query[...] = acc
        else:
            for k in range(N):
                out[k, TOK * (c - 1) : TOK * c] = acc


def attend_kernel(query, got, out, scores):
    q = query[...]
    peak = None
    for k in range(N):
        s = (
            lax.dot_general(
                q, got[k, 0:TOK], (((1,), (1,)), ((), ())), preferred_element_type=F32
            )
            * SCALE
        )
        scores[:, TOK * k : TOK * k + TOK] = s
        peak = s if peak is None else jnp.maximum(peak, s)
    peak = jnp.max(peak, axis=1, keepdims=True)
    total, acc = None, None
    for k in range(N):
        e = jnp.exp(scores[:, TOK * k : TOK * k + TOK] - peak)
        total = e if total is None else total + e
        term = jnp.dot(e.astype(BF), got[k, TOK : 2 * TOK], preferred_element_type=F32)
        acc = term if acc is None else acc + term
    context = (acc / jnp.sum(total, axis=1, keepdims=True)).astype(BF)
    for v in range(N):
        out[v] = context


def output_kernel(got, weight, out):
    halves = columns_of(got, weight)
    for i in range(2):
        out[:, 128 * i : 128 * i + 128] = halves[i].astype(BF)


def shape(dims, kind):
    return jax.ShapeDtypeStruct(dims, kind)


def exchange(x, axis):
    return lax.all_to_all(x, axis, 0, 0, tiled=True)


def shards(
    patches,
    slot_variable,
    embed_weight,
    variable_embed,
    norm_gain,
    pool_keys,
    pool_value,
    pool_out,
    block_gain,
    attend_weight,
    out_proj,
):
    v_idx, k_idx = lax.axis_index("var"), lax.axis_index("tok")

    swap = [(v * N + k, k * N + v) for v in range(N) for k in range(N)]
    value = lax.ppermute(pool_value, ("var", "tok"), swap)
    value = lax.all_gather(value, "tok", axis=0)

    def piece(weight):
        rows = lax.dynamic_slice(weight, (16 * (k_idx // 2), 0), (16, D))
        rows = rows.reshape(16, N, 2, 128)
        rows = lax.dynamic_index_in_dim(rows, k_idx % 2, 2, keepdims=False)
        return jnp.transpose(rows, (1, 0, 2))

    pieces = jnp.concatenate([piece(pool_out), piece(out_proj)], 1)
    packed = call(
        embed_kernel,
        shape((N, ROWS, 128), BF),
        7,
        (pltpu.VMEM((TOK, 128), F32), pltpu.VMEM((48, 128), F32)),
        smem=(0,),
        flops=2 * SLOTS * TOK * D * 48,
        size=6_000_000,
    )(
        slot_variable,
        patches,
        embed_weight,
        variable_embed,
        norm_gain[None],
        pool_keys,
        pieces,
    )
    got = exchange(packed, "var")
    out_rows = lax.all_gather(got[:, R_PC : R_PC + 16], "tok", axis=0)
    proj_rows = lax.all_gather(got[:, R_PC + 16 : R_PC + 32], "tok", axis=0)

    def own_columns(gain):
        return lax.dynamic_slice(gain, (COLS * v_idx,), (COLS,))[None]

    partial = call(
        pool_kernel,
        shape((N, TOK, E), F32),
        3,
        (
            pltpu.VMEM((96 * N, TOK), F32),
            pltpu.VMEM((TOK * 32, TOK), F32),
            pltpu.VMEM((2, TOK * 96, 128), F32),
            pltpu.VMEM((2, N * TOK, 128), F32),
        ),
        flops=2 * 400_000_000,
        size=5_000_000,
    )(got, own_columns(norm_gain), value)
    pooled = call(pooled_kernel, shape((N, TOK, E), BF), 1, size=1_500_000)(
        exchange(partial, "var")
    )
    state, aggregated, stats = call(
        state_kernel,
        (shape((TOK, COLS), F32), shape((TOK, COLS), BF), shape((N, 8, 128), F32)),
        2,
        (pltpu.VMEM((TOK, 128), F32),),
        flops=2 * TOK * 2048 * COLS,
        size=2_000_000,
    )(exchange(pooled, "var"), out_rows)
    normed = call(norm_kernel, shape((N, TOK, COLS), BF), 3, size=1_200_000)(
        exchange(stats, "var"), state, own_columns(block_gain)
    )
    query, kv = call(
        project_kernel,
        (shape((TOK, E), BF), shape((N, 2 * TOK, E), BF)),
        2,
        flops=2 * TOK * D * 384,
        size=5_000_000,
    )(exchange(normed, "var"), attend_weight)
    context = call(
        attend_kernel,
        shape((N, TOK, E), BF),
        2,
        (pltpu.VMEM((TOK, N * TOK), F32),),
        flops=4 * TOK * 2048 * E,
        size=1_500_000,
    )(query, exchange(kv, "tok"))
    attended = call(
        output_kernel, shape((TOK, COLS), BF), 2, flops=2 * TOK * 2048 * COLS, size=2_000_000
    )(exchange(context, "var"), proj_rows)
    return (aggregated, attended)


def solution(mesh):
    return jax.shard_map(
        shards,
        mesh=mesh,
        in_specs=(
            P("var", None, "tok"),
            P("var"),
            P("var", None, None),
            P(),
            P(),
            P(),
            P("tok", "var"),
            P("var", None),
            P(),
            P(None, None, "var"),
            P("var", None),
        ),
        out_specs=(P("tok", "var"), P("tok", "var")),
        check_vma=False,
    )
```

time: 676 us -> 354 us (0.52)
  waiting for transfers between devices: 437 us -> 208 us
  blocking collectives: 116 us -> 30.2 us
  matrix products: 55.2 us -> 0 us
  starting transfers between devices: 0.42 us -> 44.8 us
  Pallas kernels: 0 us -> 40.4 us
  other arithmetic: 18.9 us -> 0.01 us
  local copies, waits for them, and re-layouts: 29.7 us -> 13.1 us
    psum x1 -> x0, waiting for transfers between devices: 139 us -> none  [shards(): token_state = lax.psum(partial_tokens, 'var')]
    reduce_scatter x2 -> x0, waiting for transfers between devices: 102 us -> none  [the longest x1 67.3 us: shards(): lax.psum_scatter(jnp.dot(context, out_proj, preferred_element_type=jnp.fl...]
    all_gather x2 -> x3, waiting for transfers between devices: 195 us -> 107 us  [the longest x1 56.5 us: shards(): value = lax.all_gather(value, 'tok', axis=0)]
    dot_general x9 -> x0, matrix products: 55.2 us -> none  [the longest x1 20 us: shards(): jnp.einsum('tsh,tshe->the', weights, values, precision=lax.Precision.HIGH...]
    ppermute x0 -> x1, waiting for transfers between devices: none -> 51.7 us  [shards(): value = lax.ppermute(pool_value, ('var', 'tok'), swap)]
    all_to_all x0 -> x6, waiting for transfers between devices: none -> 49.4 us  [exchange(): return lax.all_to_all(x, axis, 0, 0, tiled=True)]
    all_gather x2 -> x0, blocking collectives: 48.6 us -> none  [the longest x1 27 us: shards(): value_part = lax.all_gather(value_rows, 'tok', axis=0, tiled=True)]
    all_to_all x0 -> x6, starting transfers between devices: none -> 40.9 us  [exchange(): return lax.all_to_all(x, axis, 0, 0, tiled=True)]
  transfers between devices with their start and end apart: 5 -> 10, of which waited for: 5 -> 7; matrix products, arithmetic and copies ran while one was open for 4% -> 0% of each run, Pallas kernels for 0% -> 1%
where the time goes in v1:
time: 354 us; the launch traced here: 351 us
  waiting for transfers between devices  208 us (59%)
  starting transfers between devices  44.8 us (13%)
  Pallas kernels  40.4 us (11%)
  blocking collectives  30.2 us (9%)
  between operations  14 us (4%)
  local copies, waits for them, and re-layouts  13.1 us (4%)
    all_gather x1, waiting for transfers between devices, shards(): value = lax.all_gather(value, 'tok', axis=0)  56.5 us
    ppermute x1, waiting for transfers between devices, shards(): value = lax.ppermute(pool_value, ('var', 'tok'), swap)  51.7 us
    all_to_all x6, waiting for transfers between devices, exchange(): return lax.all_to_all(x, axis, 0, 0, tiled=True)  49.4 us
    all_to_all x6, starting transfers between devices, exchange(): return lax.all_to_all(x, axis, 0, 0, tiled=True)  40.9 us
    all_to_all x1, blocking collectives, exchange(): return lax.all_to_all(x, axis, 0, 0, tiled=True)  30.2 us
    all_gather x1, waiting for transfers between devices, shards(): proj_rows = lax.all_gather(got[:, R_PC + 16:R_PC + 32], 'tok', axis=0)  27.4 us
    pallas_call x1, Pallas kernels, shards(): call(pool_kernel, shape((N, TOK, E), F32), 3, (pltpu.VMEM((96 * N, TOK),...  25.4 us
    all_gather x1, waiting for transfers between devices, shards(): out_rows = lax.all_gather(got[:, R_PC:R_PC + 16], 'tok', axis=0)  22.8 us
  transfers between devices with their start and end apart: 10, of which 7 were waited for; matrix products, arithmetic and copies ran while one was open for 0% of the time, Pallas kernels for 1%

profile of v1, /device:TPU:34, one launch (start us, length us, event | category | flops | bytes accessed | tf_op | source)
XLA Modules:
  0.0 350.9 jit_solution(2064725471742123860)
XLA Ops:
  7.2 1.1 constant_dynamic-slice_fusion.1
  8.9 1.4 copy.19.keys
  10.4 8.5 %shard_map.122 = bf16[16,608,128]{2,1,0:T(8,128)(2,1)S(1)} custom-call(s32[6]{0:T(128)S(1)} %copy-done.11, bf16[6,16,128]{2,1,0:T(8,128)(2,1)S(1)} %copy-done.10, bf16[6,16,4096]{2,1,0:T(8,128)(2,1)S(1)} %copy-done.8, bf16[91,4096]{1,0:T(8,128)(2,1)S(1)} %copy-done.9, bf16[1,4096]{1,0:T(2,128)(2,1)S(1)} %broadcast_in_dim.9.gain, ...), custom_call_target="tpu_custom_call" | custom-call | flops 301989888 | bytes 6000000 | tf_op jit(solution)/shard_map/pallas_call | solution.py:321
  18.9 1.5 copy-done
  20.4 9.6 %all-to-all-start = ((bf16[16,608,128]{2,1,0:T(8,128)(2,1)}), bf16[16,608,128]{2,1,0:T(8,128)(2,1)S(1)}, u32[]{:S(2)}, u32[]{:S(2)}) async-start(bf16[16,608,128]{2,1,0:T(8,128)(2,1)} %copy-done), calls=%async_computation | async-start | bytes 4980736 | tf_op jit(solution)/shard_map/all_to_all | solution.py:292
  30.0 3.8 %collective-permute-start = (bf16[256,128]{1,0:T(8,128)(2,1)S(1)}, bf16[256,128]{1,0:T(8,128)(2,1)S(1)}, u32[]{:S(2)}, u32[]{:S(2)}) collective-permute-start(bf16[256,128]{1,0:T(8,128)(2,1)S(1)} %copy-done.14), channel_id=1, source_target_pairs={{0,0},{1,16},{2,32},{3,48},{4,64},{5,80},{6,96},{7,112},{8,128},{9... | collective-permute-start | bytes 196616 | tf_op jit(solution)/shard_map/ppermute | solution.py:311
  33.8 51.7 %collective-permute-done = bf16[256,128]{1,0:T(8,128)(2,1)S(1)} collective-permute-done((bf16[256,128]{1,0:T(8,128)(2,1)S(1)}, bf16[256,128]{1,0:T(8,128)(2,1)S(1)}, u32[]{:S(2)}, u32[]{:S(2)}) %collective-permute-start) | collective-permute-done | bytes 65568 | tf_op jit(solution)/shard_map/ppermute | solution.py:311
  86.3 56.5 %all-gather.7.cloned.1.call-done = bf16[4096,128]{1,0:T(8,128)(2,1)} async-done(((bf16[256,128]{1,0:T(8,128)(2,1)}), bf16[4096,128]{1,0:T(8,128)(2,1)}) %all-gather.7.cloned.1.call-update) | async-done | bytes 1048592 | tf_op jit(solution)/shard_map/all_gather | solution.py:312
  142.7 1.2 copy-done.4
  144.0 25.4 %shard_map.123 = f32[16,128,128]{2,1,0:T(8,128)} custom-call(bf16[16,608,128]{2,1,0:T(8,128)(2,1)S(1)} %all-to-all-done.got, bf16[1,256]{1,0:T(2,128)(2,1)S(1)} %broadcast_in_dim.10.gain, bf16[16,256,128]{2,1,0:T(8,128)(2,1)S(1)} %bitcast.13), custom_call_target="tpu_custom_call" | custom-call | flops 800000000 | bytes 5000000 | tf_op jit(solution)/shard_map/pallas_call | solution.py:345
  169.3 8.4 %all-to-all-start.1 = ((f32[16,128,128]{2,1,0:T(8,128)}), f32[16,128,128]{2,1,0:T(8,128)S(1)}, u32[]{:S(2)}, u32[]{:S(2)}) async-start(f32[16,128,128]{2,1,0:T(8,128)} %shard_map.123), calls=%async_computation.1 | async-start | bytes 2097152 | tf_op jit(solution)/shard_map/all_to_all | solution.py:292
  178.5 26.0 %all-to-all-done.1.got = f32[16,128,128]{2,1,0:T(8,128)S(1)} async-done(((f32[16,128,128]{2,1,0:T(8,128)}), f32[16,128,128]{2,1,0:T(8,128)S(1)}, u32[]{:S(2)}, u32[]{:S(2)}) %all-to-all-start.1) | async-done | bytes 1048608 | tf_op jit(solution)/shard_map/all_to_all | solution.py:292
  204.5 0.9 shard_map.124
  205.4 5.2 %all-to-all-start.2 = ((bf16[16,128,128]{2,1,0:T(8,128)(2,1)}), bf16[16,128,128]{2,1,0:T(8,128)(2,1)S(1)}, u32[]{:S(2)}, u32[]{:S(2)}) async-start(bf16[16,128,128]{2,1,0:T(8,128)(2,1)} %shard_map.124), calls=%async_computation.2 | async-start | bytes 1048576 | tf_op jit(solution)/shard_map/all_to_all | solution.py:292
  210.6 22.8 %all-gather.9.cloned.1.call-done = bf16[256,16,128]{2,1,0:T(8,128)(2,1)} async-done(((bf16[16,16,128]{2,1,0:T(8,128)(2,1)}), bf16[256,16,128]{2,1,0:T(8,128)(2,1)}) %all-gather.9.cloned.1.call-update) | async-done | bytes 1048592 | tf_op jit(solution)/shard_map/all_gather | solution.py:339
  233.4 0.8 copy-done.2
  234.2 1.0 copy-done.3
  235.2 1.2 copy-done.5
  236.4 1.3 shard_map.125
  237.7 7.0 %all-to-all-start.3 = ((f32[16,8,128]{2,1,0:T(8,128)}), f32[16,8,128]{2,1,0:T(8,128)S(1)}, u32[]{:S(2)}, u32[]{:S(2)}) async-start(f32[16,8,128]{2,1,0:T(8,128)} %get-tuple-element.8), calls=%async_computation.3 | async-start | bytes 131072 | tf_op jit(solution)/shard_map/all_to_all | solution.py:292
  244.6 0.8 dynamic_slice.24
  245.4 6.1 %all-to-all-done.3.got = f32[16,8,128]{2,1,0:T(8,128)S(1)} async-done(((f32[16,8,128]{2,1,0:T(8,128)}), f32[16,8,128]{2,1,0:T(8,128)S(1)}, u32[]{:S(2)}, u32[]{:S(2)}) %all-to-all-start.3) | async-done | bytes 65568 | tf_op jit(solution)/shard_map/all_to_all | solution.py:292
  251.8 30.2 %all_to_all.35.got = bf16[16,128,256]{2,1,0:T(8,128)(2,1)S(1)} all-to-all(bf16[16,128,256]{2,1,0:T(8,128)(2,1)S(1)} %shard_map.126), channel_id=1, replica_groups=mesh['var'=16,'tok'=16] {'var'}, dimensions={0} | all-to-all | bytes 2097152 | tf_op jit(solution)/shard_map/all_to_all | solution.py:292
  281.9 1.0 shard_map.127
  282.9 1.0 copy-done.7
  283.9 5.6 %all-to-all-start.5 = ((bf16[16,256,128]{2,1,0:T(8,128)(2,1)}), bf16[16,256,128]{2,1,0:T(8,128)(2,1)S(1)}, u32[]{:S(2)}, u32[]{:S(2)}) async-start(bf16[16,256,128]{2,1,0:T(8,128)(2,1)} %copy-done.7), calls=%async_computation.5 | async-start | bytes 2097152 | tf_op jit(solution)/shard_map/all_to_all | solution.py:292
  290.3 17.3 %all-to-all-done.5.got = bf16[16,256,128]{2,1,0:T(8,128)(2,1)S(1)} async-done(((bf16[16,256,128]{2,1,0:T(8,128)(2,1)}), bf16[16,256,128]{2,1,0:T(8,128)(2,1)S(1)}, u32[]{:S(2)}, u32[]{:S(2)}) %all-to-all-start.5) | async-done | bytes 1048608 | tf_op jit(solution)/shard_map/all_to_all | solution.py:292
  307.6 2.0 shard_map.128
  309.6 5.1 %all-to-all-start.6 = ((bf16[16,128,128]{2,1,0:T(8,128)(2,1)}), bf16[16,128,128]{2,1,0:T(8,128)(2,1)S(1)}, u32[]{:S(2)}, u32[]{:S(2)}) async-start(bf16[16,128,128]{2,1,0:T(8,128)(2,1)} %shard_map.128), calls=%async_computation.6 | async-start | bytes 1048576 | tf_op jit(solution)/shard_map/all_to_all | solution.py:292
  314.7 27.4 %all-gather.11.cloned.1.call-done = bf16[256,16,128]{2,1,0:T(8,128)(2,1)} async-done(((bf16[16,16,128]{2,1,0:T(8,128)(2,1)}), bf16[256,16,128]{2,1,0:T(8,128)(2,1)}) %all-gather.11.cloned.1.call-update) | async-done | bytes 1048592 | tf_op jit(solution)/shard_map/all_gather | solution.py:340
  342.1 1.2 copy-done.6
  343.3 1.1 shard_map.129
  (45 shorter events, 3.1 us)
Async XLA Ops:
  7.2 3.1 copy-start.13
  7.2 3.2 copy-start.10
  7.2 3.2 copy-start.11
  7.2 3.2 copy-start.8
  7.2 3.2 copy-start.9
  18.9 1.5 copy-start
  20.4 9.7 %copy-start.14 = (bf16[256,128]{1,0:T(8,128)(2,1)S(1)}, bf16[256,128]{1,0:T(8,128)(2,1)}, u32[]{:S(2)}) copy-start(bf16[256,128]{1,0:T(8,128)(2,1)} %param.17) | copy-start | bytes 196612
  20.4 122.4 %all-to-all-start = ((bf16[16,608,128]{2,1,0:T(8,128)(2,1)}), bf16[16,608,128]{2,1,0:T(8,128)(2,1)S(1)}, u32[]{:S(2)}, u32[]{:S(2)}) async-start(bf16[16,608,128]{2,1,0:T(8,128)(2,1)} %copy-done), calls=%async_computation | async-start | bytes 4980736 | tf_op jit(solution)/shard_map/all_to_all | solution.py:292
  30.0 112.7 %all-gather.7.cloned.1.call-start = ((), (), s32[]{:S(2)}) async-start(), calls=%async_computation.7 | async-start | bytes 1114112 | tf_op jit(solution)/shard_map/all_gather | solution.py:312
  30.0 55.5 %collective-permute-start = (bf16[256,128]{1,0:T(8,128)(2,1)S(1)}, bf16[256,128]{1,0:T(8,128)(2,1)S(1)}, u32[]{:S(2)}, u32[]{:S(2)}) collective-permute-start(bf16[256,128]{1,0:T(8,128)(2,1)S(1)} %copy-done.14), channel_id=1, source_target_pairs={{0,0},{1,16},{2,32},{3,48},{4,64},{5,80},{6,96},{7,112},{8,128},{9... | collective-permute-start | bytes 196616 | tf_op jit(solution)/shard_map/ppermute | solution.py:311
  85.5 0.6 copy-start.12
  142.7 1.2 copy-start.4
  169.3 35.2 %all-to-all-start.1 = ((f32[16,128,128]{2,1,0:T(8,128)}), f32[16,128,128]{2,1,0:T(8,128)S(1)}, u32[]{:S(2)}, u32[]{:S(2)}) async-start(f32[16,128,128]{2,1,0:T(8,128)} %shard_map.123), calls=%async_computation.1 | async-start | bytes 2097152 | tf_op jit(solution)/shard_map/all_to_all | solution.py:292
  177.8 55.6 %all-gather.9.cloned.1.call-start = ((), (), s32[]{:S(2)}) async-start(), calls=%async_computation.8 | async-start | bytes 1114112 | tf_op jit(solution)/shard_map/all_gather | solution.py:339
  205.4 28.0 %all-to-all-start.2 = ((bf16[16,128,128]{2,1,0:T(8,128)(2,1)}), bf16[16,128,128]{2,1,0:T(8,128)(2,1)S(1)}, u32[]{:S(2)}, u32[]{:S(2)}) async-start(bf16[16,128,128]{2,1,0:T(8,128)(2,1)} %shard_map.124), calls=%async_computation.2 | async-start | bytes 1048576 | tf_op jit(solution)/shard_map/all_to_all | solution.py:292
  233.4 0.8 copy-start.2
  234.2 1.0 copy-start.3
  235.2 1.2 copy-start.5
  236.4 45.5 %copy-start.1 = (bf16[3,4096,128]{2,1,0:T(8,128)(2,1)S(1)}, bf16[3,4096,128]{2,1,0:T(8,128)(2,1)}, u32[]{:S(2)}) copy-start(bf16[3,4096,128]{2,1,0:T(8,128)(2,1)} %weight.3) | copy-start | bytes 9437188
  237.7 13.8 %all-to-all-start.3 = ((f32[16,8,128]{2,1,0:T(8,128)}), f32[16,8,128]{2,1,0:T(8,128)S(1)}, u32[]{:S(2)}, u32[]{:S(2)}) async-start(f32[16,8,128]{2,1,0:T(8,128)} %get-tuple-element.8), calls=%async_computation.3 | async-start | bytes 131072 | tf_op jit(solution)/shard_map/all_to_all | solution.py:292
  282.9 1.0 copy-start.7
  283.9 23.7 %all-to-all-start.5 = ((bf16[16,256,128]{2,1,0:T(8,128)(2,1)}), bf16[16,256,128]{2,1,0:T(8,128)(2,1)S(1)}, u32[]{:S(2)}, u32[]{:S(2)}) async-start(bf16[16,256,128]{2,1,0:T(8,128)(2,1)} %copy-done.7), calls=%async_computation.5 | async-start | bytes 2097152 | tf_op jit(solution)/shard_map/all_to_all | solution.py:292
  289.5 52.6 %all-gather.11.cloned.1.call-start = ((), (), s32[]{:S(2)}) async-start(), calls=%async_computation.9 | async-start | bytes 1114112 | tf_op jit(solution)/shard_map/all_gather | solution.py:340
  309.6 32.5 %all-to-all-start.6 = ((bf16[16,128,128]{2,1,0:T(8,128)(2,1)}), bf16[16,128,128]{2,1,0:T(8,128)(2,1)S(1)}, u32[]{:S(2)}, u32[]{:S(2)}) async-start(bf16[16,128,128]{2,1,0:T(8,128)(2,1)} %shard_map.128), calls=%async_computation.6 | async-start | bytes 1048576 | tf_op jit(solution)/shard_map/all_to_all | solution.py:292
  342.1 1.2 copy-start.6
Sparse Core Ops, SparseCore 0:
  86.3 56.3 all-gather.6
  181.9 51.3 all-gather.8
  293.7 48.3 all-gather.10

commit v2 on v1

v2 whole, which is shorter than its diff:
```python
import functools
import math

import jax
import jax.numpy as jnp
from jax import lax
from jax.experimental import pallas as pl
from jax.experimental.pallas import tpu as pltpu
from jax.sharding import PartitionSpec as P

F32 = jnp.float32
BF = jnp.bfloat16
N = 16
SLOTS = 6
TOK = 128
COLS = 256
D = 4096
E = 128
SCALE = 1.0 / math.sqrt(128)

Z = 8
WIDE = 512
HALF = 48


R_U, R_P, R_WH, R_WL, R_M, R_ST, ROWS = 0, 384, 480, 576, 672, 720, 784
W_V, W_P, W_O, W_ROWS = 0, 32, 48, 64


def split2(x):
    hi = x.astype(BF)
    return hi, (x - hi.astype(F32)).astype(BF)


def split3(x):
    hi = x.astype(BF)
    rest = x - hi.astype(F32)
    mid = rest.astype(BF)
    return hi, mid, (rest - mid.astype(F32)).astype(BF)


def call(
    kernel, out_shape, n_in, scratch=(), smem=(), unread=(), blocks=None, vmem=24, flops=0, size=0
):
    many = isinstance(out_shape, (tuple, list))
    shapes = list(out_shape) if many else [out_shape]
    spaces = {i: pltpu.SMEM for i in smem} | {i: pl.ANY for i in unread}
    blocks = blocks or {}
    specs = []
    for i in range(n_in):
        if i in blocks:
            part, index = blocks[i]
            specs.append(pl.BlockSpec(part, index, pipeline_mode=pl.Buffered(1)))
        else:
            specs.append(pl.BlockSpec(memory_space=spaces.get(i, pltpu.VMEM)))
    outs = [pl.BlockSpec(memory_space=pltpu.VMEM)] * len(shapes)
    return pl.pallas_call(
        kernel,
        out_shape=out_shape,
        grid=(1,) if blocks else (),
        in_specs=specs,
        out_specs=outs if many else outs[0],
        scratch_shapes=list(scratch),
        compiler_params=pltpu.CompilerParams(vmem_limit_bytes=vmem * 1024 * 1024),
        cost_estimate=pl.CostEstimate(flops=flops, bytes_accessed=size, transcendentals=0),
    )


def weights_kernel(place, value, pool_rows, proj_rows, out):
    half = place[0] % 2
    for v in range(N):
        z = v % Z
        out[v, W_V : W_V + 32] = value[32 * z : 32 * z + 32]
        at = pl.ds(pl.multiple_of(COLS * v + 128 * half, 128), 128)
        out[v, W_P : W_P + 16] = pool_rows[:, at]
        out[v, W_O : W_O + 16] = proj_rows[:, at]


def embed_kernel(slot, patches, weight, table, gain, keys, common, var_out, columns):
    wide = table.shape[0]
    row = lax.broadcasted_iota(jnp.int32, (8, wide), 0)
    col = lax.broadcasted_iota(jnp.int32, (8, wide), 1)
    pick = jnp.zeros((8, wide), F32)
    for s in range(SLOTS):
        pick = jnp.where((row == s) & (col == slot[s]), 1.0, pick)
    var_rows = jnp.dot(pick.astype(BF), table[...], preferred_element_type=F32)
    var_out[...] = var_rows
    gain_row = gain[...].astype(F32)
    columns[...] = jnp.zeros_like(columns)
    scores = []
    for s in range(SLOTS):
        emb = lax.dot_general(
            patches[s], weight[s], (((0,), (0,)), ((), ())), preferred_element_type=F32
        )
        emb = emb + var_rows[s : s + 1]
        mean = jnp.sum(emb, axis=1, keepdims=True) * (1.0 / D)
        emb = emb - mean
        spread = jnp.sum(emb * emb, axis=1, keepdims=True) * (1.0 / D)
        rstd = lax.rsqrt(spread + 1e-05)
        normed = (emb * rstd * gain_row).astype(BF)
        score = lax.dot_general(
            keys[...], normed, (((1,), (1,)), ((), ())), preferred_element_type=F32
        )
        scores.append(jnp.where(slot[s] >= 0, score * SCALE, -1e30))
        columns[:, s : s + 1] = mean
        columns[:, 6 + s : 7 + s] = rstd
    turned = jnp.transpose(columns[...])
    top = scores[0]
    for s in range(1, SLOTS):
        top = jnp.maximum(top, scores[s])
    for s in range(SLOTS):
        a = 16 * s
        hi, lo = split2(jnp.where(slot[s] >= 0, jnp.exp(scores[s] - top), 0.0))
        common[R_P - R_P + a : R_P - R_P + a + 16] = patches[s]
        common[R_WH - R_P + a : R_WH - R_P + a + 16] = hi
        common[R_WL - R_P + a : R_WL - R_P + a + 16] = lo
    tops = split3(top)
    stats = []
    for rows in (turned[0:6], turned[6:12]):
        stats.extend(x.astype(F32) for x in split3(rows))
    stats.append(jnp.zeros((28, TOK), F32))
    for i in range(3):
        common[R_M - R_P + 16 * i : R_M - R_P + 16 * i + 16] = tops[i]
    common[R_ST - R_P :] = jnp.concatenate(stats, 0).astype(BF)


def chunks(x, z, j):
    at = [256 * k + 32 * z for k in range(4 * j, 4 * j + 4)]
    return jnp.concatenate([x[:, a : a + 32] for a in at], 1)


def pack_kernel(weight, common, var_rows, early, out):
    for s in range(SLOTS):
        wide = weight[s].astype(F32)
        for z in range(Z):
            for j in range(4):
                a = R_U + 96 * j + 16 * s
                out[z, a : a + 16] = chunks(wide, z, j).astype(BF)
    stats = common[R_ST - R_P :].astype(F32)[:36]
    for z in range(Z):
        out[z, R_P:R_ST] = common[0 : R_ST - R_P]
        rows = [stats] + [chunks(var_rows[...], z, j)[:6] for j in range(4)]
        rows.append(jnp.zeros((4, TOK), F32))
        out[z, R_ST:] = jnp.concatenate(rows, 0).astype(BF)


def pool_kernel(got, gain, summed, tails, weights, turned, rows):
    tops = []
    for z in range(Z):
        m = [got[z, R_M + 16 * i : R_M + 16 * i + 16].astype(F32) for i in range(3)]
        tops.append((m[0] + m[1]) + m[2])
    top = tops[0]
    for z in range(1, Z):
        top = jnp.maximum(top, tops[z])
    total = jnp.zeros((16, TOK), F32)
    for z in range(Z):
        factor = jnp.exp(tops[z] - top)
        for s in range(SLOTS):
            a = 16 * s
            w = got[z, R_WH + a : R_WH + a + 16].astype(F32) + got[
                z, R_WL + a : R_WL + a + 16
            ].astype(F32)
            w = w * factor
            total = total + w
            weights[96 * z + a : 96 * z + a + 16] = w
    lane = lax.broadcasted_iota(jnp.int32, (HALF, TOK), 1)
    for h in range(N):
        w = weights[pl.ds(h, HALF, stride=16)]
        parts = [jnp.where(lane % 4 == q, w, 0.0) for q in range(4)]
        parts.append(jnp.zeros((256 - 4 * HALF, TOK), F32))
        w = jnp.concatenate(parts, 0)
        for i in range(2):
            part = jnp.transpose(w[128 * i : 128 * i + 128])
            hi = part.astype(BF).astype(F32)
            turned[i, pl.ds(h, TOK, stride=32)] = hi
            turned[i, pl.ds(16 + h, TOK, stride=32)] = (part - hi).astype(BF).astype(F32)
    gain_row = gain[...].astype(F32)

    def source(z, carry):
        st = got[z, R_ST : R_ST + 64].astype(F32)
        mean = (st[0:6] + st[6:12]) + st[12:18]
        rstd = (st[18:24] + st[24:30]) + st[30:36]
        both = jnp.transpose(jnp.concatenate([mean, rstd, jnp.zeros((116, TOK), F32)], 0))
        for s in range(SLOTS):
            a = 16 * s
            p = got[z, R_P + a : R_P + a + 16]
            col_mean, col_rstd = both[:, s : s + 1], both[:, 6 + s : 7 + s]
            for i in range(2):
                u = jnp.concatenate(
                    [got[z, 96 * j + a : 96 * j + a + 16] for j in (2 * i, 2 * i + 1)], 1
                )
                emb = lax.dot_general(
                    p, u, (((0,), (0,)), ((), ())), preferred_element_type=F32
                )
                for n in range(2):
                    j = 2 * i + n
                    var = st[36 + 6 * j + s : 37 + 6 * j + s]
                    x = emb[:, 128 * n : 128 * n + 128] + var
                    x = (x - col_mean) * col_rstd * gain_row[:, 128 * j : 128 * j + 128]
                    rows[j, pl.ds(6 * z + s, TOK, stride=HALF)] = x
        return carry

    lax.fori_loop(0, Z, source, 0)

    def four_tokens(g, carry):
        at = pl.ds(pl.multiple_of(g * 128, 128), 128)
        lhs = jnp.concatenate([turned[0, at], turned[1, at][:, : 4 * HALF - 128]], 1).astype(BF)
        span = pl.ds(pl.multiple_of(g * 4 * HALF, 4 * HALF), 4 * HALF)
        for i in range(2):
            rhs = jnp.concatenate([rows[2 * i, span], rows[2 * i + 1, span]], 1).astype(BF)
            y = jnp.dot(lhs, rhs, preferred_element_type=F32)
            for q in range(4):
                part = y[32 * q : 32 * q + 16] + y[32 * q + 16 : 32 * q + 32]
                for n in range(2):
                    summed[2 * i + n, pl.ds(4 * g + q, 16, stride=TOK)] = part[
                        :, 128 * n : 128 * n + 128
                    ]
        return carry

    lax.fori_loop(0, TOK // 4, four_tokens, 0, unroll=4)
    tails[0] = top
    tails[1] = total


def values_kernel(summed, tails, value, out):
    for h in range(N):
        at = pl.ds(TOK * h, TOK)
        hi, lo = split2(jnp.concatenate([summed[j, at] for j in range(4)], 1))
        right = jnp.concatenate([value[k, h] for k in range(N)], 0)
        out[h, 0:TOK] = jnp.dot(hi, right, preferred_element_type=F32) + jnp.dot(
            lo, right, preferred_element_type=F32
        )
        out[h, TOK : TOK + 1] = tails[0, h : h + 1]
        out[h, TOK + 1 : TOK + 2] = tails[1, h : h + 1]
        out[h, TOK + 2 : TOK + 8] = jnp.zeros((6, TOK), F32)


def pooled_kernel(got, out):
    tops = [got[Z * x, TOK : TOK + 1] for x in range(2)]
    totals = [got[Z * x, TOK + 1 : TOK + 2] for x in range(2)]
    top = jnp.maximum(tops[0], tops[1])
    factors = [jnp.exp(t - top) for t in tops]
    total = factors[0] * totals[0] + factors[1] * totals[1]
    both = jnp.concatenate([f / total for f in factors] + [jnp.zeros((126, TOK), F32)], 0)
    both = jnp.transpose(both)
    pooled = None
    for x in range(2):
        part = got[Z * x, 0:TOK]
        for z in range(1, Z):
            part = part + got[Z * x + z, 0:TOK]
        part = part * both[:, x : x + 1]
        pooled = part if pooled is None else pooled + part
    pooled = pooled.astype(BF)
    for v in range(N):
        out[v] = pooled


def columns_of(blocks, weight):
    halves = []
    for half in range(2):
        acc = None
        for h in range(0, N, 2):
            left = jnp.concatenate([blocks[h], blocks[h + 1]], 1)
            right = jnp.concatenate(
                [weight[2 * j + half, h + i] for i in range(2) for j in range(8)], 0
            )
            term = jnp.dot(left, right, preferred_element_type=F32)
            acc = term if acc is None else acc + term
        halves.append(acc)
    return halves


def state_kernel(got, weight, state, aggregated, stats, columns):
    halves = columns_of(got, weight)
    mean = (
        jnp.sum(halves[0], axis=1, keepdims=True) + jnp.sum(halves[1], axis=1, keepdims=True)
    ) * (1.0 / COLS)
    spread = None
    for i in range(2):
        state[:, 128 * i : 128 * i + 128] = halves[i]
        aggregated[:, 128 * i : 128 * i + 128] = halves[i].astype(BF)
        c = halves[i] - mean
        term = jnp.sum(c * c, axis=1, keepdims=True)
        spread = term if spread is None else spread + term
    columns[...] = jnp.zeros_like(columns)
    columns[:, 0:1] = mean
    columns[:, 1:2] = spread
    turned = jnp.transpose(columns[...])[0:8]
    for v in range(N):
        stats[v] = turned


def norm_kernel(got, state, gain, out):
    mean = got[0, 0:1]
    for v in range(1, N):
        mean = mean + got[v, 0:1]
    mean = mean * (1.0 / N)
    spread = jnp.zeros((1, TOK), F32)
    for v in range(N):
        gap = got[v, 0:1] - mean
        spread = spread + (got[v, 1:2] + COLS * gap * gap)
    rstd = lax.rsqrt(spread * (1.0 / D) + 1e-05)
    both = jnp.transpose(jnp.concatenate([mean, rstd, jnp.zeros((126, TOK), F32)], 0))
    normed = ((state[...] - both[:, 0:1]) * both[:, 1:2] * gain[...].astype(F32)).astype(BF)
    for v in range(N):
        out[v] = normed


def project_kernel(got, weight, query, out):
    for c in range(3):
        acc = None
        for v in range(N):
            term = jnp.dot(
                got[v], weight[c, COLS * v : COLS * v + COLS], preferred_element_type=F32
            )
            acc = term if acc is None else acc + term
        acc = acc.astype(BF)
        if c == 0:
            query[...] = acc
        else:
            for k in range(N):
                out[k, TOK * (c - 1) : TOK * c] = acc


def attend_kernel(query, got, out, scores):
    q = query[...]
    peak = None
    for k in range(N):
        s = (
            lax.dot_general(
                q, got[k, 0:TOK], (((1,), (1,)), ((), ())), preferred_element_type=F32
            )
            * SCALE
        )
        scores[:, TOK * k : TOK * k + TOK] = s
        peak = s if peak is None else jnp.maximum(peak, s)
    peak = jnp.max(peak, axis=1, keepdims=True)
    total, acc = None, None
    for k in range(N):
        e = jnp.exp(scores[:, TOK * k : TOK * k + TOK] - peak)
        total = e if total is None else total + e
        term = jnp.dot(e.astype(BF), got[k, TOK : 2 * TOK], preferred_element_type=F32)
        acc = term if acc is None else acc + term
    context = (acc / jnp.sum(total, axis=1, keepdims=True)).astype(BF)
    for v in range(N):
        out[v] = context


def output_kernel(got, weight, out):
    halves = columns_of(got, weight)
    for i in range(2):
        out[:, 128 * i : 128 * i + 128] = halves[i].astype(BF)


def shape(dims, kind):
    return jax.ShapeDtypeStruct(dims, kind)


def exchange(x, axis):
    return lax.all_to_all(x, axis, 0, 0, tiled=True)


def shards(
    patches,
    slot_variable,
    embed_weight,
    variable_embed,
    norm_gain,
    pool_keys,
    pool_value,
    pool_out,
    block_gain,
    attend_weight,
    out_proj,
):
    v_idx, k_idx = lax.axis_index("var"), lax.axis_index("tok")
    place = jnp.stack([k_idx, k_idx // 2]).astype(jnp.int32)

    rows_of_k = pl.BlockSpec((16, D), lambda i, place: (place[1], 0))
    parts = pl.pallas_call(
        weights_kernel,
        out_shape=shape((N, W_ROWS, 128), BF),
        grid_spec=pltpu.PrefetchScalarGridSpec(
            num_scalar_prefetch=1,
            grid=(1,),
            in_specs=[pl.BlockSpec((COLS, E), lambda i, place: (0, 0)), rows_of_k, rows_of_k],
            out_specs=pl.BlockSpec((N, W_ROWS, 128), lambda i, place: (0, 0, 0)),
        ),
        cost_estimate=pl.CostEstimate(flops=0, bytes_accessed=800_000, transcendentals=0),
    )(place, pool_value, pool_out, out_proj)
    parts = exchange(parts, "var")
    common, var_rows = call(
        embed_kernel,
        (shape((ROWS - R_P, TOK), BF), shape((8, D), F32)),
        6,
        (pltpu.VMEM((TOK, 128), F32),),
        smem=(0,),
        flops=2 * SLOTS * TOK * D * 48,
        size=4_000_000,
    )(
        slot_variable,
        patches,
        embed_weight,
        variable_embed,
        norm_gain[None],
        pool_keys.T,
    )
    packed = call(pack_kernel, shape((Z, ROWS, 128), BF), 4, unread=(3,), size=3_000_000)(
        embed_weight, common, var_rows, parts
    )
    parts = lax.all_gather(parts, "tok", axis=0)
    rings = [list(range(Z)), list(range(Z, N))]
    got = lax.all_to_all(packed, "var", 0, 0, tiled=True, axis_index_groups=rings)
    gain = lax.dynamic_index_in_dim(norm_gain.reshape(N, Z, 32), v_idx % Z, 1, keepdims=False)

    summed, tails = call(
        pool_kernel,
        (shape((4, N * TOK, 128), F32), shape((2, N, TOK), F32)),
        2,
        (
            pltpu.VMEM((96 * Z, TOK), F32),
            pltpu.VMEM((2, TOK * 32, TOK), F32),
            pltpu.VMEM((4, TOK * HALF, 128), F32),
        ),
        vmem=36,
        flops=2 * 400_000_000,
        size=5_000_000,
    )(got, gain.reshape(1, WIDE))
    partial = call(
        values_kernel,
        shape((N, TOK + 8, E), F32),
        3,
        blocks={2: ((N, N, 32, E), lambda i: (0, 0, 0, 0))},
        flops=4 * TOK * WIDE * 2048,
        size=7_000_000,
    )(summed, tails, parts)
    pooled = call(pooled_kernel, shape((N, TOK, E), BF), 1, size=1_500_000)(
        exchange(partial, "var")
    )
    state, aggregated, stats = call(
        state_kernel,
        (shape((TOK, COLS), F32), shape((TOK, COLS), BF), shape((N, 8, 128), F32)),
        2,
        (pltpu.VMEM((TOK, 128), F32),),
        blocks={1: ((N, N, 16, 128), lambda i: (0, 0, W_P // 16, 0))},
        flops=2 * TOK * 2048 * COLS,
        size=2_000_000,
    )(exchange(pooled, "var"), parts)
    normed = call(norm_kernel, shape((N, TOK, COLS), BF), 3, size=1_200_000)(
        exchange(stats, "var"),
        state,
        lax.dynamic_slice(block_gain, (COLS * v_idx,), (COLS,))[None],
    )
    query, kv = call(
        project_kernel,
        (shape((TOK, E), BF), shape((N, 2 * TOK, E), BF)),
        2,
        flops=2 * TOK * D * 384,
        size=5_000_000,
    )(exchange(normed, "var"), attend_weight)
    context = call(
        attend_kernel,
        shape((N, TOK, E), BF),
        2,
        (pltpu.VMEM((TOK, N * TOK), F32),),
        flops=4 * TOK * 2048 * E,
        size=1_500_000,
    )(query, exchange(kv, "tok"))
    attended = call(
        output_kernel,
        shape((TOK, COLS), BF),
        2,
        blocks={1: ((N, N, 16, 128), lambda i: (0, 0, W_O // 16, 0))},
        flops=2 * TOK * 2048 * COLS,
        size=2_000_000,
    )(exchange(context, "var"), parts)
    return (aggregated, attended)


def solution(mesh):
    return jax.shard_map(
        shards,
        mesh=mesh,
        in_specs=(
            P("var", None, "tok"),
            P("var"),
            P("var", None, None),
            P(),
            P(),
            P(),
            P("tok", "var"),
            P("var", None),
            P(),
            P(None, None, "var"),
            P("var", None),
        ),
        out_specs=(P("tok", "var"), P("tok", "var")),
        check_vma=False,
    )
```

time: 354 us -> 258 us (0.73)
  waiting for transfers between devices: 208 us -> 44.6 us
  blocking collectives: 30.2 us -> 145 us
  starting transfers between devices: 44.8 us -> 8.75 us
  local copies, waits for them, and re-layouts: 13.1 us -> 7.39 us
  Pallas kernels: 40.4 us -> 36.6 us
    all_to_all x1 -> x6, blocking collectives: 30.2 us -> 145 us  [exchange(): return lax.all_to_all(x, axis, 0, 0, tiled=True)]
    all_gather x3 -> x1, waiting for transfers between devices: 107 us -> 0.01 us  [shards(): parts = lax.all_gather(parts, 'tok', axis=0)]
    ppermute x1 -> x0, waiting for transfers between devices: 51.7 us -> none  [shards(): value = lax.ppermute(pool_value, ('var', 'tok'), swap)]
    all_to_all x6 -> x1, waiting for transfers between devices: 49.4 us -> 6.07 us  [exchange(): return lax.all_to_all(x, axis, 0, 0, tiled=True)]
    all_to_all x0 -> x1, waiting for transfers between devices: none -> 38.5 us  [shards(): lax.all_to_all(packed, 'var', 0, 0, tiled=True, axis_index_groups=rings)]
    all_to_all x6 -> x1, starting transfers between devices: 40.9 us -> 4.94 us  [exchange(): return lax.all_to_all(x, axis, 0, 0, tiled=True)]
    ppermute x1 -> x0, starting transfers between devices: 3.79 us -> none  [shards(): value = lax.ppermute(pool_value, ('var', 'tok'), swap)]
    all_to_all x0 -> x1, starting transfers between devices: none -> 3.78 us  [shards(): lax.all_to_all(packed, 'var', 0, 0, tiled=True, axis_index_groups=rings)]
  transfers between devices with their start and end apart: 10 -> 3, of which waited for: 7 -> 2; matrix products, arithmetic and copies ran while one was open for 0% -> 0% of each run, Pallas kernels for 1% -> 11%
where the time goes in v2:
time: 258 us; the launch traced here: 257 us
  blocking collectives  145 us (56%)
  waiting for transfers between devices  44.6 us (17%)
  Pallas kernels  36.6 us (14%)
  between operations  14.2 us (6%)
  starting transfers between devices  8.75 us (3%)
  local copies, waits for them, and re-layouts  7.39 us (3%)
    all_to_all x6, blocking collectives, exchange(): return lax.all_to_all(x, axis, 0, 0, tiled=True)  145 us
    all_to_all x1, waiting for transfers between devices, shards(): lax.all_to_all(packed, 'var', 0, 0, tiled=True, axis_index_groups=rings)  38.5 us
    pallas_call x1, Pallas kernels, shards(): call(pool_kernel, (shape((4, N * TOK, 128), F32), shape((2, N, TOK), F32)...  18.5 us
    pallas_call x1, Pallas kernels, shards(): call(embed_kernel, (shape((ROWS - R_P, TOK), BF), shape((8, D), F32)), 6,...  7.02 us
    unnamed x26, local copies, waits for them, and re-layouts  6.41 us
    all_to_all x1, waiting for transfers between devices, exchange(): return lax.all_to_all(x, axis, 0, 0, tiled=True)  6.07 us
  transfers between devices with their start and end apart: 3, of which 2 were waited for; matrix products, arithmetic and copies ran while one was open for 0% of the time, Pallas kernels for 11%

profile of v2, /device:TPU:34, one launch (start us, length us, event | category | flops | bytes accessed | tf_op | source)
XLA Modules:
  0.0 257.2 jit_solution(9978851878101035615)
XLA Ops:
  7.2 0.0 all-gather.3.cloned.1.call-start
  7.2 0.7 pad_add_fusion.place
  7.9 0.0 copy-start.10
  7.9 0.0 copy-start.11
  7.9 2.5 shard_map.123
  10.5 19.5 %all_to_all.40.early = bf16[16,64,128]{2,1,0:T(8,128)(2,1)} all-to-all(bf16[16,64,128]{2,1,0:T(8,128)(2,1)} %shard_map.123), channel_id=1, replica_groups=mesh['var'=16,'tok'=16] {'var'}, dimensions={0} | all-to-all | bytes 524288 | tf_op jit(solution)/shard_map/all_to_all | solution.py:360
  30.0 0.0 all-gather.3.cloned.1.call-update
  30.1 7.0 %shard_map.122 = (bf16[400,128]{1,0:T(8,128)(2,1)S(1)}, f32[8,4096]{1,0:T(8,128)S(1)}) custom-call(s32[6]{0:T(128)S(1)} %copy-done.11, bf16[6,16,128]{2,1,0:T(8,128)(2,1)S(1)} %copy-done.10, bf16[6,16,4096]{2,1,0:T(8,128)(2,1)S(1)} %copy-done.6, bf16[91,4096]{1,0:T(8,128)(2,1)S(1)} %copy-done.8, bf16[1,4096]{1,0:T(2,128)(2,1)S(1)} %broadcast_in_dim.6.gain, ...), custom_call_target="tpu_custom_call" | custom-call | flops 301989888 | bytes 4000000 | tf_op jit(solution)/shard_map/pallas_call | solution.py:392
  37.1 2.0 shard_map.124
  39.1 3.8 %all-to-all-start.1 = ((bf16[8,784,128]{2,1,0:T(8,128)(2,1)}), bf16[8,784,128]{2,1,0:T(8,128)(2,1)S(1)}, u32[]{:S(2)}, u32[]{:S(2)}) async-start(bf16[8,784,128]{2,1,0:T(8,128)(2,1)} %shard_map.124), calls=%async_computation.1 | async-start | bytes 3211264 | tf_op jit(solution)/shard_map/all_to_all | solution.py:413
  42.9 0.1 reshape.11
  43.0 0.1 reshape.12.gain
  43.1 38.5 %all-to-all-done.1.got = bf16[8,784,128]{2,1,0:T(8,128)(2,1)S(1)} async-done(((bf16[8,784,128]{2,1,0:T(8,128)(2,1)}), bf16[8,784,128]{2,1,0:T(8,128)(2,1)S(1)}, u32[]{:S(2)}, u32[]{:S(2)}) %all-to-all-start.1) | async-done | bytes 1605664 | tf_op jit(solution)/shard_map/all_to_all | solution.py:413
  81.6 18.5 %shard_map.125 = (f32[4,2048,128]{2,1,0:T(8,128)S(1)}, f32[2,16,128]{2,1,0:T(8,128)S(1)}) custom-call(bf16[8,784,128]{2,1,0:T(8,128)(2,1)S(1)} %all-to-all-done.1.got, bf16[1,512]{1,0:T(2,128)(2,1)S(1)} %reshape.12.gain), custom_call_target="tpu_custom_call" | custom-call | flops 800000000 | bytes 5000000 | tf_op jit(solution)/shard_map/pallas_call | solution.py:416
  100.1 2.0 copy-done.3
  102.1 2.2 copy-done
  104.3 2.2 copy-done.4
  106.5 1.3 shard_map.126
  107.8 33.4 %all_to_all.41.got = f32[16,136,128]{2,1,0:T(8,128)S(1)} all-to-all(f32[16,136,128]{2,1,0:T(8,128)S(1)} %shard_map.126), channel_id=1, replica_groups=mesh['var'=16,'tok'=16] {'var'}, dimensions={0} | all-to-all | bytes 2228224 | tf_op jit(solution)/shard_map/all_to_all | solution.py:360
  141.2 0.2 shard_map.127
  141.5 19.4 %all_to_all.42.got = bf16[16,128,128]{2,1,0:T(8,128)(2,1)S(1)} all-to-all(bf16[16,128,128]{2,1,0:T(8,128)(2,1)S(1)} %shard_map.127), channel_id=1, replica_groups=mesh['var'=16,'tok'=16] {'var'}, dimensions={0} | all-to-all | bytes 1048576 | tf_op jit(solution)/shard_map/all_to_all | solution.py:360
  160.9 1.4 shard_map.128
  162.3 4.9 %all-to-all-start.4 = ((f32[16,8,128]{2,1,0:T(8,128)}), f32[16,8,128]{2,1,0:T(8,128)S(1)}, u32[]{:S(2)}, u32[]{:S(2)}) async-start(f32[16,8,128]{2,1,0:T(8,128)} %get-tuple-element.16), calls=%async_computation.4 | async-start | bytes 131072 | tf_op jit(solution)/shard_map/all_to_all | solution.py:360
  167.2 0.8 dynamic_slice.8
  168.0 6.1 %all-to-all-done.4.got = f32[16,8,128]{2,1,0:T(8,128)S(1)} async-done(((f32[16,8,128]{2,1,0:T(8,128)}), f32[16,8,128]{2,1,0:T(8,128)S(1)}, u32[]{:S(2)}, u32[]{:S(2)}) %all-to-all-start.4) | async-done | bytes 65568 | tf_op jit(solution)/shard_map/all_to_all | solution.py:360
  174.0 0.3 shard_map.129
  174.3 28.9 %all_to_all.43.got = bf16[16,128,256]{2,1,0:T(8,128)(2,1)S(1)} all-to-all(bf16[16,128,256]{2,1,0:T(8,128)(2,1)S(1)} %shard_map.129), channel_id=1, replica_groups=mesh['var'=16,'tok'=16] {'var'}, dimensions={0} | all-to-all | bytes 2097152 | tf_op jit(solution)/shard_map/all_to_all | solution.py:360
  203.2 1.0 shard_map.130
  204.2 24.2 %all_to_all.44.got = bf16[16,256,128]{2,1,0:T(8,128)(2,1)S(1)} all-to-all(bf16[16,256,128]{2,1,0:T(8,128)(2,1)S(1)} %get-tuple-element.19), channel_id=1, replica_groups=mesh['var'=16,'tok'=16] {'tok'}, dimensions={0} | all-to-all | bytes 2097152 | tf_op jit(solution)/shard_map/all_to_all | solution.py:360
  228.4 1.2 shard_map.131
  229.6 19.6 %all_to_all.45.got = bf16[16,128,128]{2,1,0:T(8,128)(2,1)S(1)} all-to-all(bf16[16,128,128]{2,1,0:T(8,128)(2,1)S(1)} %shard_map.131), channel_id=1, replica_groups=mesh['var'=16,'tok'=16] {'var'}, dimensions={0} | all-to-all | bytes 1048576 | tf_op jit(solution)/shard_map/all_to_all | solution.py:360
  249.2 1.2 shard_map.132
  (25 shorter events, 0.1 us)
Async XLA Ops:
  7.2 94.9 %all-gather.3.cloned.1.call-start = ((), (), s32[]{:S(2)}) async-start(), calls=%async_computation.8 | async-start | bytes 4456448 | tf_op jit(solution)/shard_map/all_gather | solution.py:411
  7.9 22.1 %copy-start.12 = (bf16[4096]{0:T(1024)(128)(2,1)S(1)}, bf16[4096]{0:T(1024)(128)(2,1)}, u32[]{:S(2)}) copy-start(bf16[4096]{0:T(1024)(128)(2,1)} %param.15) | copy-start | bytes 24580
  7.9 22.2 %copy-start.6 = (bf16[6,16,4096]{2,1,0:T(8,128)(2,1)S(1)}, bf16[6,16,4096]{2,1,0:T(8,128)(2,1)}, u32[]{:S(2)}) copy-start(bf16[6,16,4096]{2,1,0:T(8,128)(2,1)} %weight.4) | copy-start | bytes 2359300
  7.9 22.2 %copy-start.8 = (bf16[91,4096]{1,0:T(8,128)(2,1)S(1)}, bf16[91,4096]{1,0:T(8,128)(2,1)}, u32[]{:S(2)}) copy-start(bf16[91,4096]{1,0:T(8,128)(2,1)} %table.1) | copy-start | bytes 2236420
  7.9 22.2 %copy-start.9 = (bf16[4096,16]{0,1:T(8,128)(2,1)S(1)}, bf16[4096,16]{0,1:T(8,128)(2,1)}, u32[]{:S(2)}) copy-start(bf16[4096,16]{0,1:T(8,128)(2,1)} %param.16) | copy-start | bytes 393220
  7.9 22.2 %copy-start.10 = (bf16[6,16,128]{2,1,0:T(8,128)(2,1)S(1)}, bf16[6,16,128]{2,1,0:T(8,128)(2,1)}, u32[]{:S(2)}) copy-start(bf16[6,16,128]{2,1,0:T(8,128)(2,1)} %patches.1) | copy-start | bytes 73732
  7.9 22.2 %copy-start.11 = (s32[6]{0:T(128)S(1)}, s32[6]{0:T(128)}, u32[]{:S(2)}) copy-start(s32[6]{0:T(128)} %slot.1) | copy-start | bytes 76
  30.0 7.1 %copy-start.7 = (bf16[16,64,128]{2,1,0:T(8,128)(2,1)S(1)}, bf16[16,64,128]{2,1,0:T(8,128)(2,1)}, u32[]{:S(2)}) copy-start(bf16[16,64,128]{2,1,0:T(8,128)(2,1)} %all_to_all.40.early) | copy-start | bytes 786436
  39.1 42.5 %all-to-all-start.1 = ((bf16[8,784,128]{2,1,0:T(8,128)(2,1)}), bf16[8,784,128]{2,1,0:T(8,128)(2,1)S(1)}, u32[]{:S(2)}, u32[]{:S(2)}) async-start(bf16[8,784,128]{2,1,0:T(8,128)(2,1)} %shard_map.124), calls=%async_computation.1 | async-start | bytes 3211264 | tf_op jit(solution)/shard_map/all_to_all | solution.py:413
  100.1 2.0 copy-start.3
  102.1 2.2 copy-start
  104.3 2.2 copy-start.4
  107.8 53.1 %copy-start.1 = (bf16[256,64,128]{2,1,0:T(8,128)(2,1)S(1)}, bf16[256,64,128]{2,1,0:T(8,128)(2,1)}, u32[]{:S(2)}) copy-start(bf16[256,64,128]{2,1,0:T(8,128)(2,1)} %all-gather.3.cloned.1.call-done) | copy-start | bytes 12582916
  162.3 11.8 %all-to-all-start.4 = ((f32[16,8,128]{2,1,0:T(8,128)}), f32[16,8,128]{2,1,0:T(8,128)S(1)}, u32[]{:S(2)}, u32[]{:S(2)}) async-start(f32[16,8,128]{2,1,0:T(8,128)} %get-tuple-element.16), calls=%async_computation.4 | async-start | bytes 131072 | tf_op jit(solution)/shard_map/all_to_all | solution.py:360
  174.0 29.2 %copy-start.5 = (bf16[3,4096,128]{2,1,0:T(8,128)(2,1)S(1)}, bf16[3,4096,128]{2,1,0:T(8,128)(2,1)}, u32[]{:S(2)}) copy-start(bf16[3,4096,128]{2,1,0:T(8,128)(2,1)} %weight.5) | copy-start | bytes 9437188
  204.2 45.0 %copy-start.2 = (bf16[256,64,128]{2,1,0:T(8,128)(2,1)S(1)}, bf16[256,64,128]{2,1,0:T(8,128)(2,1)}, u32[]{:S(2)}) copy-start(bf16[256,64,128]{2,1,0:T(8,128)(2,1)} %all-gather.3.cloned.1.call-done) | copy-start | bytes 12582916
Sparse Core Ops, SparseCore 0:
  30.1 57.4 all-gather.2

commit v3 on v1

v3 whole, which is shorter than its diff:
```python
import functools
import math

import jax
import jax.numpy as jnp
from jax import lax
from jax.experimental import pallas as pl
from jax.experimental.pallas import tpu as pltpu
from jax.sharding import PartitionSpec as P

F32 = jnp.float32
BF = jnp.bfloat16
N = 16
SLOTS = 6
TOK = 128
COLS = 256
D = 4096
E = 128
SCALE = 1.0 / math.sqrt(128)

Z = 8
WIDE = 512
PART = 64
PAIRS = 48
ROW_STEP, LEFT_STEP, SUM_STEP = 100, 36, 65


R_U, R_P, R_WH, R_WL, R_M, R_ST, ROWS = 0, 192, 240, 288, 336, 368, 416
W_V, W_P, W_O, W_ROWS = 0, 32, 64, 80


def split2(x):
    hi = x.astype(BF)
    return hi, (x - hi.astype(F32)).astype(BF)


def split3(x):
    hi = x.astype(BF)
    rest = x - hi.astype(F32)
    mid = rest.astype(BF)
    return hi, mid, (rest - mid.astype(F32)).astype(BF)


def call(kernel, out_shape, n_in, scratch=(), smem=(), hbm=(), vmem=16, flops=0, size=0):
    spaces = {i: pltpu.SMEM for i in smem} | {i: pltpu.HBM for i in hbm}
    vm = pl.BlockSpec(memory_space=pltpu.VMEM)
    many = isinstance(out_shape, (tuple, list))
    return pl.pallas_call(
        kernel,
        out_shape=out_shape,
        in_specs=[pl.BlockSpec(memory_space=spaces.get(i, pltpu.VMEM)) for i in range(n_in)],
        out_specs=[vm] * len(out_shape) if many else vm,
        scratch_shapes=list(scratch),
        compiler_params=pltpu.CompilerParams(vmem_limit_bytes=vmem * 1024 * 1024),
        cost_estimate=pl.CostEstimate(flops=flops, bytes_accessed=size, transcendentals=0),
    )


def fetch(parts, row, into, sem):
    copy = pltpu.make_async_copy(parts.at[:, N * row : N * row + into.shape[1]], into, sem)
    copy.start()
    copy.wait()


def weights_kernel(place, value, pool_rows, proj_rows, out):
    half = place[1]
    for v in range(N):
        z = v % Z
        out[v, W_V : W_V + 32] = value[32 * z : 32 * z + 32]
        for x in range(2):
            at = pl.ds(pl.multiple_of(COLS * (Z * x + z) + 128 * half, 128), 128)
            out[v, W_P + 16 * x : W_P + 16 * x + 16] = pool_rows[:, at]
        at = pl.ds(pl.multiple_of(COLS * v + 128 * half, 128), 128)
        out[v, W_O : W_O + 16] = proj_rows[:, at]


def chunks(x, z, j):
    at = [256 * k + 32 * z for k in range(4 * j, 4 * j + 4)]
    return jnp.concatenate([x[:, a : a + 32] for a in at], 1)


def embed_kernel(slot, place, patches, weight, table, gain, keys, out, columns, common):
    wide = table.shape[0]
    row = lax.broadcasted_iota(jnp.int32, (8, wide), 0)
    col = lax.broadcasted_iota(jnp.int32, (8, wide), 1)
    pick = jnp.zeros((8, wide), F32)
    for s in range(SLOTS):
        pick = jnp.where((row == s) & (col == slot[s]), 1.0, pick)
    var_rows = jnp.dot(pick.astype(BF), table[...], preferred_element_type=F32)
    gain_row = gain[...].astype(F32)
    columns[...] = jnp.zeros_like(columns)
    scores = []
    for s in range(SLOTS):
        emb = lax.dot_general(
            patches[s], weight[s], (((0,), (0,)), ((), ())), preferred_element_type=F32
        )
        emb = emb + var_rows[s : s + 1]
        mean = jnp.sum(emb, axis=1, keepdims=True) * (1.0 / D)
        emb = emb - mean
        spread = jnp.sum(emb * emb, axis=1, keepdims=True) * (1.0 / D)
        rstd = lax.rsqrt(spread + 1e-05)
        normed = (emb * rstd * gain_row).astype(BF)
        score = lax.dot_general(
            keys[...], normed, (((1,), (1,)), ((), ())), preferred_element_type=F32
        )
        scores.append(jnp.where(slot[s] >= 0, score * SCALE, -1e30))
        columns[:, s : s + 1] = mean
        columns[:, 6 + s : 7 + s] = rstd
    turned = jnp.transpose(columns[...])
    top = scores[0]
    for s in range(1, SLOTS):
        top = jnp.maximum(top, scores[s])
    weights = [jnp.where(slot[s] >= 0, jnp.exp(scores[s] - top), 0.0) for s in range(SLOTS)]

    def beside(low, high, x):
        at = slice(PART * x, PART * x + PART)
        return jnp.concatenate([low[:, at], high[:, at]], 1)

    tops = [t.astype(F32) for t in split3(top)] + [jnp.zeros((N, TOK), F32)]
    for x in range(2):
        for i in range(3):
            a = 16 * i
            low, high = patches[i].astype(F32), patches[i + 3].astype(F32)
            common[x, a : a + 16] = beside(low, high, x).astype(BF)
            hi, lo = split2(beside(weights[i], weights[i + 3], x))
            common[x, R_WH - R_P + a : R_WH - R_P + a + 16] = hi
            common[x, R_WL - R_P + a : R_WL - R_P + a + 16] = lo
        for i in range(2):
            a = R_M - R_P + 16 * i
            common[x, a : a + 16] = beside(tops[2 * i], tops[2 * i + 1], x).astype(BF)
        stats = []
        for first in (0, 6):
            both = beside(turned[first : first + 3], turned[first + 3 : first + 6], x)
            stats.extend(part.astype(F32) for part in split3(both))
        for z in range(Z):
            out[Z * x + z, R_P:R_ST] = common[x]
            rows = stats + [chunks(var_rows, z, j)[:6] for j in range(4)]
            rows.append(jnp.zeros((6, TOK), F32))
            out[Z * x + z, R_ST:] = jnp.concatenate(rows, 0).astype(BF)
    for i in range(3):
        wide = weight[3 * place[1] + i].astype(F32)
        for z in range(Z):
            for j in range(4):
                a = R_U + 48 * j + 16 * i
                part = chunks(wide, z, j).astype(BF)
                for x in range(2):
                    out[Z * x + z, a : a + 16] = part


def hand_on_kernel(parts, early, out):
    for first, last in ((W_V, W_P), (W_P, W_O), (W_O, W_ROWS)):
        size = last - first
        for h in range(N):
            a = N * first + size * h
            out[a : a + size] = parts[h, first:last]


def pool_kernel(place, got, swapped, gain, summed, weights, turned, rows):
    tops = []
    for v in range(N):
        m = [got[v, R_M + 16 * i : R_M + 16 * i + 16].astype(F32) for i in range(2)]
        tops.append((m[0][:, :PART] + m[0][:, PART:]) + m[1][:, :PART])
    top = tops[0]
    for v in range(1, N):
        top = jnp.maximum(top, tops[v])
    total = jnp.zeros((N, TOK), F32)
    for v in range(N):
        factor = jnp.exp(tops[v] - top)
        factor = jnp.concatenate([factor, factor], 1)
        for i in range(3):
            a = 16 * i
            w = got[v, R_WH + a : R_WH + a + 16].astype(F32) + got[
                v, R_WL + a : R_WL + a + 16
            ].astype(F32)
            w = w * factor
            total = total + w
            weights[48 * v + a : 48 * v + a + 16] = w
    inverse = 1.0 / (total[:, :PART] + total[:, PART:])
    inverse = jnp.concatenate([inverse, inverse], 1)
    odd = lax.broadcasted_iota(jnp.int32, (PAIRS, TOK), 1) % 2 == 1
    for h in range(0, N, 2):
        w = [weights[pl.ds(h + n, PAIRS, stride=16)] * inverse[h + n : h + n + 1] for n in range(2)]
        low = jnp.concatenate([x[:, :PART] for x in w], 1)
        high = jnp.concatenate([x[:, PART:] for x in w], 1)
        gap = jnp.zeros((ROW_STEP - 2 * PAIRS, TOK), F32)
        parts = [jnp.where(odd, 0.0, low), jnp.where(odd, 0.0, high), gap]
        parts += [jnp.where(odd, low, 0.0), jnp.where(odd, high, 0.0)]
        parts.append(jnp.zeros((256 - ROW_STEP - 2 * PAIRS, TOK), F32))
        w = jnp.concatenate(parts, 0)
        for j in range(2):
            part = jnp.transpose(w[128 * j : 128 * j + 128])
            hi = part.astype(BF).astype(F32)
            lo = (part - hi).astype(BF).astype(F32)
            for n in range(2):
                at = slice(PART * n, PART * n + PART)
                turned[j, pl.ds(h + n, PART, stride=LEFT_STEP)] = hi[at]
                turned[j, pl.ds(16 + h + n, PART, stride=LEFT_STEP)] = lo[at]
    gain_row = gain[...].astype(F32)
    even_core = place[1] == 0

    def source(v, carry):
        st = got[v, R_ST:ROWS].astype(F32)
        mean = (st[0:3] + st[3:6]) + st[6:9]
        rstd = (st[9:12] + st[12:15]) + st[15:18]
        both = jnp.transpose(jnp.concatenate([mean, rstd, jnp.zeros((122, TOK), F32)], 0))
        for i in range(3):
            p = got[v, R_P + 16 * i : R_P + 16 * i + 16]
            us = []
            for ref in (got, swapped):
                at = [48 * j + 16 * i for j in range(4)]
                us.append(jnp.concatenate([ref[v, a : a + 16] for a in at], 1))
            sides = (jnp.where(even_core, us[0], us[1]), jnp.where(even_core, us[1], us[0]))
            for n in range(2):
                at = slice(PART * n, PART * n + PART)
                emb = lax.dot_general(
                    p[:, at], sides[n], (((0,), (0,)), ((), ())), preferred_element_type=F32
                )
                col_mean, col_rstd = both[at, i : i + 1], both[at, 3 + i : 4 + i]
                for j in range(4):
                    a = 18 + 6 * j + 3 * n + i
                    x = emb[:, 128 * j : 128 * j + 128] + st[a : a + 1]
                    x = (x - col_mean) * col_rstd * gain_row[:, 128 * j : 128 * j + 128]
                    rows[j, pl.ds(PAIRS * n + 3 * v + i, PART, stride=ROW_STEP)] = x
        return carry

    for j in range(4):
        for i in range(2 * PAIRS, ROW_STEP):
            rows[j, pl.ds(i, PART, stride=ROW_STEP)] = jnp.zeros((PART, 128), F32)
    lax.fori_loop(0, N, source, 0, unroll=4)

    for j in range(2):
        for i in range(32, LEFT_STEP):
            turned[j, pl.ds(i, PART, stride=LEFT_STEP)] = jnp.zeros((PART, 128), F32)

    def two_tokens(g, carry):
        at = pl.ds(pl.multiple_of(g * 2 * LEFT_STEP, 8), 2 * LEFT_STEP)
        lhs = jnp.concatenate([turned[0, at], turned[1, at][:, : 2 * ROW_STEP - 128]], 1)
        span = pl.ds(pl.multiple_of(g * 2 * ROW_STEP, 8), 2 * ROW_STEP)
        rhs = jnp.concatenate([rows[j, span] for j in range(4)], 1)
        y = jnp.dot(lhs.astype(BF), rhs.astype(BF), preferred_element_type=F32)
        for q in range(2):
            a = LEFT_STEP * q
            part = y[a : a + 16] + y[a + 16 : a + 32]
            for j in range(4):
                summed[j, pl.ds(2 * g + q, 16, stride=SUM_STEP)] = part[
                    :, 128 * j : 128 * j + 128
                ]
        return carry

    lax.fori_loop(0, PART // 2, two_tokens, 0, unroll=4)


def values_kernel(summed, parts, out, value, sem):
    fetch(parts, W_V, value, sem)
    for h in range(N):
        at = slice(SUM_STEP * h, SUM_STEP * h + PART)
        hi, lo = split2(jnp.concatenate([summed[j, at] for j in range(4)], 1))
        right = jnp.concatenate([value[k, 32 * h : 32 * h + 32] for k in range(N)], 0)
        whole = jnp.dot(jnp.concatenate([hi, lo], 0), right, preferred_element_type=F32)
        out[h // 2, PART * (h % 2) : PART * (h % 2) + PART] = whole[:PART] + whole[PART:]


def pooled_kernel(got, out):
    total = got[0]
    for z in range(1, Z):
        total = total + got[z]
    total = total.astype(BF)
    for z in range(Z):
        out[z] = total


def columns_of(blocks, weight):
    halves = []
    for half in range(2):
        acc = None
        for h in range(0, N, 2):
            left = jnp.concatenate([blocks[h], blocks[h + 1]], 1)
            right = jnp.concatenate(
                [
                    weight[2 * j + half, a : a + 16]
                    for a in (16 * h, 16 * h + 16)
                    for j in range(8)
                ],
                0,
            )
            term = jnp.dot(left, right, preferred_element_type=F32)
            acc = term if acc is None else acc + term
        halves.append(acc)
    return halves


def state_kernel(got, parts, state, stats, columns, weight, sem):
    fetch(parts, W_P, weight, sem)
    lefts = [jnp.concatenate([got[z, 0:PART], got[z, PART : 2 * PART]], 1) for z in range(Z)]
    total = None
    for c in range(4):
        acc = None
        for z in range(Z):
            right = jnp.concatenate(
                [
                    weight[2 * j + c % 2, a : a + 16]
                    for a in (64 * z + 16 * (c // 2), 64 * z + 32 + 16 * (c // 2))
                    for j in range(8)
                ],
                0,
            )
            term = jnp.dot(lefts[z], right, preferred_element_type=F32)
            acc = term if acc is None else acc + term
        state[:, 128 * c : 128 * c + 128] = acc
        total = acc if total is None else total + acc
    mean = jnp.sum(total, axis=1, keepdims=True) * (1.0 / WIDE)
    spread = jnp.zeros((PART, 128), F32)
    for c in range(4):
        gap = state[:, 128 * c : 128 * c + 128] - mean
        spread = spread + gap * gap
    columns[...] = jnp.zeros_like(columns)
    columns[0:PART, 0:1] = mean
    columns[0:PART, 1:2] = jnp.sum(spread, axis=1, keepdims=True)
    turned = jnp.transpose(columns[...])[0:8]
    for z in range(Z):
        stats[z] = turned


def norm_kernel(got, state, gain, out):
    mean = got[0, 0:1]
    for z in range(1, Z):
        mean = mean + got[z, 0:1]
    mean = mean * (1.0 / Z)
    spread = jnp.zeros((1, TOK), F32)
    for z in range(Z):
        gap = got[z, 0:1] - mean
        spread = spread + (got[z, 1:2] + WIDE * gap * gap)
    rstd = lax.rsqrt(spread * (1.0 / D) + 1e-05)
    both = jnp.transpose(jnp.concatenate([mean, rstd, jnp.zeros((126, TOK), F32)], 0))
    both = both[0:PART]
    normed = ((state[...] - both[:, 0:1]) * both[:, 1:2] * gain[...].astype(F32)).astype(BF)
    for z in range(Z):
        out[z] = normed


def project_kernel(place, own, other, weight, state, query, out, keep, send, whole):
    halves = [
        pl.ds(pl.multiple_of(PART * p, PART), PART) for p in (place[2], 1 - place[2])
    ]
    first = place[2] == 0
    low, high = state[:, 0:COLS].astype(BF), state[:, COLS:].astype(BF)
    keep[...] = jnp.where(first, low, high)
    send[...] = jnp.where(first, high, low)
    for c in range(3):
        acc = None
        for z in range(Z):
            left = jnp.concatenate([own[z], other[z]], 0)
            for x in range(2):
                at = COLS * (Z * x + z)
                term = jnp.dot(
                    left[:, COLS * x : COLS * x + COLS],
                    weight[c, at : at + COLS],
                    preferred_element_type=F32,
                )
                acc = term if acc is None else acc + term
        for i in range(2):
            whole[halves[i]] = acc[PART * i : PART * i + PART]
        result = whole[...].astype(BF)
        if c == 0:
            query[...] = result
        else:
            for k in range(Z):
                out[k, TOK * (c - 1) : TOK * c] = result


def attend_kernel(query, own, other, out, scores):
    q = query[...]
    blocks = [(ref, k) for ref in (own, other) for k in range(Z)]
    peak = None
    for i, (ref, k) in enumerate(blocks):
        s = (
            lax.dot_general(
                q, ref[k, 0:TOK], (((1,), (1,)), ((), ())), preferred_element_type=F32
            )
            * SCALE
        )
        scores[:, TOK * i : TOK * i + TOK] = s
        peak = s if peak is None else jnp.maximum(peak, s)
    peak = jnp.max(peak, axis=1, keepdims=True)
    total, acc = None, None
    for i, (ref, k) in enumerate(blocks):
        e = jnp.exp(scores[:, TOK * i : TOK * i + TOK] - peak)
        total = e if total is None else total + e
        term = jnp.dot(e.astype(BF), ref[k, TOK : 2 * TOK], preferred_element_type=F32)
        acc = term if acc is None else acc + term
    context = (acc / jnp.sum(total, axis=1, keepdims=True)).astype(BF)
    for v in range(N):
        out[v] = context


def output_kernel(place, got, parts, own, other, out, aggregated, weight, sem):
    fetch(parts, W_O, weight, sem)
    halves = columns_of(got, weight)
    for i in range(2):
        out[:, 128 * i : 128 * i + 128] = halves[i].astype(BF)
    for p, ref in ((place[2], own), (1 - place[2], other)):
        aggregated[pl.ds(pl.multiple_of(PART * p, PART), PART)] = ref[...]


def shape(dims, kind):
    return jax.ShapeDtypeStruct(dims, kind)


RINGS = [list(range(Z)), list(range(Z, N))]
CORES = [list(range(0, N, 2)), list(range(1, N, 2))]


def exchange(x, axis, groups=None):
    return lax.all_to_all(x, axis, 0, 0, tiled=True, axis_index_groups=groups)


def swap(x, axis, bits):
    return lax.ppermute(x, axis, [(i, i ^ bits) for i in range(N)])


def shards(
    patches,
    slot_variable,
    embed_weight,
    variable_embed,
    norm_gain,
    pool_keys,
    pool_value,
    pool_out,
    block_gain,
    attend_weight,
    out_proj,
):
    v_idx, k_idx = lax.axis_index("var"), lax.axis_index("tok")
    place = jnp.stack([k_idx // 2, k_idx % 2, v_idx // Z]).astype(jnp.int32)

    rows_of_k = pl.BlockSpec((16, D), lambda i, place: (place[0], 0))
    parts = pl.pallas_call(
        weights_kernel,
        out_shape=shape((N, W_ROWS, 128), BF),
        grid_spec=pltpu.PrefetchScalarGridSpec(
            num_scalar_prefetch=1,
            grid=(1,),
            in_specs=[pl.BlockSpec((COLS, E), lambda i, place: (0, 0)), rows_of_k, rows_of_k],
            out_specs=pl.BlockSpec((N, W_ROWS, 128), lambda i, place: (0, 0, 0)),
        ),
        cost_estimate=pl.CostEstimate(flops=0, bytes_accessed=800_000, transcendentals=0),
    )(place, pool_value, pool_out, out_proj)
    parts = exchange(parts, "var")
    packed = call(
        embed_kernel,
        shape((N, ROWS, 128), BF),
        7,
        (pltpu.VMEM((TOK, 128), F32), pltpu.VMEM((2, R_ST - R_P, TOK), BF)),
        smem=(0, 1),
        flops=2 * SLOTS * TOK * D * 48,
        size=6_000_000,
    )(
        slot_variable,
        place,
        patches,
        embed_weight,
        variable_embed,
        norm_gain[None],
        pool_keys.T,
    )
    parts = call(hand_on_kernel, shape((N * W_ROWS, 128), BF), 2, hbm=(1,), size=600_000)(
        parts, packed
    )
    parts = lax.all_gather(parts, "tok", axis=0)
    got = exchange(packed, "var")
    swapped = swap(got[:, R_U:R_P], "tok", 1)
    gain = lax.dynamic_index_in_dim(norm_gain.reshape(N, Z, 32), v_idx % Z, 1, keepdims=False)

    summed = call(
        pool_kernel,
        shape((4, N * SUM_STEP, 128), F32),
        4,
        (
            pltpu.VMEM((PAIRS * N, TOK), F32),
            pltpu.VMEM((2, PART * LEFT_STEP, TOK), F32),
            pltpu.VMEM((4, PART * ROW_STEP, 128), F32),
        ),
        smem=(0,),
        vmem=26,
        flops=2 * 400_000_000,
        size=5_000_000,
    )(place, got, swapped, gain.reshape(1, WIDE))
    partial = call(
        values_kernel,
        shape((Z, TOK, E), F32),
        2,
        (pltpu.VMEM((N, 32 * N, E), BF), pltpu.SemaphoreType.DMA),
        hbm=(1,),
        vmem=60,
        flops=4 * PART * WIDE * 2048,
        size=5_000_000,
    )(summed, parts)
    pooled = call(pooled_kernel, shape((Z, TOK, E), BF), 1, size=800_000)(
        exchange(partial, "var", RINGS)
    )
    state, stats = call(
        state_kernel,
        (shape((PART, WIDE), F32), shape((Z, 8, 128), F32)),
        2,
        (
            pltpu.VMEM((TOK, 128), F32),
            pltpu.VMEM((N, 32 * N, 128), BF),
            pltpu.SemaphoreType.DMA,
        ),
        hbm=(1,),
        vmem=60,
        flops=2 * PART * 2048 * WIDE,
        size=3_000_000,
    )(exchange(pooled, "var", RINGS), parts)
    gain = lax.dynamic_index_in_dim(block_gain.reshape(2, Z, COLS), v_idx % Z, 1, keepdims=False)
    normed = call(norm_kernel, shape((Z, PART, WIDE), BF), 3, size=700_000)(
        exchange(stats, "var", RINGS), state, gain.reshape(1, WIDE)
    )
    normed = exchange(normed, "var", RINGS)
    query, kv, keep, send = call(
        project_kernel,
        (
            shape((TOK, E), BF),
            shape((Z, 2 * TOK, E), BF),
            shape((PART, COLS), BF),
            shape((PART, COLS), BF),
        ),
        5,
        (pltpu.VMEM((TOK, E), F32),),
        smem=(0,),
        flops=2 * TOK * D * 384,
        size=5_000_000,
    )(place, normed, swap(normed, "var", Z), attend_weight, state)
    kv = exchange(kv, "tok", CORES)
    context = call(
        attend_kernel,
        shape((N, TOK, E), BF),
        3,
        (pltpu.VMEM((TOK, N * TOK), F32),),
        flops=4 * TOK * 2048 * E,
        size=1_500_000,
    )(query, kv, swap(kv, "tok", 1))
    attended, aggregated = call(
        output_kernel,
        (shape((TOK, COLS), BF), shape((TOK, COLS), BF)),
        5,
        (pltpu.VMEM((N, 16 * N, 128), BF), pltpu.SemaphoreType.DMA),
        smem=(0,),
        hbm=(2,),
        vmem=60,
        flops=2 * TOK * 2048 * COLS,
        size=2_000_000,
    )(place, exchange(context, "var"), parts, keep, swap(send, "var", Z))
    return (aggregated, attended)


def solution(mesh):
    return jax.shard_map(
        shards,
        mesh=mesh,
        in_specs=(
            P("var", None, "tok"),
            P("var"),
            P("var", None, None),
            P(),
            P(),
            P(),
            P("tok", "var"),
            P("var", None),
            P(),
            P(None, None, "var"),
            P("var", None),
        ),
        out_specs=(P("tok", "var"), P("tok", "var")),
        check_vma=False,
    )
```

time: 354 us -> 240 us (0.68)
  waiting for transfers between devices: 208 us -> 54.3 us
  blocking collectives: 30.2 us -> 99.5 us
  starting transfers between devices: 44.8 us -> 27.2 us
  local copies, waits for them, and re-layouts: 13.1 us -> 6.13 us
  Pallas kernels: 40.4 us -> 36.8 us
    all_gather x3 -> x1, waiting for transfers between devices: 107 us -> 7.47 us  [shards(): parts = lax.all_gather(parts, 'tok', axis=0)]
    all_to_all x1 -> x4, blocking collectives: 30.2 us -> 99.5 us  [exchange(): return lax.all_to_all(x, axis, 0, 0, tiled=True, axis_index_groups=groups)]
    ppermute x1 -> x4, waiting for transfers between devices: 51.7 us -> 15.5 us  [swap(): return lax.ppermute(x, axis, [(i, i ^ bits) for i in range(N)])]
    all_to_all x6 -> x4, waiting for transfers between devices: 49.4 us -> 31.4 us  [exchange(): return lax.all_to_all(x, axis, 0, 0, tiled=True, axis_index_groups=groups)]
    all_to_all x6 -> x4, starting transfers between devices: 40.9 us -> 25.2 us  [exchange(): return lax.all_to_all(x, axis, 0, 0, tiled=True, axis_index_groups=groups)]
    unnamed x31 -> x32, local copies, waits for them, and re-layouts: 9.97 us -> 5.83 us
    pallas_call x7 -> x10, Pallas kernels: 31.9 us -> 29.6 us  [the longest x1 9.66 us: shards(): call(pool_kernel, shape((4, N * SUM_STEP, 128), F32), 4, (pltpu.VMEM((PAI...]
  transfers between devices with their start and end apart: 10 -> 9, of which waited for: 7 -> 9; matrix products, arithmetic and copies ran while one was open for 0% -> 0% of each run, Pallas kernels for 1% -> 7%
where the time goes in v3:
time: 240 us; the launch traced here: 239 us
  blocking collectives  99.5 us (41%)
  waiting for transfers between devices  54.3 us (23%)
  Pallas kernels  36.8 us (15%)
  starting transfers between devices  27.2 us (11%)
  between operations  14.3 us (6%)
  local copies, waits for them, and re-layouts  6.13 us (3%)
    all_to_all x4, blocking collectives, exchange(): return lax.all_to_all(x, axis, 0, 0, tiled=True, axis_index_groups=groups)  99.5 us
    all_to_all x4, waiting for transfers between devices, exchange(): return lax.all_to_all(x, axis, 0, 0, tiled=True, axis_index_groups=groups)  31.4 us
    all_to_all x4, starting transfers between devices, exchange(): return lax.all_to_all(x, axis, 0, 0, tiled=True, axis_index_groups=groups)  25.2 us
    ppermute x4, waiting for transfers between devices, swap(): return lax.ppermute(x, axis, [(i, i ^ bits) for i in range(N)])  15.5 us
    pallas_call x1, Pallas kernels, shards(): call(pool_kernel, shape((4, N * SUM_STEP, 128), F32), 4, (pltpu.VMEM((PAI...  9.66 us
    all_gather x1, waiting for transfers between devices, shards(): parts = lax.all_gather(parts, 'tok', axis=0)  7.47 us
    pallas_call x1, Pallas kernels, shards(): call(embed_kernel, shape((N, ROWS, 128), BF), 7, (pltpu.VMEM((TOK, 128),...  7.21 us
    unnamed x32, local copies, waits for them, and re-layouts  5.83 us
  transfers between devices with their start and end apart: 9, of which 9 were waited for; matrix products, arithmetic and copies ran while one was open for 0% of the time, Pallas kernels for 7%

profile of v3, /device:TPU:34, one launch (start us, length us, event | category | flops | bytes accessed | tf_op | source)
XLA Modules:
  0.0 238.9 jit_solution(225983682401560288)
XLA Ops:
  7.8 2.6 %shard_map.124 = bf16[16,80,128]{2,1,0:T(8,128)(2,1)} custom-call(s32[3]{0:T(128)} %pad_add_fusion.place, bf16[256,128]{1,0:T(8,128)(2,1)} %value.1, bf16[128,4096]{1,0:T(8,128)(2,1)} %pool_rows.1, bf16[128,4096]{1,0:T(8,128)(2,1)} %proj_rows.1), custom_call_target="tpu_custom_call" | custom-call | bytes 800000 | tf_op jit(solution)/shard_map/pallas_call | solution.py:438
  10.4 9.5 %all-to-all-start.1 = ((bf16[16,80,128]{2,1,0:T(8,128)(2,1)}), bf16[16,80,128]{2,1,0:T(8,128)(2,1)S(1)}, u32[]{:S(2)}, u32[]{:S(2)}) async-start(bf16[16,80,128]{2,1,0:T(8,128)(2,1)} %shard_map.124), calls=%async_computation.1 | async-start | bytes 655360 | tf_op jit(solution)/shard_map/all_to_all | solution.py:414
  20.0 1.1 copy-done.3
  21.2 7.2 %shard_map.122.early = bf16[16,416,128]{2,1,0:T(8,128)(2,1)S(1)} custom-call(s32[6]{0:T(128)S(1)} %copy-done.10, s32[3]{0:T(128)S(1)} %copy-done.9, bf16[6,16,128]{2,1,0:T(8,128)(2,1)S(1)} %copy-done.8, bf16[6,16,4096]{2,1,0:T(8,128)(2,1)S(1)} %copy-done.2, bf16[91,4096]{1,0:T(8,128)(2,1)S(1)} %copy-done.3, bf16[1,4096]{1,0:T(2,128)(2,1)S(1)} %broadcast_in_dim.3.gain, ...), custom_call_target="tpu_custom_call" | custom-call | flops 301989888 | bytes 6000000 | tf_op jit(solution)/shard_map/pallas_call | solution.py:450
  28.4 2.9 %all-to-all-done.1.parts = bf16[16,80,128]{2,1,0:T(8,128)(2,1)S(1)} async-done(((bf16[16,80,128]{2,1,0:T(8,128)(2,1)}), bf16[16,80,128]{2,1,0:T(8,128)(2,1)S(1)}, u32[]{:S(2)}, u32[]{:S(2)}) %all-to-all-start.1) | async-done | bytes 327712 | tf_op jit(solution)/shard_map/all_to_all | solution.py:414
  31.3 0.7 shard_map.125
  32.1 45.5 %all_to_all.40.got = bf16[16,416,128]{2,1,0:T(8,128)(2,1)S(1)} all-to-all(bf16[16,416,128]{2,1,0:T(8,128)(2,1)S(1)} %shard_map.122.early), channel_id=1, replica_groups=mesh['var'=16,'tok'=16] {'var'}, dimensions={0} | all-to-all | bytes 3407872 | tf_op jit(solution)/shard_map/all_to_all | solution.py:414
  78.0 2.0 collective-permute-done.swapped
  80.1 9.7 %shard_map.123.summed = f32[4,1040,128]{2,1,0:T(8,128)S(1)} custom-call(s32[3]{0:T(128)S(1)} %copy-done.9, bf16[16,416,128]{2,1,0:T(8,128)(2,1)S(1)} %all_to_all.40.got, bf16[16,192,128]{2,1,0:T(8,128)(2,1)S(1)} %collective-permute-done.swapped, bf16[1,512]{1,0:T(2,128)(2,1)S(1)} %reshape.19.gain), custom_call_target="tpu_custom_call" | custom-call | flops 800000000 | bytes 5000000 | tf_op jit(solution)/shard_map/pallas_call | solution.py:475
  89.7 1.3 copy-done
  91.1 7.5 %all-gather.3.cloned.1.call-done = bf16[20480,128]{1,0:T(8,128)(2,1)} async-done(((bf16[1280,128]{1,0:T(8,128)(2,1)}), bf16[20480,128]{1,0:T(8,128)(2,1)}) %all-gather.3.cloned.1.call-update) | async-done | bytes 5242896 | tf_op jit(solution)/shard_map/all_gather | solution.py:470
  98.5 4.7 %shard_map.126 = f32[8,128,128]{2,1,0:T(8,128)} custom-call(f32[4,1040,128]{2,1,0:T(8,128)} %copy-done, bf16[16,1280,128]{2,1,0:T(8,128)(2,1)} %bitcast.8), custom_call_target="tpu_custom_call" | custom-call | flops 268435456 | bytes 5000000 | tf_op jit(solution)/shard_map/pallas_call | solution.py:489
  103.3 23.0 %all_to_all.41.got = f32[8,128,128]{2,1,0:T(8,128)S(1)} all-to-all(f32[8,128,128]{2,1,0:T(8,128)} %shard_map.126), channel_id=1, replica_groups={{0,16,32,48,64,80,96,112},{128,144,160,176,192,208,224,240},{1,17,33,49..., dimensions={0} | all-to-all | bytes 1048576 | tf_op jit(solution)/shard_map/all_to_all | solution.py:414
  127.0 4.8 %all-to-all-start.3 = ((bf16[8,128,128]{2,1,0:T(8,128)(2,1)}), bf16[8,128,128]{2,1,0:T(8,128)(2,1)S(1)}, u32[]{:S(2)}, u32[]{:S(2)}) async-start(bf16[8,128,128]{2,1,0:T(8,128)(2,1)} %shard_map.127), calls=%async_computation.3 | async-start | bytes 524288 | tf_op jit(solution)/shard_map/all_to_all | solution.py:414
  131.8 10.5 %all-to-all-done.3.got = bf16[8,128,128]{2,1,0:T(8,128)(2,1)S(1)} async-done(((bf16[8,128,128]{2,1,0:T(8,128)(2,1)}), bf16[8,128,128]{2,1,0:T(8,128)(2,1)S(1)}, u32[]{:S(2)}, u32[]{:S(2)}) %all-to-all-start.3) | async-done | bytes 262176 | tf_op jit(solution)/shard_map/all_to_all | solution.py:414
  142.9 4.0 %shard_map.128 = (f32[64,512]{1,0:T(8,128)}, f32[8,8,128]{2,1,0:T(8,128)}) custom-call(bf16[8,128,128]{2,1,0:T(8,128)(2,1)} %copy-done.12, bf16[16,1280,128]{2,1,0:T(8,128)(2,1)} %bitcast.9), custom_call_target="tpu_custom_call" | custom-call | flops 134217728 | bytes 3000000 | tf_op jit(solution)/shard_map/pallas_call | solution.py:502
  146.9 4.7 %all-to-all-start.4 = ((f32[8,8,128]{2,1,0:T(8,128)}), f32[8,8,128]{2,1,0:T(8,128)S(1)}, u32[]{:S(2)}, u32[]{:S(2)}) async-start(f32[8,8,128]{2,1,0:T(8,128)} %get-tuple-element.10), calls=%async_computation.4 | async-start | bytes 65536 | tf_op jit(solution)/shard_map/all_to_all | solution.py:414
  151.7 6.6 %all-to-all-done.4.got = f32[8,8,128]{2,1,0:T(8,128)S(1)} async-done(((f32[8,8,128]{2,1,0:T(8,128)}), f32[8,8,128]{2,1,0:T(8,128)S(1)}, u32[]{:S(2)}, u32[]{:S(2)}) %all-to-all-start.4) | async-done | bytes 32800 | tf_op jit(solution)/shard_map/all_to_all | solution.py:414
  158.2 0.9 copy-done.4
  159.4 17.4 %all_to_all.42.own = bf16[8,64,512]{2,1,0:T(8,128)(2,1)S(1)} all-to-all(bf16[8,64,512]{2,1,0:T(8,128)(2,1)S(1)} %shard_map.129), channel_id=1, replica_groups={{0,16,32,48,64,80,96,112},{128,144,160,176,192,208,224,240},{1,17,33,49..., dimensions={0} | all-to-all | bytes 1048576 | tf_op jit(solution)/shard_map/all_to_all | solution.py:414
  176.7 1.3 collective-permute-start.1
  178.0 7.9 %collective-permute-done.1.other = bf16[8,64,512]{2,1,0:T(8,128)(2,1)S(1)} collective-permute-done((bf16[8,64,512]{2,1,0:T(8,128)(2,1)S(1)}, bf16[8,64,512]{2,1,0:T(8,128)(2,1)S(1)}, u32[]{:S(2)}, u32[]{:S(2)}) %collective-permute-start.1) | collective-permute-done | bytes 524320 | tf_op jit(solution)/shard_map/ppermute | solution.py:418
  185.9 0.9 copy-done.5
  186.8 1.6 shard_map.130
  188.4 13.6 %all_to_all.43.own = bf16[8,256,128]{2,1,0:T(8,128)(2,1)S(1)} all-to-all(bf16[8,256,128]{2,1,0:T(8,128)(2,1)S(1)} %get-tuple-element.13), channel_id=1, replica_groups={{0,2,4,6,8,10,12,14},{1,3,5,7,9,11,13,15},{16,18,20,22,24,26,28,30},{17..., dimensions={0} | all-to-all | bytes 1048576 | tf_op jit(solution)/shard_map/all_to_all | solution.py:414
  202.0 1.9 collective-permute-done.2.other
  203.9 2.0 shard_map.131
  205.9 6.3 %all-to-all-start.7 = ((bf16[16,128,128]{2,1,0:T(8,128)(2,1)}), bf16[16,128,128]{2,1,0:T(8,128)(2,1)S(1)}, u32[]{:S(2)}, u32[]{:S(2)}) async-start(bf16[16,128,128]{2,1,0:T(8,128)(2,1)} %shard_map.131), calls=%async_computation.7 | async-start | bytes 1048576 | tf_op jit(solution)/shard_map/all_to_all | solution.py:414
  212.8 3.6 %collective-permute-done.3.other = bf16[64,256]{1,0:T(8,128)(2,1)S(1)} collective-permute-done((bf16[64,256]{1,0:T(8,128)(2,1)S(1)}, bf16[64,256]{1,0:T(8,128)(2,1)S(1)}, u32[]{:S(2)}, u32[]{:S(2)}) %collective-permute-start.3) | collective-permute-done | bytes 32800 | tf_op jit(solution)/shard_map/ppermute | solution.py:418
  216.4 11.4 %all-to-all-done.7.got = bf16[16,128,128]{2,1,0:T(8,128)(2,1)S(1)} async-done(((bf16[16,128,128]{2,1,0:T(8,128)(2,1)}), bf16[16,128,128]{2,1,0:T(8,128)(2,1)S(1)}, u32[]{:S(2)}, u32[]{:S(2)}) %all-to-all-start.7) | async-done | bytes 524320 | tf_op jit(solution)/shard_map/all_to_all | solution.py:414
  227.9 0.8 copy-done.11
  228.7 3.4 %shard_map.132 = (bf16[128,256]{1,0:T(8,128)(2,1)}, bf16[128,256]{1,0:T(8,128)(2,1)}) custom-call(s32[3]{0:T(128)} %pad_add_fusion.place, bf16[16,128,128]{2,1,0:T(8,128)(2,1)} %copy-done.11, bf16[16,1280,128]{2,1,0:T(8,128)(2,1)} %bitcast.10, bf16[64,256]{1,0:T(8,128)(2,1)} %copy-done.7, bf16[64,256]{1,0:T(8,128)(2,1)} %copy-done.13), custom_call_target="tpu_custom_call" | custom-call | flops 134217728 | bytes 2000000 | tf_op jit(solution)/shard_map/pallas_call | solution.py:544
  (42 shorter events, 3.3 us)
Async XLA Ops:
  7.2 12.8 %copy-start.14 = (bf16[4096]{0:T(1024)(128)(2,1)S(1)}, bf16[4096]{0:T(1024)(128)(2,1)}, u32[]{:S(2)}) copy-start(bf16[4096]{0:T(1024)(128)(2,1)} %param.15) | copy-start | bytes 24580
  7.2 12.8 %copy-start.6 = (bf16[4096,16]{0,1:T(8,128)(2,1)S(1)}, bf16[4096,16]{0,1:T(8,128)(2,1)}, u32[]{:S(2)}) copy-start(bf16[4096,16]{0,1:T(8,128)(2,1)} %param.16) | copy-start | bytes 393220
  7.2 12.8 %copy-start.8 = (bf16[6,16,128]{2,1,0:T(8,128)(2,1)S(1)}, bf16[6,16,128]{2,1,0:T(8,128)(2,1)}, u32[]{:S(2)}) copy-start(bf16[6,16,128]{2,1,0:T(8,128)(2,1)} %patches.1) | copy-start | bytes 73732
  7.2 12.8 %copy-start.10 = (s32[6]{0:T(128)S(1)}, s32[6]{0:T(128)}, u32[]{:S(2)}) copy-start(s32[6]{0:T(128)} %slot.1) | copy-start | bytes 76
  7.2 12.8 %copy-start.2 = (bf16[6,16,4096]{2,1,0:T(8,128)(2,1)S(1)}, bf16[6,16,4096]{2,1,0:T(8,128)(2,1)}, u32[]{:S(2)}) copy-start(bf16[6,16,4096]{2,1,0:T(8,128)(2,1)} %weight.2) | copy-start | bytes 2359300
  7.8 12.2 %copy-start.9 = (s32[3]{0:T(128)S(1)}, s32[3]{0:T(128)}, u32[]{:S(2)}) copy-start(s32[3]{0:T(128)} %pad_add_fusion.place) | copy-start | bytes 40
  10.4 20.9 %all-to-all-start.1 = ((bf16[16,80,128]{2,1,0:T(8,128)(2,1)}), bf16[16,80,128]{2,1,0:T(8,128)(2,1)S(1)}, u32[]{:S(2)}, u32[]{:S(2)}) async-start(bf16[16,80,128]{2,1,0:T(8,128)(2,1)} %shard_map.124), calls=%async_computation.1 | async-start | bytes 655360 | tf_op jit(solution)/shard_map/all_to_all | solution.py:414
  19.9 78.6 %all-gather.3.cloned.1.call-start = ((), (), s32[]{:S(2)}) async-start(), calls=%async_computation.8 | async-start | bytes 5570560 | tf_op jit(solution)/shard_map/all_gather | solution.py:470
  20.0 1.1 copy-start.3
  77.7 2.4 collective-permute-start
  89.7 1.3 copy-start
  103.3 28.5 %copy-start.15 = (bf16[4096]{0:T(1024)(128)(2,1)S(1)}, bf16[4096]{0:T(1024)(128)(2,1)}, u32[]{:S(2)}) copy-start(bf16[4096]{0:T(1024)(128)(2,1)} %param.19) | copy-start | bytes 24580
  127.0 15.3 %all-to-all-start.3 = ((bf16[8,128,128]{2,1,0:T(8,128)(2,1)}), bf16[8,128,128]{2,1,0:T(8,128)(2,1)S(1)}, u32[]{:S(2)}, u32[]{:S(2)}) async-start(bf16[8,128,128]{2,1,0:T(8,128)(2,1)} %shard_map.127), calls=%async_computation.3 | async-start | bytes 524288 | tf_op jit(solution)/shard_map/all_to_all | solution.py:414
  142.2 0.7 copy-start.12
  142.9 42.9 %copy-start.1 = (bf16[3,4096,128]{2,1,0:T(8,128)(2,1)S(1)}, bf16[3,4096,128]{2,1,0:T(8,128)(2,1)}, u32[]{:S(2)}) copy-start(bf16[3,4096,128]{2,1,0:T(8,128)(2,1)} %weight.3) | copy-start | bytes 9437188
  146.9 11.3 %all-to-all-start.4 = ((f32[8,8,128]{2,1,0:T(8,128)}), f32[8,8,128]{2,1,0:T(8,128)S(1)}, u32[]{:S(2)}, u32[]{:S(2)}) async-start(f32[8,8,128]{2,1,0:T(8,128)} %get-tuple-element.10), calls=%async_computation.4 | async-start | bytes 65536 | tf_op jit(solution)/shard_map/all_to_all | solution.py:414
  158.2 0.9 copy-start.4
  176.7 9.2 %collective-permute-start.1 = (bf16[8,64,512]{2,1,0:T(8,128)(2,1)S(1)}, bf16[8,64,512]{2,1,0:T(8,128)(2,1)S(1)}, u32[]{:S(2)}, u32[]{:S(2)}) collective-permute-start(bf16[8,64,512]{2,1,0:T(8,128)(2,1)S(1)} %all_to_all.42.own), channel_id=1, source_target_pairs={{0,128},{16,144},{32,160},{48,176},{64,192},{80,208},{96,224},{112... | collective-permute-start | bytes 1572872 | tf_op jit(solution)/shard_map/ppermute | solution.py:418
  185.9 0.9 copy-start.5
  188.4 15.5 %copy-start.7 = (bf16[64,256]{1,0:T(8,128)(2,1)}, bf16[64,256]{1,0:T(8,128)(2,1)S(1)}, u32[]{:S(2)}) copy-start(bf16[64,256]{1,0:T(8,128)(2,1)S(1)} %get-tuple-element.14.own) | copy-start | bytes 98308
  202.0 1.9 collective-permute-start.2
  205.9 21.9 %all-to-all-start.7 = ((bf16[16,128,128]{2,1,0:T(8,128)(2,1)}), bf16[16,128,128]{2,1,0:T(8,128)(2,1)S(1)}, u32[]{:S(2)}, u32[]{:S(2)}) async-start(bf16[16,128,128]{2,1,0:T(8,128)(2,1)} %shard_map.131), calls=%async_computation.7 | async-start | bytes 1048576 | tf_op jit(solution)/shard_map/all_to_all | solution.py:414
  212.2 4.2 %collective-permute-start.3 = (bf16[64,256]{1,0:T(8,128)(2,1)S(1)}, bf16[64,256]{1,0:T(8,128)(2,1)S(1)}, u32[]{:S(2)}, u32[]{:S(2)}) collective-permute-start(bf16[64,256]{1,0:T(8,128)(2,1)S(1)} %get-tuple-element.15), channel_id=1, source_target_pairs={{0,128},{16,144},{32,160},{48,176},{64,192},{80,208},{96,224},{112... | collective-permute-start | bytes 98312 | tf_op jit(solution)/shard_map/ppermute | solution.py:418
  216.4 11.4 %copy-start.13 = (bf16[64,256]{1,0:T(8,128)(2,1)}, bf16[64,256]{1,0:T(8,128)(2,1)S(1)}, u32[]{:S(2)}) copy-start(bf16[64,256]{1,0:T(8,128)(2,1)S(1)} %collective-permute-done.3.other) | copy-start | bytes 98308
  227.9 0.8 copy-start.11
Sparse Core Ops, SparseCore 0:
  32.2 66.2 all-gather.2

commit v4 on v3

--- a/solution.py
+++ b/solution.py
@@ -492,7 +492,7 @@
         2,
         (pltpu.VMEM((N, 32 * N, E), BF), pltpu.SemaphoreType.DMA),
         hbm=(1,),
-        vmem=60,
+        vmem=16,
         flops=4 * PART * WIDE * 2048,
         size=5_000_000,
     )(summed, parts)
@@ -509,7 +509,7 @@
             pltpu.SemaphoreType.DMA,
         ),
         hbm=(1,),
-        vmem=60,
+        vmem=16,
         flops=2 * PART * 2048 * WIDE,
         size=3_000_000,
     )(exchange(pooled, "var", RINGS), parts)
@@ -548,7 +548,7 @@
         (pltpu.VMEM((N, 16 * N, 128), BF), pltpu.SemaphoreType.DMA),
         smem=(0,),
         hbm=(2,),
-        vmem=60,
+        vmem=16,
         flops=2 * TOK * 2048 * COLS,
         size=2_000_000,
     )(place, exchange(context, "var"), parts, keep, swap(send, "var", Z))

time: 240 us -> 237 us (0.988)
  Pallas kernels: 36.8 us -> 28.1 us
  local copies, waits for them, and re-layouts: 6.13 us -> 12.5 us
    unnamed x32 -> x30, local copies, waits for them, and re-layouts: 5.83 us -> 12.1 us
    pallas_call x1, Pallas kernels: 4.72 us -> 0.85 us  [shards(): call(values_kernel, shape((Z, TOK, E), F32), 2, (pltpu.VMEM((N, 32 * N, E...]
    pallas_call x1, Pallas kernels: 3.98 us -> 0.82 us  [shards(): call(state_kernel, (shape((PART, WIDE), F32), shape((Z, 8, 128), F32)), 2...]
where the time goes in v4:
time: 237 us; the launch traced here: 236 us
  blocking collectives  99.2 us (42%)
  waiting for transfers between devices  54.4 us (23%)
  Pallas kernels  28.1 us (12%)
  starting transfers between devices  27.2 us (11%)
  between operations  14.3 us (6%)
  local copies, waits for them, and re-layouts  12.5 us (5%)
    all_to_all x4, blocking collectives, exchange(): return lax.all_to_all(x, axis, 0, 0, tiled=True, axis_index_groups=groups)  99.2 us
    all_to_all x4, waiting for transfers between devices, exchange(): return lax.all_to_all(x, axis, 0, 0, tiled=True, axis_index_groups=groups)  31.4 us
    all_to_all x4, starting transfers between devices, exchange(): return lax.all_to_all(x, axis, 0, 0, tiled=True, axis_index_groups=groups)  25.2 us
    ppermute x4, waiting for transfers between devices, swap(): return lax.ppermute(x, axis, [(i, i ^ bits) for i in range(N)])  15.4 us
    unnamed x30, local copies, waits for them, and re-layouts  12.1 us
    pallas_call x1, Pallas kernels, shards(): call(pool_kernel, shape((4, N * SUM_STEP, 128), F32), 4, (pltpu.VMEM((PAI...  9.65 us
    all_gather x1, waiting for transfers between devices, shards(): parts = lax.all_gather(parts, 'tok', axis=0)  7.54 us
    pallas_call x1, Pallas kernels, shards(): call(embed_kernel, shape((N, ROWS, 128), BF), 7, (pltpu.VMEM((TOK, 128),...  7.16 us
  transfers between devices with their start and end apart: 9, of which 9 were waited for; matrix products, arithmetic and copies ran while one was open for 0% of the time, Pallas kernels for 7%

profile of v4, /device:TPU:34, one launch (start us, length us, event | category | flops | bytes accessed | tf_op | source)
XLA Modules:
  0.0 236.4 jit_solution(16672076411712438916)
XLA Ops:
  7.9 2.6 %shard_map.124 = bf16[16,80,128]{2,1,0:T(8,128)(2,1)} custom-call(s32[3]{0:T(128)} %pad_add_fusion.place, bf16[256,128]{1,0:T(8,128)(2,1)} %value.1, bf16[128,4096]{1,0:T(8,128)(2,1)} %pool_rows.1, bf16[128,4096]{1,0:T(8,128)(2,1)} %proj_rows.1), custom_call_target="tpu_custom_call" | custom-call | bytes 800000 | tf_op jit(solution)/shard_map/pallas_call | solution.py:438
  10.5 9.5 %all-to-all-start.1 = ((bf16[16,80,128]{2,1,0:T(8,128)(2,1)}), bf16[16,80,128]{2,1,0:T(8,128)(2,1)S(1)}, u32[]{:S(2)}, u32[]{:S(2)}) async-start(bf16[16,80,128]{2,1,0:T(8,128)(2,1)} %shard_map.124), calls=%async_computation.1 | async-start | bytes 655360 | tf_op jit(solution)/shard_map/all_to_all | solution.py:414
  20.1 1.1 copy-done.7
  21.2 7.2 %shard_map.122.early = bf16[16,416,128]{2,1,0:T(8,128)(2,1)S(1)} custom-call(s32[6]{0:T(128)S(1)} %copy-done.12, s32[3]{0:T(128)S(1)} %copy-done.11, bf16[6,16,128]{2,1,0:T(8,128)(2,1)S(1)} %copy-done.10, bf16[6,16,4096]{2,1,0:T(8,128)(2,1)S(1)} %copy-done.6, bf16[91,4096]{1,0:T(8,128)(2,1)S(1)} %copy-done.7, bf16[1,4096]{1,0:T(2,128)(2,1)S(1)} %broadcast_in_dim.3.gain, ...), custom_call_target="tpu_custom_call" | custom-call | flops 301989888 | bytes 6000000 | tf_op jit(solution)/shard_map/pallas_call | solution.py:450
  28.4 3.0 %all-to-all-done.1.parts = bf16[16,80,128]{2,1,0:T(8,128)(2,1)S(1)} async-done(((bf16[16,80,128]{2,1,0:T(8,128)(2,1)}), bf16[16,80,128]{2,1,0:T(8,128)(2,1)S(1)}, u32[]{:S(2)}, u32[]{:S(2)}) %all-to-all-start.1) | async-done | bytes 327712 | tf_op jit(solution)/shard_map/all_to_all | solution.py:414
  32.1 45.5 %all_to_all.40.got = bf16[16,416,128]{2,1,0:T(8,128)(2,1)S(1)} all-to-all(bf16[16,416,128]{2,1,0:T(8,128)(2,1)S(1)} %shard_map.122.early), channel_id=1, replica_groups=mesh['var'=16,'tok'=16] {'var'}, dimensions={0} | all-to-all | bytes 3407872 | tf_op jit(solution)/shard_map/all_to_all | solution.py:414
  78.0 2.0 collective-permute-done.swapped
  80.1 9.6 %shard_map.123.summed = f32[4,1040,128]{2,1,0:T(8,128)S(1)} custom-call(s32[3]{0:T(128)S(1)} %copy-done.11, bf16[16,416,128]{2,1,0:T(8,128)(2,1)S(1)} %all_to_all.40.got, bf16[16,192,128]{2,1,0:T(8,128)(2,1)S(1)} %collective-permute-done.swapped, bf16[1,512]{1,0:T(2,128)(2,1)S(1)} %reshape.19.gain), custom_call_target="tpu_custom_call" | custom-call | flops 800000000 | bytes 5000000 | tf_op jit(solution)/shard_map/pallas_call | solution.py:475
  89.7 1.3 copy-done.3
  91.1 7.5 %all-gather.3.cloned.1.call-done = bf16[20480,128]{1,0:T(8,128)(2,1)} async-done(((bf16[1280,128]{1,0:T(8,128)(2,1)}), bf16[20480,128]{1,0:T(8,128)(2,1)}) %all-gather.3.cloned.1.call-update) | async-done | bytes 5242896 | tf_op jit(solution)/shard_map/all_gather | solution.py:470
  98.6 2.5 %copy-done = bf16[20480,128]{1,0:T(8,128)(2,1)S(1)} copy-done((bf16[20480,128]{1,0:T(8,128)(2,1)S(1)}, bf16[20480,128]{1,0:T(8,128)(2,1)}, u32[]{:S(2)}) %copy-start) | copy-done | bytes 5242904
  101.1 1.6 copy-done.4
  102.7 0.9 shard_map.126
  103.5 22.8 %all_to_all.41.got = f32[8,128,128]{2,1,0:T(8,128)S(1)} all-to-all(f32[8,128,128]{2,1,0:T(8,128)S(1)} %shard_map.126), channel_id=1, replica_groups={{0,16,32,48,64,80,96,112},{128,144,160,176,192,208,224,240},{1,17,33,49..., dimensions={0} | all-to-all | bytes 1048576 | tf_op jit(solution)/shard_map/all_to_all | solution.py:414
  127.1 4.8 %all-to-all-start.3 = ((bf16[8,128,128]{2,1,0:T(8,128)(2,1)}), bf16[8,128,128]{2,1,0:T(8,128)(2,1)S(1)}, u32[]{:S(2)}, u32[]{:S(2)}) async-start(bf16[8,128,128]{2,1,0:T(8,128)(2,1)} %shard_map.127), calls=%async_computation.3 | async-start | bytes 524288 | tf_op jit(solution)/shard_map/all_to_all | solution.py:414
  131.9 10.5 %all-to-all-done.3.got = bf16[8,128,128]{2,1,0:T(8,128)(2,1)S(1)} async-done(((bf16[8,128,128]{2,1,0:T(8,128)(2,1)}), bf16[8,128,128]{2,1,0:T(8,128)(2,1)S(1)}, u32[]{:S(2)}, u32[]{:S(2)}) %all-to-all-start.3) | async-done | bytes 262176 | tf_op jit(solution)/shard_map/all_to_all | solution.py:414
  142.3 2.5 %copy-done.1 = bf16[20480,128]{1,0:T(8,128)(2,1)S(1)} copy-done((bf16[20480,128]{1,0:T(8,128)(2,1)S(1)}, bf16[20480,128]{1,0:T(8,128)(2,1)}, u32[]{:S(2)}) %copy-start.1) | copy-done | bytes 5242904
  144.8 0.8 shard_map.128
  146.3 4.7 %all-to-all-start.4 = ((f32[8,8,128]{2,1,0:T(8,128)}), f32[8,8,128]{2,1,0:T(8,128)S(1)}, u32[]{:S(2)}, u32[]{:S(2)}) async-start(f32[8,8,128]{2,1,0:T(8,128)} %copy-done.9), calls=%async_computation.4 | async-start | bytes 65536 | tf_op jit(solution)/shard_map/all_to_all | solution.py:414
  151.0 6.6 %all-to-all-done.4.got = f32[8,8,128]{2,1,0:T(8,128)S(1)} async-done(((f32[8,8,128]{2,1,0:T(8,128)}), f32[8,8,128]{2,1,0:T(8,128)S(1)}, u32[]{:S(2)}, u32[]{:S(2)}) %all-to-all-start.4) | async-done | bytes 32800 | tf_op jit(solution)/shard_map/all_to_all | solution.py:414
  157.8 17.4 %all_to_all.42.own = bf16[8,64,512]{2,1,0:T(8,128)(2,1)S(1)} all-to-all(bf16[8,64,512]{2,1,0:T(8,128)(2,1)S(1)} %shard_map.129), channel_id=1, replica_groups={{0,16,32,48,64,80,96,112},{128,144,160,176,192,208,224,240},{1,17,33,49..., dimensions={0} | all-to-all | bytes 1048576 | tf_op jit(solution)/shard_map/all_to_all | solution.py:414
  175.1 1.3 collective-permute-start.1
  176.4 7.9 %collective-permute-done.1.other = bf16[8,64,512]{2,1,0:T(8,128)(2,1)S(1)} collective-permute-done((bf16[8,64,512]{2,1,0:T(8,128)(2,1)S(1)}, bf16[8,64,512]{2,1,0:T(8,128)(2,1)S(1)}, u32[]{:S(2)}, u32[]{:S(2)}) %collective-permute-start.1) | collective-permute-done | bytes 524320 | tf_op jit(solution)/shard_map/ppermute | solution.py:418
  184.3 1.6 shard_map.130
  185.9 13.6 %all_to_all.43.own = bf16[8,256,128]{2,1,0:T(8,128)(2,1)S(1)} all-to-all(bf16[8,256,128]{2,1,0:T(8,128)(2,1)S(1)} %get-tuple-element.13), channel_id=1, replica_groups={{0,2,4,6,8,10,12,14},{1,3,5,7,9,11,13,15},{16,18,20,22,24,26,28,30},{17..., dimensions={0} | all-to-all | bytes 1048576 | tf_op jit(solution)/shard_map/all_to_all | solution.py:414
  199.5 1.9 collective-permute-done.2.other
  201.4 2.0 shard_map.131
  203.4 6.3 %all-to-all-start.7 = ((bf16[16,128,128]{2,1,0:T(8,128)(2,1)}), bf16[16,128,128]{2,1,0:T(8,128)(2,1)S(1)}, u32[]{:S(2)}, u32[]{:S(2)}) async-start(bf16[16,128,128]{2,1,0:T(8,128)(2,1)} %shard_map.131), calls=%async_computation.7 | async-start | bytes 1048576 | tf_op jit(solution)/shard_map/all_to_all | solution.py:414
  210.3 3.6 %collective-permute-done.3.other = bf16[64,256]{1,0:T(8,128)(2,1)S(1)} collective-permute-done((bf16[64,256]{1,0:T(8,128)(2,1)S(1)}, bf16[64,256]{1,0:T(8,128)(2,1)S(1)}, u32[]{:S(2)}, u32[]{:S(2)}) %collective-permute-start.3) | collective-permute-done | bytes 32800 | tf_op jit(solution)/shard_map/ppermute | solution.py:418
  213.9 11.4 %all-to-all-done.7.got = bf16[16,128,128]{2,1,0:T(8,128)(2,1)S(1)} async-done(((bf16[16,128,128]{2,1,0:T(8,128)(2,1)}), bf16[16,128,128]{2,1,0:T(8,128)(2,1)S(1)}, u32[]{:S(2)}, u32[]{:S(2)}) %all-to-all-start.7) | async-done | bytes 524320 | tf_op jit(solution)/shard_map/all_to_all | solution.py:414
  225.3 2.5 %copy-done.2 = bf16[20480,128]{1,0:T(8,128)(2,1)S(1)} copy-done((bf16[20480,128]{1,0:T(8,128)(2,1)S(1)}, bf16[20480,128]{1,0:T(8,128)(2,1)}, u32[]{:S(2)}) %copy-start.2) | copy-done | bytes 5242904
  227.8 1.7 shard_map.132
  (40 shorter events, 4.0 us)
Async XLA Ops:
  7.2 12.8 %copy-start.13 = (bf16[4096]{0:T(1024)(128)(2,1)S(1)}, bf16[4096]{0:T(1024)(128)(2,1)}, u32[]{:S(2)}) copy-start(bf16[4096]{0:T(1024)(128)(2,1)} %param.15) | copy-start | bytes 24580
  7.2 12.9 %copy-start.8 = (bf16[4096,16]{0,1:T(8,128)(2,1)S(1)}, bf16[4096,16]{0,1:T(8,128)(2,1)}, u32[]{:S(2)}) copy-start(bf16[4096,16]{0,1:T(8,128)(2,1)} %param.16) | copy-start | bytes 393220
  7.2 12.9 %copy-start.10 = (bf16[6,16,128]{2,1,0:T(8,128)(2,1)S(1)}, bf16[6,16,128]{2,1,0:T(8,128)(2,1)}, u32[]{:S(2)}) copy-start(bf16[6,16,128]{2,1,0:T(8,128)(2,1)} %patches.1) | copy-start | bytes 73732
  7.2 12.9 %copy-start.12 = (s32[6]{0:T(128)S(1)}, s32[6]{0:T(128)}, u32[]{:S(2)}) copy-start(s32[6]{0:T(128)} %slot.1) | copy-start | bytes 76
  7.2 12.9 %copy-start.6 = (bf16[6,16,4096]{2,1,0:T(8,128)(2,1)S(1)}, bf16[6,16,4096]{2,1,0:T(8,128)(2,1)}, u32[]{:S(2)}) copy-start(bf16[6,16,4096]{2,1,0:T(8,128)(2,1)} %weight.2) | copy-start | bytes 2359300
  7.9 12.2 %copy-start.11 = (s32[3]{0:T(128)S(1)}, s32[3]{0:T(128)}, u32[]{:S(2)}) copy-start(s32[3]{0:T(128)} %pad_add_fusion.place) | copy-start | bytes 40
  10.5 20.9 %all-to-all-start.1 = ((bf16[16,80,128]{2,1,0:T(8,128)(2,1)}), bf16[16,80,128]{2,1,0:T(8,128)(2,1)S(1)}, u32[]{:S(2)}, u32[]{:S(2)}) async-start(bf16[16,80,128]{2,1,0:T(8,128)(2,1)} %shard_map.124), calls=%async_computation.1 | async-start | bytes 655360 | tf_op jit(solution)/shard_map/all_to_all | solution.py:414
  20.0 78.6 %all-gather.3.cloned.1.call-start = ((), (), s32[]{:S(2)}) async-start(), calls=%async_computation.8 | async-start | bytes 5570560 | tf_op jit(solution)/shard_map/all_gather | solution.py:470
  20.1 1.1 copy-start.7
  77.7 2.4 %collective-permute-start = (bf16[16,192,128]{2,1,0:T(8,128)(2,1)S(1)}, bf16[16,192,128]{2,1,0:T(8,128)(2,1)S(1)}, u32[]{:S(2)}, u32[]{:S(2)}) collective-permute-start(bf16[16,192,128]{2,1,0:T(8,128)(2,1)S(1)} %slice.4), channel_id=1, source_target_pairs={{0,1},{1,0},{2,3},{3,2},{4,5},{5,4},{6,7},{7,6},{8,9},{9,8},{10,11... | collective-permute-start | bytes 2359304 | tf_op jit(solution)/shard_map/ppermute | solution.py:418
  89.7 1.3 copy-start.3
  98.6 2.5 %copy-start = (bf16[20480,128]{1,0:T(8,128)(2,1)S(1)}, bf16[20480,128]{1,0:T(8,128)(2,1)}, u32[]{:S(2)}) copy-start(bf16[20480,128]{1,0:T(8,128)(2,1)} %all-gather.3.cloned.1.call-done) | copy-start | bytes 15728644
  101.1 1.6 copy-start.4
  103.5 28.3 %copy-start.14 = (bf16[4096]{0:T(1024)(128)(2,1)S(1)}, bf16[4096]{0:T(1024)(128)(2,1)}, u32[]{:S(2)}) copy-start(bf16[4096]{0:T(1024)(128)(2,1)} %param.19) | copy-start | bytes 24580
  127.1 15.3 %all-to-all-start.3 = ((bf16[8,128,128]{2,1,0:T(8,128)(2,1)}), bf16[8,128,128]{2,1,0:T(8,128)(2,1)S(1)}, u32[]{:S(2)}, u32[]{:S(2)}) async-start(bf16[8,128,128]{2,1,0:T(8,128)(2,1)} %shard_map.127), calls=%async_computation.3 | async-start | bytes 524288 | tf_op jit(solution)/shard_map/all_to_all | solution.py:414
  142.3 2.5 %copy-start.1 = (bf16[20480,128]{1,0:T(8,128)(2,1)S(1)}, bf16[20480,128]{1,0:T(8,128)(2,1)}, u32[]{:S(2)}) copy-start(bf16[20480,128]{1,0:T(8,128)(2,1)} %all-gather.3.cloned.1.call-done) | copy-start | bytes 15728644
  144.8 39.5 %copy-start.5 = (bf16[3,4096,128]{2,1,0:T(8,128)(2,1)S(1)}, bf16[3,4096,128]{2,1,0:T(8,128)(2,1)}, u32[]{:S(2)}) copy-start(bf16[3,4096,128]{2,1,0:T(8,128)(2,1)} %weight.3) | copy-start | bytes 9437188
  145.6 0.6 copy-start.9
  146.3 11.3 %all-to-all-start.4 = ((f32[8,8,128]{2,1,0:T(8,128)}), f32[8,8,128]{2,1,0:T(8,128)S(1)}, u32[]{:S(2)}, u32[]{:S(2)}) async-start(f32[8,8,128]{2,1,0:T(8,128)} %copy-done.9), calls=%async_computation.4 | async-start | bytes 65536 | tf_op jit(solution)/shard_map/all_to_all | solution.py:414
  175.1 9.2 %collective-permute-start.1 = (bf16[8,64,512]{2,1,0:T(8,128)(2,1)S(1)}, bf16[8,64,512]{2,1,0:T(8,128)(2,1)S(1)}, u32[]{:S(2)}, u32[]{:S(2)}) collective-permute-start(bf16[8,64,512]{2,1,0:T(8,128)(2,1)S(1)} %all_to_all.42.own), channel_id=1, source_target_pairs={{0,128},{16,144},{32,160},{48,176},{64,192},{80,208},{96,224},{112... | collective-permute-start | bytes 1572872 | tf_op jit(solution)/shard_map/ppermute | solution.py:418
  199.5 1.9 collective-permute-start.2
  203.4 21.9 %all-to-all-start.7 = ((bf16[16,128,128]{2,1,0:T(8,128)(2,1)}), bf16[16,128,128]{2,1,0:T(8,128)(2,1)S(1)}, u32[]{:S(2)}, u32[]{:S(2)}) async-start(bf16[16,128,128]{2,1,0:T(8,128)(2,1)} %shard_map.131), calls=%async_computation.7 | async-start | bytes 1048576 | tf_op jit(solution)/shard_map/all_to_all | solution.py:414
  209.7 4.2 %collective-permute-start.3 = (bf16[64,256]{1,0:T(8,128)(2,1)S(1)}, bf16[64,256]{1,0:T(8,128)(2,1)S(1)}, u32[]{:S(2)}, u32[]{:S(2)}) collective-permute-start(bf16[64,256]{1,0:T(8,128)(2,1)S(1)} %get-tuple-element.15), channel_id=1, source_target_pairs={{0,128},{16,144},{32,160},{48,176},{64,192},{80,208},{96,224},{112... | collective-permute-start | bytes 98312 | tf_op jit(solution)/shard_map/ppermute | solution.py:418
  225.3 2.5 %copy-start.2 = (bf16[20480,128]{1,0:T(8,128)(2,1)S(1)}, bf16[20480,128]{1,0:T(8,128)(2,1)}, u32[]{:S(2)}) copy-start(bf16[20480,128]{1,0:T(8,128)(2,1)} %all-gather.3.cloned.1.call-done) | copy-start | bytes 15728644
Sparse Core Ops, SparseCore 0:
  32.3 66.2 all-gather.2

commit v5 on v4

--- a/solution.py
+++ b/solution.py
@@ -26,7 +26,7 @@
 
 
 R_U, R_P, R_WH, R_WL, R_M, R_ST, ROWS = 0, 192, 240, 288, 336, 368, 416
-W_V, W_P, W_O, W_ROWS = 0, 32, 64, 80
+W_V, W_P, W_O, W_ROWS = 0, 32, 48, 64
 
 
 def split2(x):
@@ -56,21 +56,13 @@
     )
 
 
-def fetch(parts, row, into, sem):
-    copy = pltpu.make_async_copy(parts.at[:, N * row : N * row + into.shape[1]], into, sem)
-    copy.start()
-    copy.wait()
-
-
 def weights_kernel(place, value, pool_rows, proj_rows, out):
     half = place[1]
     for v in range(N):
         z = v % Z
         out[v, W_V : W_V + 32] = value[32 * z : 32 * z + 32]
-        for x in range(2):
-            at = pl.ds(pl.multiple_of(COLS * (Z * x + z) + 128 * half, 128), 128)
-            out[v, W_P + 16 * x : W_P + 16 * x + 16] = pool_rows[:, at]
         at = pl.ds(pl.multiple_of(COLS * v + 128 * half, 128), 128)
+        out[v, W_P : W_P + 16] = pool_rows[:, at]
         out[v, W_O : W_O + 16] = proj_rows[:, at]
 
 
@@ -250,14 +242,22 @@
     lax.fori_loop(0, PART // 2, two_tokens, 0, unroll=4)
 
 
-def values_kernel(summed, parts, out, value, sem):
-    fetch(parts, W_V, value, sem)
+def values_kernel(summed, parts, out, pool_part, proj_part, value, sems):
+    copies = []
+    for i, (row, into) in enumerate(((W_V, value), (W_P, pool_part), (W_O, proj_part))):
+        span = pl.ds(N * row, into.shape[1])
+        copies.append(pltpu.make_async_copy(parts.at[:, span], into, sems.at[i]))
+    for copy in copies:
+        copy.start()
+    copies[0].wait()
     for h in range(N):
         at = slice(SUM_STEP * h, SUM_STEP * h + PART)
         hi, lo = split2(jnp.concatenate([summed[j, at] for j in range(4)], 1))
         right = jnp.concatenate([value[k, 32 * h : 32 * h + 32] for k in range(N)], 0)
         whole = jnp.dot(jnp.concatenate([hi, lo], 0), right, preferred_element_type=F32)
         out[h // 2, PART * (h % 2) : PART * (h % 2) + PART] = whole[:PART] + whole[PART:]
+    for copy in copies[1:]:
+        copy.wait()
 
 
 def pooled_kernel(got, out):
@@ -265,20 +265,19 @@
     for z in range(1, Z):
         total = total + got[z]
     total = total.astype(BF)
-    for z in range(Z):
-        out[z] = total
-
-
-def columns_of(blocks, weight):
+    for v in range(N):
+        out[v] = total
+
+
+def columns_of(pairs, weight):
     halves = []
     for half in range(2):
         acc = None
-        for h in range(0, N, 2):
-            left = jnp.concatenate([blocks[h], blocks[h + 1]], 1)
+        for i, left in enumerate(pairs):
             right = jnp.concatenate(
                 [
                     weight[2 * j + half, a : a + 16]
-                    for a in (16 * h, 16 * h + 16)
+                    for a in (32 * i, 32 * i + 16)
                     for j in range(8)
                 ],
                 0,
@@ -289,83 +288,59 @@
     return halves
 
 
-def state_kernel(got, parts, state, stats, columns, weight, sem):
-    fetch(parts, W_P, weight, sem)
-    lefts = [jnp.concatenate([got[z, 0:PART], got[z, PART : 2 * PART]], 1) for z in range(Z)]
-    total = None
-    for c in range(4):
-        acc = None
-        for z in range(Z):
-            right = jnp.concatenate(
-                [
-                    weight[2 * j + c % 2, a : a + 16]
-                    for a in (64 * z + 16 * (c // 2), 64 * z + 32 + 16 * (c // 2))
-                    for j in range(8)
-                ],
-                0,
-            )
-            term = jnp.dot(lefts[z], right, preferred_element_type=F32)
-            acc = term if acc is None else acc + term
-        state[:, 128 * c : 128 * c + 128] = acc
-        total = acc if total is None else total + acc
-    mean = jnp.sum(total, axis=1, keepdims=True) * (1.0 / WIDE)
-    spread = jnp.zeros((PART, 128), F32)
-    for c in range(4):
-        gap = state[:, 128 * c : 128 * c + 128] - mean
+def state_kernel(got, weight, state, aggregated, stats, columns):
+    pairs = []
+    for z in range(Z):
+        sides = [
+            jnp.concatenate([got[v, 0:PART], got[v, PART : 2 * PART]], 1) for v in (z, Z + z)
+        ]
+        pairs.append(jnp.concatenate(sides, 0))
+    halves = columns_of(pairs, weight)
+    mean = jnp.sum(halves[0] + halves[1], axis=1, keepdims=True) * (1.0 / COLS)
+    spread = jnp.zeros((TOK, 128), F32)
+    for i in range(2):
+        state[:, 128 * i : 128 * i + 128] = halves[i]
+        aggregated[:, 128 * i : 128 * i + 128] = halves[i].astype(BF)
+        gap = halves[i] - mean
         spread = spread + gap * gap
     columns[...] = jnp.zeros_like(columns)
-    columns[0:PART, 0:1] = mean
-    columns[0:PART, 1:2] = jnp.sum(spread, axis=1, keepdims=True)
+    columns[:, 0:1] = mean
+    columns[:, 1:2] = jnp.sum(spread, axis=1, keepdims=True)
     turned = jnp.transpose(columns[...])[0:8]
-    for z in range(Z):
-        stats[z] = turned
+    for v in range(N):
+        stats[v] = turned
 
 
 def norm_kernel(got, state, gain, out):
     mean = got[0, 0:1]
-    for z in range(1, Z):
-        mean = mean + got[z, 0:1]
-    mean = mean * (1.0 / Z)
+    for v in range(1, N):
+        mean = mean + got[v, 0:1]
+    mean = mean * (1.0 / N)
     spread = jnp.zeros((1, TOK), F32)
-    for z in range(Z):
-        gap = got[z, 0:1] - mean
-        spread = spread + (got[z, 1:2] + WIDE * gap * gap)
+    for v in range(N):
+        gap = got[v, 0:1] - mean
+        spread = spread + (got[v, 1:2] + COLS * gap * gap)
     rstd = lax.rsqrt(spread * (1.0 / D) + 1e-05)
     both = jnp.transpose(jnp.concatenate([mean, rstd, jnp.zeros((126, TOK), F32)], 0))
-    both = both[0:PART]
     normed = ((state[...] - both[:, 0:1]) * both[:, 1:2] * gain[...].astype(F32)).astype(BF)
-    for z in range(Z):
-        out[z] = normed
-
-
-def project_kernel(place, own, other, weight, state, query, out, keep, send, whole):
-    halves = [
-        pl.ds(pl.multiple_of(PART * p, PART), PART) for p in (place[2], 1 - place[2])
-    ]
-    first = place[2] == 0
-    low, high = state[:, 0:COLS].astype(BF), state[:, COLS:].astype(BF)
-    keep[...] = jnp.where(first, low, high)
-    send[...] = jnp.where(first, high, low)
+    for v in range(N):
+        out[v] = normed
+
+
+def project_kernel(got, weight, query, out):
     for c in range(3):
         acc = None
-        for z in range(Z):
-            left = jnp.concatenate([own[z], other[z]], 0)
-            for x in range(2):
-                at = COLS * (Z * x + z)
-                term = jnp.dot(
-                    left[:, COLS * x : COLS * x + COLS],
-                    weight[c, at : at + COLS],
-                    preferred_element_type=F32,
-                )
-                acc = term if acc is None else acc + term
-        for i in range(2):
-            whole[halves[i]] = acc[PART * i : PART * i + PART]
-        result = whole[...].astype(BF)
+        for v in range(N):
+            term = jnp.dot(
+                got[v], weight[c, COLS * v : COLS * v + COLS], preferred_element_type=F32
+            )
+            acc = term if acc is None else acc + term
+        acc = acc.astype(BF)
         if c == 0:
-            query[...] = result
+            query[...] = acc
         else:
             for k in range(Z):
-                out[k, TOK * (c - 1) : TOK * c] = result
+                out[k, TOK * (c - 1) : TOK * c] = acc
 
 
 def attend_kernel(query, own, other, out, scores):
@@ -393,13 +368,11 @@
         out[v] = context
 
 
-def output_kernel(place, got, parts, own, other, out, aggregated, weight, sem):
-    fetch(parts, W_O, weight, sem)
-    halves = columns_of(got, weight)
+def output_kernel(got, weight, out):
+    pairs = [jnp.concatenate([got[h], got[h + 1]], 1) for h in range(0, N, 2)]
+    halves = columns_of(pairs, weight)
     for i in range(2):
         out[:, 128 * i : 128 * i + 128] = halves[i].astype(BF)
-    for p, ref in ((place[2], own), (1 - place[2], other)):
-        aggregated[pl.ds(pl.multiple_of(PART * p, PART), PART)] = ref[...]
 
 
 def shape(dims, kind):
@@ -432,7 +405,7 @@
     out_proj,
 ):
     v_idx, k_idx = lax.axis_index("var"), lax.axis_index("tok")
-    place = jnp.stack([k_idx // 2, k_idx % 2, v_idx // Z]).astype(jnp.int32)
+    place = jnp.stack([k_idx // 2, k_idx % 2]).astype(jnp.int32)
 
     rows_of_k = pl.BlockSpec((16, D), lambda i, place: (place[0], 0))
     parts = pl.pallas_call(
@@ -486,52 +459,41 @@
         flops=2 * 400_000_000,
         size=5_000_000,
     )(place, got, swapped, gain.reshape(1, WIDE))
-    partial = call(
+    partial, pool_part, proj_part = call(
         values_kernel,
-        shape((Z, TOK, E), F32),
+        (
+            shape((Z, TOK, E), F32),
+            shape((N, 16 * N, 128), BF),
+            shape((N, 16 * N, 128), BF),
+        ),
         2,
-        (pltpu.VMEM((N, 32 * N, E), BF), pltpu.SemaphoreType.DMA),
+        (pltpu.VMEM((N, 32 * N, E), BF), pltpu.SemaphoreType.DMA((3,))),
         hbm=(1,),
-        vmem=16,
         flops=4 * PART * WIDE * 2048,
-        size=5_000_000,
+        size=9_000_000,
     )(summed, parts)
-    pooled = call(pooled_kernel, shape((Z, TOK, E), BF), 1, size=800_000)(
+    pooled = call(pooled_kernel, shape((N, TOK, E), BF), 1, size=1_000_000)(
         exchange(partial, "var", RINGS)
     )
-    state, stats = call(
+    state, aggregated, stats = call(
         state_kernel,
-        (shape((PART, WIDE), F32), shape((Z, 8, 128), F32)),
+        (shape((TOK, COLS), F32), shape((TOK, COLS), BF), shape((N, 8, 128), F32)),
         2,
-        (
-            pltpu.VMEM((TOK, 128), F32),
-            pltpu.VMEM((N, 32 * N, 128), BF),
-            pltpu.SemaphoreType.DMA,
-        ),
-        hbm=(1,),
-        vmem=16,
-        flops=2 * PART * 2048 * WIDE,
-        size=3_000_000,
-    )(exchange(pooled, "var", RINGS), parts)
-    gain = lax.dynamic_index_in_dim(block_gain.reshape(2, Z, COLS), v_idx % Z, 1, keepdims=False)
-    normed = call(norm_kernel, shape((Z, PART, WIDE), BF), 3, size=700_000)(
-        exchange(stats, "var", RINGS), state, gain.reshape(1, WIDE)
+        (pltpu.VMEM((TOK, 128), F32),),
+        flops=2 * TOK * 2048 * COLS,
+        size=2_000_000,
+    )(exchange(pooled, "var"), pool_part)
+    gain = lax.dynamic_slice(block_gain, (COLS * v_idx,), (COLS,))[None]
+    normed = call(norm_kernel, shape((N, TOK, COLS), BF), 3, size=1_200_000)(
+        exchange(stats, "var"), state, gain
     )
-    normed = exchange(normed, "var", RINGS)
-    query, kv, keep, send = call(
+    query, kv = call(
         project_kernel,
-        (
-            shape((TOK, E), BF),
-            shape((Z, 2 * TOK, E), BF),
-            shape((PART, COLS), BF),
-            shape((PART, COLS), BF),
-        ),
-        5,
-        (pltpu.VMEM((TOK, E), F32),),
-        smem=(0,),
+        (shape((TOK, E), BF), shape((Z, 2 * TOK, E), BF)),
+        2,
         flops=2 * TOK * D * 384,
         size=5_000_000,
-    )(place, normed, swap(normed, "var", Z), attend_weight, state)
+    )(exchange(normed, "var"), attend_weight)
     kv = exchange(kv, "tok", CORES)
     context = call(
         attend_kernel,
@@ -541,17 +503,9 @@
         flops=4 * TOK * 2048 * E,
         size=1_500_000,
     )(query, kv, swap(kv, "tok", 1))
-    attended, aggregated = call(
-        output_kernel,
-        (shape((TOK, COLS), BF), shape((TOK, COLS), BF)),
-        5,
-        (pltpu.VMEM((N, 16 * N, 128), BF), pltpu.SemaphoreType.DMA),
-        smem=(0,),
-        hbm=(2,),
-        vmem=16,
-        flops=2 * TOK * 2048 * COLS,
-        size=2_000_000,
-    )(place, exchange(context, "var"), parts, keep, swap(send, "var", Z))
+    attended = call(
+        output_kernel, shape((TOK, COLS), BF), 2, flops=2 * TOK * 2048 * COLS, size=2_000_000
+    )(exchange(context, "var"), proj_part)
     return (aggregated, attended)
 
 

time: 237 us -> 232 us (0.979)
  blocking collectives: 99.2 us -> 153 us
  waiting for transfers between devices: 54.4 us -> 14.4 us
  starting transfers between devices: 27.2 us -> 15 us
  local copies, waits for them, and re-layouts: 12.5 us -> 7.85 us
    all_to_all x4 -> x6, blocking collectives: 99.2 us -> 153 us  [exchange(): return lax.all_to_all(x, axis, 0, 0, tiled=True, axis_index_groups=groups)]
    all_to_all x4 -> x2, waiting for transfers between devices: 31.4 us -> 7.08 us  [exchange(): return lax.all_to_all(x, axis, 0, 0, tiled=True, axis_index_groups=groups)]
    ppermute x4 -> x2, waiting for transfers between devices: 15.4 us -> 3.94 us  [swap(): return lax.ppermute(x, axis, [(i, i ^ bits) for i in range(N)])]
    all_to_all x4 -> x2, starting transfers between devices: 25.2 us -> 14.9 us  [exchange(): return lax.all_to_all(x, axis, 0, 0, tiled=True, axis_index_groups=groups)]
    unnamed x30 -> x26, local copies, waits for them, and re-layouts: 12.1 us -> 6.79 us
    all_gather x1, waiting for transfers between devices: 7.54 us -> 3.35 us  [shards(): parts = lax.all_gather(parts, 'tok', axis=0)]
  transfers between devices with their start and end apart: 9 -> 5, of which waited for: 9 -> 5; matrix products, arithmetic and copies ran while one was open for 0% -> 0% of each run, Pallas kernels for 7% -> 7%
where the time goes in v5:
time: 232 us; the launch traced here: 231 us
  blocking collectives  153 us (66%)
  Pallas kernels  25.9 us (11%)
  starting transfers between devices  15 us (6%)
  waiting for transfers between devices  14.4 us (6%)
  between operations  14.3 us (6%)
  local copies, waits for them, and re-layouts  7.85 us (3%)
    all_to_all x6, blocking collectives, exchange(): return lax.all_to_all(x, axis, 0, 0, tiled=True, axis_index_groups=groups)  153 us
    all_to_all x2, starting transfers between devices, exchange(): return lax.all_to_all(x, axis, 0, 0, tiled=True, axis_index_groups=groups)  14.9 us
    pallas_call x1, Pallas kernels, shards(): call(pool_kernel, shape((4, N * SUM_STEP, 128), F32), 4, (pltpu.VMEM((PAI...  9.66 us
    pallas_call x1, Pallas kernels, shards(): call(embed_kernel, shape((N, ROWS, 128), BF), 7, (pltpu.VMEM((TOK, 128),...  7.16 us
    all_to_all x2, waiting for transfers between devices, exchange(): return lax.all_to_all(x, axis, 0, 0, tiled=True, axis_index_groups=groups)  7.08 us
    unnamed x26, local copies, waits for them, and re-layouts  6.79 us
  transfers between devices with their start and end apart: 5, of which 5 were waited for; matrix products, arithmetic and copies ran while one was open for 0% of the time, Pallas kernels for 7%

profile of v5, /device:TPU:34, one launch (start us, length us, event | category | flops | bytes accessed | tf_op | source)
XLA Modules:
  0.0 230.9 jit_solution(832359881503244406)
XLA Ops:
  7.2 0.6 pad_add_fusion.place
  7.8 2.5 %shard_map.124 = bf16[16,64,128]{2,1,0:T(8,128)(2,1)} custom-call(s32[2]{0:T(128)} %pad_add_fusion.place, bf16[256,128]{1,0:T(8,128)(2,1)} %value.1, bf16[128,4096]{1,0:T(8,128)(2,1)} %pool_rows.1, bf16[128,4096]{1,0:T(8,128)(2,1)} %proj_rows.1), custom_call_target="tpu_custom_call" | custom-call | bytes 800000 | tf_op jit(solution)/shard_map/pallas_call | solution.py:411
  10.3 9.5 %all-to-all-start.1 = ((bf16[16,64,128]{2,1,0:T(8,128)(2,1)}), bf16[16,64,128]{2,1,0:T(8,128)(2,1)S(1)}, u32[]{:S(2)}, u32[]{:S(2)}) async-start(bf16[16,64,128]{2,1,0:T(8,128)(2,1)} %shard_map.124), calls=%async_computation.1 | async-start | bytes 524288 | tf_op jit(solution)/shard_map/all_to_all | solution.py:387
  20.0 0.9 copy-done.8
  20.9 0.7 copy-done.9
  21.6 7.2 %shard_map.122.early = bf16[16,416,128]{2,1,0:T(8,128)(2,1)S(1)} custom-call(s32[6]{0:T(128)S(1)} %copy-done.11, s32[2]{0:T(128)S(1)} %copy-done.10, bf16[6,16,128]{2,1,0:T(8,128)(2,1)S(1)} %copy-done.9, bf16[6,16,4096]{2,1,0:T(8,128)(2,1)S(1)} %copy-done.6, bf16[91,4096]{1,0:T(8,128)(2,1)S(1)} %copy-done.7, bf16[1,4096]{1,0:T(2,128)(2,1)S(1)} %broadcast_in_dim.6.gain, ...), custom_call_target="tpu_custom_call" | custom-call | flops 301989888 | bytes 6000000 | tf_op jit(solution)/shard_map/pallas_call | solution.py:423
  28.8 1.0 all-to-all-done.1.parts
  29.8 0.7 shard_map.125
  30.5 47.4 %all_to_all.40.got = bf16[16,416,128]{2,1,0:T(8,128)(2,1)S(1)} all-to-all(bf16[16,416,128]{2,1,0:T(8,128)(2,1)S(1)} %shard_map.122.early), channel_id=1, replica_groups=mesh['var'=16,'tok'=16] {'var'}, dimensions={0} | all-to-all | bytes 3407872 | tf_op jit(solution)/shard_map/all_to_all | solution.py:387
  78.0 0.1 collective-permute-start
  78.3 0.1 reshape.12.gain
  78.4 2.0 collective-permute-done.swapped
  80.4 9.7 %shard_map.123.summed = f32[4,1040,128]{2,1,0:T(8,128)S(1)} custom-call(s32[2]{0:T(128)S(1)} %copy-done.10, bf16[16,416,128]{2,1,0:T(8,128)(2,1)S(1)} %all_to_all.40.got, bf16[16,192,128]{2,1,0:T(8,128)(2,1)S(1)} %collective-permute-done.swapped, bf16[1,512]{1,0:T(2,128)(2,1)S(1)} %reshape.12.gain), custom_call_target="tpu_custom_call" | custom-call | flops 800000000 | bytes 5000000 | tf_op jit(solution)/shard_map/pallas_call | solution.py:448
  90.1 1.3 copy-done
  91.4 3.3 %all-gather.3.cloned.1.call-done = bf16[16384,128]{1,0:T(8,128)(2,1)} async-done(((bf16[1024,128]{1,0:T(8,128)(2,1)}), bf16[16384,128]{1,0:T(8,128)(2,1)}) %all-gather.3.cloned.1.call-update) | async-done | bytes 4194320 | tf_op jit(solution)/shard_map/all_gather | solution.py:443
  94.8 1.6 copy-done.1
  96.4 2.2 copy-done.2
  98.6 1.0 shard_map.126
  99.6 22.8 %all_to_all.41.got = f32[8,128,128]{2,1,0:T(8,128)S(1)} all-to-all(f32[8,128,128]{2,1,0:T(8,128)S(1)} %get-tuple-element.10), channel_id=1, replica_groups={{0,16,32,48,64,80,96,112},{128,144,160,176,192,208,224,240},{1,17,33,49..., dimensions={0} | all-to-all | bytes 1048576 | tf_op jit(solution)/shard_map/all_to_all | solution.py:387
  122.4 19.7 %all_to_all.42.got = bf16[16,128,128]{2,1,0:T(8,128)(2,1)S(1)} all-to-all(bf16[16,128,128]{2,1,0:T(8,128)(2,1)S(1)} %shard_map.127), channel_id=1, replica_groups=mesh['var'=16,'tok'=16] {'var'}, dimensions={0} | all-to-all | bytes 1048576 | tf_op jit(solution)/shard_map/all_to_all | solution.py:387
  142.1 1.3 shard_map.128
  143.4 5.4 %all-to-all-start.4 = ((f32[16,8,128]{2,1,0:T(8,128)}), f32[16,8,128]{2,1,0:T(8,128)S(1)}, u32[]{:S(2)}, u32[]{:S(2)}) async-start(f32[16,8,128]{2,1,0:T(8,128)} %get-tuple-element.13), calls=%async_computation.4 | async-start | bytes 131072 | tf_op jit(solution)/shard_map/all_to_all | solution.py:387
  148.8 0.8 dynamic_slice.8
  149.6 6.1 %all-to-all-done.4.got = f32[16,8,128]{2,1,0:T(8,128)S(1)} async-done(((f32[16,8,128]{2,1,0:T(8,128)}), f32[16,8,128]{2,1,0:T(8,128)S(1)}, u32[]{:S(2)}, u32[]{:S(2)}) %all-to-all-start.4) | async-done | bytes 65568 | tf_op jit(solution)/shard_map/all_to_all | solution.py:387
  155.6 0.3 shard_map.129
  155.9 29.4 %all_to_all.43.got = bf16[16,128,256]{2,1,0:T(8,128)(2,1)S(1)} all-to-all(bf16[16,128,256]{2,1,0:T(8,128)(2,1)S(1)} %shard_map.129), channel_id=1, replica_groups=mesh['var'=16,'tok'=16] {'var'}, dimensions={0} | all-to-all | bytes 2097152 | tf_op jit(solution)/shard_map/all_to_all | solution.py:387
  185.4 1.0 shard_map.130
  186.4 12.7 %all_to_all.44.own = bf16[8,256,128]{2,1,0:T(8,128)(2,1)S(1)} all-to-all(bf16[8,256,128]{2,1,0:T(8,128)(2,1)S(1)} %get-tuple-element.16), channel_id=1, replica_groups={{0,2,4,6,8,10,12,14},{1,3,5,7,9,11,13,15},{16,18,20,22,24,26,28,30},{17..., dimensions={0} | all-to-all | bytes 1048576 | tf_op jit(solution)/shard_map/all_to_all | solution.py:387
  199.1 1.9 collective-permute-done.1.other
  201.0 1.2 shard_map.131
  202.2 20.8 %all_to_all.45.got = bf16[16,128,128]{2,1,0:T(8,128)(2,1)S(1)} all-to-all(bf16[16,128,128]{2,1,0:T(8,128)(2,1)S(1)} %shard_map.131), channel_id=1, replica_groups=mesh['var'=16,'tok'=16] {'var'}, dimensions={0} | all-to-all | bytes 1048576 | tf_op jit(solution)/shard_map/all_to_all | solution.py:387
  223.0 1.1 shard_map.132
  (30 shorter events, 0.4 us)
Async XLA Ops:
  7.2 12.7 %copy-start.12 = (bf16[4096]{0:T(1024)(128)(2,1)S(1)}, bf16[4096]{0:T(1024)(128)(2,1)}, u32[]{:S(2)}) copy-start(bf16[4096]{0:T(1024)(128)(2,1)} %param.15) | copy-start | bytes 24580
  7.2 12.7 %copy-start.11 = (s32[6]{0:T(128)S(1)}, s32[6]{0:T(128)}, u32[]{:S(2)}) copy-start(s32[6]{0:T(128)} %slot.1) | copy-start | bytes 76
  7.2 12.7 %copy-start.6 = (bf16[6,16,4096]{2,1,0:T(8,128)(2,1)S(1)}, bf16[6,16,4096]{2,1,0:T(8,128)(2,1)}, u32[]{:S(2)}) copy-start(bf16[6,16,4096]{2,1,0:T(8,128)(2,1)} %weight.2) | copy-start | bytes 2359300
  7.2 12.7 %copy-start.7 = (bf16[91,4096]{1,0:T(8,128)(2,1)S(1)}, bf16[91,4096]{1,0:T(8,128)(2,1)}, u32[]{:S(2)}) copy-start(bf16[91,4096]{1,0:T(8,128)(2,1)} %table.1) | copy-start | bytes 2236420
  7.8 12.1 %copy-start.10 = (s32[2]{0:T(128)S(1)}, s32[2]{0:T(128)}, u32[]{:S(2)}) copy-start(s32[2]{0:T(128)} %pad_add_fusion.place) | copy-start | bytes 28
  10.3 19.4 %all-to-all-start.1 = ((bf16[16,64,128]{2,1,0:T(8,128)(2,1)}), bf16[16,64,128]{2,1,0:T(8,128)(2,1)S(1)}, u32[]{:S(2)}, u32[]{:S(2)}) async-start(bf16[16,64,128]{2,1,0:T(8,128)(2,1)} %shard_map.124), calls=%async_computation.1 | async-start | bytes 524288 | tf_op jit(solution)/shard_map/all_to_all | solution.py:387
  19.8 74.9 %all-gather.3.cloned.1.call-start = ((), (), s32[]{:S(2)}) async-start(), calls=%async_computation.8 | async-start | bytes 4456448 | tf_op jit(solution)/shard_map/all_gather | solution.py:443
  19.9 0.9 copy-start.8
  20.9 0.7 copy-start.9
  78.0 2.4 %collective-permute-start = (bf16[16,192,128]{2,1,0:T(8,128)(2,1)S(1)}, bf16[16,192,128]{2,1,0:T(8,128)(2,1)S(1)}, u32[]{:S(2)}, u32[]{:S(2)}) collective-permute-start(bf16[16,192,128]{2,1,0:T(8,128)(2,1)S(1)} %slice.4), channel_id=1, source_target_pairs={{0,1},{1,0},{2,3},{3,2},{4,5},{5,4},{6,7},{7,6},{8,9},{9,8},{10,11... | collective-permute-start | bytes 2359304 | tf_op jit(solution)/shard_map/ppermute | solution.py:391
  90.1 1.3 copy-start
  94.8 1.6 copy-start.1
  96.4 2.2 copy-start.2
  99.6 43.8 %copy-start.4 = (bf16[16,256,128]{2,1,0:T(8,128)(2,1)}, bf16[16,256,128]{2,1,0:T(8,128)(2,1)S(1)}, u32[]{:S(2)}) copy-start(bf16[16,256,128]{2,1,0:T(8,128)(2,1)S(1)} %get-tuple-element.17.weight) | copy-start | bytes 3145732
  143.4 42.0 %copy-start.3 = (bf16[3,4096,128]{2,1,0:T(8,128)(2,1)S(1)}, bf16[3,4096,128]{2,1,0:T(8,128)(2,1)}, u32[]{:S(2)}) copy-start(bf16[3,4096,128]{2,1,0:T(8,128)(2,1)} %weight.3) | copy-start | bytes 9437188
  143.4 12.2 %all-to-all-start.4 = ((f32[16,8,128]{2,1,0:T(8,128)}), f32[16,8,128]{2,1,0:T(8,128)S(1)}, u32[]{:S(2)}, u32[]{:S(2)}) async-start(f32[16,8,128]{2,1,0:T(8,128)} %get-tuple-element.13), calls=%async_computation.4 | async-start | bytes 131072 | tf_op jit(solution)/shard_map/all_to_all | solution.py:387
  186.4 36.7 %copy-start.5 = (bf16[16,256,128]{2,1,0:T(8,128)(2,1)S(1)}, bf16[16,256,128]{2,1,0:T(8,128)(2,1)}, u32[]{:S(2)}) copy-start(bf16[16,256,128]{2,1,0:T(8,128)(2,1)} %copy-done.4) | copy-start | bytes 3145732
  199.1 1.9 collective-permute-start.1
Sparse Core Ops, SparseCore 0:
  30.6 64.0 all-gather.2

commit v6 on v5

--- a/solution.py
+++ b/solution.py
@@ -147,7 +147,7 @@
             out[a : a + size] = parts[h, first:last]
 
 
-def pool_kernel(place, got, swapped, gain, summed, weights, turned, rows):
+def pool_kernel(place, got, swapped, gain, high_out, low_out, weights, turned, rows, summed):
     tops = []
     for v in range(N):
         m = [got[v, R_M + 16 * i : R_M + 16 * i + 16].astype(F32) for i in range(2)]
@@ -240,9 +240,14 @@
         return carry
 
     lax.fori_loop(0, PART // 2, two_tokens, 0, unroll=4)
-
-
-def values_kernel(summed, parts, out, pool_part, proj_part, value, sems):
+    for h in range(N):
+        at = slice(SUM_STEP * h, SUM_STEP * h + PART)
+        hi, lo = split2(jnp.concatenate([summed[j, at] for j in range(4)], 1))
+        high_out[PART * h : PART * h + PART] = hi
+        low_out[PART * h : PART * h + PART] = lo
+
+
+def values_kernel(high, low, parts, out, pool_part, proj_part, value, sems):
     copies = []
     for i, (row, into) in enumerate(((W_V, value), (W_P, pool_part), (W_O, proj_part))):
         span = pl.ds(N * row, into.shape[1])
@@ -251,10 +256,9 @@
         copy.start()
     copies[0].wait()
     for h in range(N):
-        at = slice(SUM_STEP * h, SUM_STEP * h + PART)
-        hi, lo = split2(jnp.concatenate([summed[j, at] for j in range(4)], 1))
+        at = slice(PART * h, PART * h + PART)
         right = jnp.concatenate([value[k, 32 * h : 32 * h + 32] for k in range(N)], 0)
-        whole = jnp.dot(jnp.concatenate([hi, lo], 0), right, preferred_element_type=F32)
+        whole = jnp.dot(jnp.concatenate([high[at], low[at]], 0), right, preferred_element_type=F32)
         out[h // 2, PART * (h % 2) : PART * (h % 2) + PART] = whole[:PART] + whole[PART:]
     for copy in copies[1:]:
         copy.wait()
@@ -445,14 +449,15 @@
     swapped = swap(got[:, R_U:R_P], "tok", 1)
     gain = lax.dynamic_index_in_dim(norm_gain.reshape(N, Z, 32), v_idx % Z, 1, keepdims=False)
 
-    summed = call(
+    high, low = call(
         pool_kernel,
-        shape((4, N * SUM_STEP, 128), F32),
+        (shape((N * PART, WIDE), BF), shape((N * PART, WIDE), BF)),
         4,
         (
             pltpu.VMEM((PAIRS * N, TOK), F32),
             pltpu.VMEM((2, PART * LEFT_STEP, TOK), F32),
             pltpu.VMEM((4, PART * ROW_STEP, 128), F32),
+            pltpu.VMEM((4, N * SUM_STEP, 128), F32),
         ),
         smem=(0,),
         vmem=26,
@@ -466,12 +471,12 @@
             shape((N, 16 * N, 128), BF),
             shape((N, 16 * N, 128), BF),
         ),
-        2,
+        3,
         (pltpu.VMEM((N, 32 * N, E), BF), pltpu.SemaphoreType.DMA((3,))),
-        hbm=(1,),
+        hbm=(2,),
         flops=4 * PART * WIDE * 2048,
         size=9_000_000,
-    )(summed, parts)
+    )(high, low, parts)
     pooled = call(pooled_kernel, shape((N, TOK, E), BF), 1, size=1_000_000)(
         exchange(partial, "var", RINGS)
     )

time: 232 us -> 233 us (level)
  local copies, waits for them, and re-layouts: 7.85 us -> 12.1 us
  waiting for transfers between devices: 14.4 us -> 10.7 us
    all_gather x1, waiting for transfers between devices: 3.35 us -> 0.42 us  [shards(): parts = lax.all_gather(parts, 'tok', axis=0)]
    unnamed x26 -> x32, local copies, waits for them, and re-layouts: 6.79 us -> 9.41 us
  transfers between devices with their start and end apart: 5 -> 5, of which waited for: 5 -> 4; matrix products, arithmetic and copies ran while one was open for 0% -> 1% of each run, Pallas kernels for 7% -> 7%
where the time goes in v6:
time: 233 us; the launch traced here: 232 us
  blocking collectives  154 us (66%)
  Pallas kernels  26 us (11%)
  starting transfers between devices  14.7 us (6%)
  between operations  14.2 us (6%)
  local copies, waits for them, and re-layouts  12.1 us (5%)
  waiting for transfers between devices  10.7 us (5%)
    all_to_all x6, blocking collectives, exchange(): return lax.all_to_all(x, axis, 0, 0, tiled=True, axis_index_groups=groups)  154 us
    all_to_all x2, starting transfers between devices, exchange(): return lax.all_to_all(x, axis, 0, 0, tiled=True, axis_index_groups=groups)  14.6 us
    pallas_call x1, Pallas kernels, shards(): call(pool_kernel, (shape((N * PART, WIDE), BF), shape((N * PART, WIDE), B...  9.9 us
    unnamed x32, local copies, waits for them, and re-layouts  9.41 us
    pallas_call x1, Pallas kernels, shards(): call(embed_kernel, shape((N, ROWS, 128), BF), 7, (pltpu.VMEM((TOK, 128),...  7.15 us
    all_to_all x2, waiting for transfers between devices, exchange(): return lax.all_to_all(x, axis, 0, 0, tiled=True, axis_index_groups=groups)  6.07 us
  transfers between devices with their start and end apart: 5, of which 4 were waited for; matrix products, arithmetic and copies ran while one was open for 1% of the time, Pallas kernels for 7%

profile of v6, /device:TPU:34, one launch (start us, length us, event | category | flops | bytes accessed | tf_op | source)
XLA Modules:
  0.0 232.2 jit_solution(4460682417424867871)
XLA Ops:
  7.9 2.4 %shard_map.124 = bf16[16,64,128]{2,1,0:T(8,128)(2,1)} custom-call(s32[2]{0:T(128)} %pad_add_fusion.place, bf16[256,128]{1,0:T(8,128)(2,1)} %value.1, bf16[128,4096]{1,0:T(8,128)(2,1)} %pool_rows.1, bf16[128,4096]{1,0:T(8,128)(2,1)} %proj_rows.1), custom_call_target="tpu_custom_call" | custom-call | bytes 800000 | tf_op jit(solution)/shard_map/pallas_call | solution.py:415
  10.3 9.5 %all-to-all-start.1 = ((bf16[16,64,128]{2,1,0:T(8,128)(2,1)}), bf16[16,64,128]{2,1,0:T(8,128)(2,1)S(1)}, u32[]{:S(2)}, u32[]{:S(2)}) async-start(bf16[16,64,128]{2,1,0:T(8,128)(2,1)} %shard_map.124), calls=%async_computation.1 | async-start | bytes 524288 | tf_op jit(solution)/shard_map/all_to_all | solution.py:391
  19.8 0.7 broadcast_in_dim.6.gain
  20.5 0.9 copy-done.8
  21.4 0.7 copy-done.9
  22.2 0.7 copy-done.10
  22.8 0.7 copy-done.12
  23.5 7.2 %shard_map.122.early = bf16[16,416,128]{2,1,0:T(8,128)(2,1)S(1)} custom-call(s32[6]{0:T(128)S(1)} %copy-done.12, s32[2]{0:T(128)S(1)} %copy-done.10, bf16[6,16,128]{2,1,0:T(8,128)(2,1)S(1)} %copy-done.9, bf16[6,16,4096]{2,1,0:T(8,128)(2,1)S(1)} %copy-done.6, bf16[91,4096]{1,0:T(8,128)(2,1)S(1)} %copy-done.7, bf16[1,4096]{1,0:T(2,128)(2,1)S(1)} %broadcast_in_dim.6.gain, ...), custom_call_target="tpu_custom_call" | custom-call | flops 301989888 | bytes 6000000 | tf_op jit(solution)/shard_map/pallas_call | solution.py:427
  30.7 0.7 shard_map.125
  31.4 48.4 %all_to_all.40.got = bf16[16,416,128]{2,1,0:T(8,128)(2,1)S(1)} all-to-all(bf16[16,416,128]{2,1,0:T(8,128)(2,1)S(1)} %shard_map.122.early), channel_id=1, replica_groups=mesh['var'=16,'tok'=16] {'var'}, dimensions={0} | all-to-all | bytes 3407872 | tf_op jit(solution)/shard_map/all_to_all | solution.py:391
  79.9 1.0 slice.4
  81.1 2.3 collective-permute-done.swapped
  83.3 0.9 copy-done.13
  84.2 1.1 copy-done.14
  85.4 9.9 %shard_map.123 = (bf16[1024,512]{1,0:T(8,128)(2,1)S(1)}, bf16[1024,512]{1,0:T(8,128)(2,1)S(1)}) custom-call(s32[2]{0:T(128)S(1)} %copy-done.11, bf16[16,416,128]{2,1,0:T(8,128)(2,1)S(1)} %all_to_all.40.got, bf16[16,192,128]{2,1,0:T(8,128)(2,1)S(1)} %copy-done.14, bf16[1,512]{1,0:T(2,128)(2,1)S(1)} %reshape.12.gain), custom_call_target="tpu_custom_call" | custom-call | flops 800000000 | bytes 5000000 | tf_op jit(solution)/shard_map/pallas_call | solution.py:452
  95.3 1.0 copy-done.4
  96.7 2.2 copy-done
  98.9 1.2 copy-done.5
  100.1 1.0 shard_map.126
  101.1 22.8 %all_to_all.41.got = f32[8,128,128]{2,1,0:T(8,128)S(1)} all-to-all(f32[8,128,128]{2,1,0:T(8,128)S(1)} %get-tuple-element.14), channel_id=1, replica_groups={{0,16,32,48,64,80,96,112},{128,144,160,176,192,208,224,240},{1,17,33,49..., dimensions={0} | all-to-all | bytes 1048576 | tf_op jit(solution)/shard_map/all_to_all | solution.py:391
  124.0 20.0 %all_to_all.42.got = bf16[16,128,128]{2,1,0:T(8,128)(2,1)S(1)} all-to-all(bf16[16,128,128]{2,1,0:T(8,128)(2,1)S(1)} %shard_map.127), channel_id=1, replica_groups=mesh['var'=16,'tok'=16] {'var'}, dimensions={0} | all-to-all | bytes 1048576 | tf_op jit(solution)/shard_map/all_to_all | solution.py:391
  144.0 1.3 shard_map.128
  145.2 5.2 %all-to-all-start.4 = ((f32[16,8,128]{2,1,0:T(8,128)}), f32[16,8,128]{2,1,0:T(8,128)S(1)}, u32[]{:S(2)}, u32[]{:S(2)}) async-start(f32[16,8,128]{2,1,0:T(8,128)} %get-tuple-element.17), calls=%async_computation.4 | async-start | bytes 131072 | tf_op jit(solution)/shard_map/all_to_all | solution.py:391
  150.4 0.8 dynamic_slice.8
  151.2 6.1 %all-to-all-done.4.got = f32[16,8,128]{2,1,0:T(8,128)S(1)} async-done(((f32[16,8,128]{2,1,0:T(8,128)}), f32[16,8,128]{2,1,0:T(8,128)S(1)}, u32[]{:S(2)}, u32[]{:S(2)}) %all-to-all-start.4) | async-done | bytes 65568 | tf_op jit(solution)/shard_map/all_to_all | solution.py:391
  157.5 29.3 %all_to_all.43.got = bf16[16,128,256]{2,1,0:T(8,128)(2,1)S(1)} all-to-all(bf16[16,128,256]{2,1,0:T(8,128)(2,1)S(1)} %shard_map.129), channel_id=1, replica_groups=mesh['var'=16,'tok'=16] {'var'}, dimensions={0} | all-to-all | bytes 2097152 | tf_op jit(solution)/shard_map/all_to_all | solution.py:391
  186.8 1.0 shard_map.130
  187.8 12.6 %all_to_all.44.own = bf16[8,256,128]{2,1,0:T(8,128)(2,1)S(1)} all-to-all(bf16[8,256,128]{2,1,0:T(8,128)(2,1)S(1)} %get-tuple-element.20), channel_id=1, replica_groups={{0,2,4,6,8,10,12,14},{1,3,5,7,9,11,13,15},{16,18,20,22,24,26,28,30},{17..., dimensions={0} | all-to-all | bytes 1048576 | tf_op jit(solution)/shard_map/all_to_all | solution.py:391
  200.4 1.9 collective-permute-done.1.other
  202.3 1.2 shard_map.131
  203.5 20.8 %all_to_all.45.got = bf16[16,128,128]{2,1,0:T(8,128)(2,1)S(1)} all-to-all(bf16[16,128,128]{2,1,0:T(8,128)(2,1)S(1)} %shard_map.131), channel_id=1, replica_groups=mesh['var'=16,'tok'=16] {'var'}, dimensions={0} | all-to-all | bytes 1048576 | tf_op jit(solution)/shard_map/all_to_all | solution.py:391
  224.3 1.1 shard_map.132
  (36 shorter events, 1.7 us)
Async XLA Ops:
  7.2 13.4 %copy-start.6 = (bf16[6,16,4096]{2,1,0:T(8,128)(2,1)S(1)}, bf16[6,16,4096]{2,1,0:T(8,128)(2,1)}, u32[]{:S(2)}) copy-start(bf16[6,16,4096]{2,1,0:T(8,128)(2,1)} %weight.2) | copy-start | bytes 2359300
  7.2 13.4 %copy-start.7 = (bf16[91,4096]{1,0:T(8,128)(2,1)S(1)}, bf16[91,4096]{1,0:T(8,128)(2,1)}, u32[]{:S(2)}) copy-start(bf16[91,4096]{1,0:T(8,128)(2,1)} %table.1) | copy-start | bytes 2236420
  10.3 20.4 %all-to-all-start.1 = ((bf16[16,64,128]{2,1,0:T(8,128)(2,1)}), bf16[16,64,128]{2,1,0:T(8,128)(2,1)S(1)}, u32[]{:S(2)}, u32[]{:S(2)}) async-start(bf16[16,64,128]{2,1,0:T(8,128)(2,1)} %shard_map.124), calls=%async_computation.1 | async-start | bytes 524288 | tf_op jit(solution)/shard_map/all_to_all | solution.py:391
  19.8 76.9 %all-gather.3.cloned.1.call-start = ((), (), s32[]{:S(2)}) async-start(), calls=%async_computation.8 | async-start | bytes 4456448 | tf_op jit(solution)/shard_map/all_gather | solution.py:447
  20.5 0.9 copy-start.8
  21.4 0.7 copy-start.9
  22.2 0.7 copy-start.10
  22.8 0.7 copy-start.12
  31.4 49.4 %copy-start.15 = (bf16[4096]{0:T(1024)(128)(2,1)S(1)}, bf16[4096]{0:T(1024)(128)(2,1)}, u32[]{:S(2)}) copy-start(bf16[4096]{0:T(1024)(128)(2,1)} %param.15) | copy-start | bytes 24580
  31.4 52.8 %copy-start.11 = (s32[2]{0:T(128)S(1)}, s32[2]{0:T(128)}, u32[]{:S(2)}) copy-start(s32[2]{0:T(128)} %pad_add_fusion.place) | copy-start | bytes 28
  80.8 2.5 %collective-permute-start = (bf16[16,192,128]{2,1,0:T(8,128)(2,1)}, bf16[16,192,128]{2,1,0:T(8,128)(2,1)S(1)}, u32[]{:S(2)}, u32[]{:S(2)}) collective-permute-start(bf16[16,192,128]{2,1,0:T(8,128)(2,1)} %slice.4), channel_id=1, source_target_pairs={{0,1},{1,0},{2,3},{3,2},{4,5},{5,4},{6,7},{7,6},{8,9},{9,8},{10,11... | collective-permute-start | bytes 2359304 | tf_op jit(solution)/shard_map/ppermute | solution.py:395
  83.3 0.9 copy-start.13
  84.2 1.1 copy-start.14
  95.3 1.0 copy-start.4
  96.7 2.2 copy-start
  98.9 1.2 copy-start.5
  101.1 44.1 %copy-start.2 = (bf16[16,256,128]{2,1,0:T(8,128)(2,1)}, bf16[16,256,128]{2,1,0:T(8,128)(2,1)S(1)}, u32[]{:S(2)}) copy-start(bf16[16,256,128]{2,1,0:T(8,128)(2,1)S(1)} %get-tuple-element.21.weight) | copy-start | bytes 3145732
  124.0 62.8 %copy-start.1 = (bf16[3,4096,128]{2,1,0:T(8,128)(2,1)S(1)}, bf16[3,4096,128]{2,1,0:T(8,128)(2,1)}, u32[]{:S(2)}) copy-start(bf16[3,4096,128]{2,1,0:T(8,128)(2,1)} %weight.3) | copy-start | bytes 9437188
  145.2 12.0 %all-to-all-start.4 = ((f32[16,8,128]{2,1,0:T(8,128)}), f32[16,8,128]{2,1,0:T(8,128)S(1)}, u32[]{:S(2)}, u32[]{:S(2)}) async-start(f32[16,8,128]{2,1,0:T(8,128)} %get-tuple-element.17), calls=%async_computation.4 | async-start | bytes 131072 | tf_op jit(solution)/shard_map/all_to_all | solution.py:391
  186.8 37.5 %copy-start.3 = (bf16[16,256,128]{2,1,0:T(8,128)(2,1)S(1)}, bf16[16,256,128]{2,1,0:T(8,128)(2,1)}, u32[]{:S(2)}) copy-start(bf16[16,256,128]{2,1,0:T(8,128)(2,1)} %copy-done.2) | copy-start | bytes 3145732
  200.4 1.9 collective-permute-start.1
Sparse Core Ops, SparseCore 0:
  31.6 65.0 all-gather.2
